TPU v7x, 32 devices: a whole 2x2x4 slice. The times are simulated.
32 devices in a mesh: dp: 8 (over z, x), row: 2 (over y), col: 2 (over core).
Axes of the slice: x: 2, y: 2, z: 4, core: 2. Of those that a mesh axis runs over, the one named last changes fastest.
Arguments:
- features: bfloat16 [8, 8, 64, 2048], P('dp', 'row', 'col'), may hold values from -6 to 6
- cotangent: bfloat16 [8, 8, 64, 2048], P('dp', 'row', 'col'), may hold values from -6 to 6
- kernel_one: float32 [4, 512, 1152], P(('row', 'col'), 'dp'), may hold values from -0.1875 to 0.1875
- kernel_two: float32 [4, 512, 1152], P(('row', 'col'), 'dp'), may hold values from -0.1875 to 0.1875
- gain_one: float32 [4, 512], P(('row', 'col'), 'dp'), may hold values from 0.5 to 1.5
- gain_two: float32 [4, 512], P(('row', 'col'), 'dp'), may hold values from 0.5 to 1.5
Outputs:
- outputs: bfloat16 [8, 8, 64, 2048], P('dp', 'row', 'col')
- input_grad: bfloat16 [8, 8, 64, 2048], P('dp', 'row', 'col')
- kernel_grad_one: float32 [4, 512, 1152], P(('row', 'col'), 'dp')
- kernel_grad_two: float32 [4, 512, 1152], P(('row', 'col'), 'dp')
All inputs are finite; a program needn't handle non-finite values.
Results may differ from a plain program's by a relative error of at most 0.028.
Values may be sent and summed in bfloat16 or wider, within the bound.
No kernel may reach another device: no remote copies, remote signals or barrier semaphores. Data moves between devices by JAX's collectives and lax.ppermute only.
A program may use at most 128 MiB of HBM per device.

v0:
```python
import functools
import math

import jax
import jax.numpy as jnp
from jax import lax
from jax.experimental import pallas as pl
from jax.experimental.pallas import tpu as pltpu
from jax.sharding import Mesh, PartitionSpec as P

GAMMA = 1.7015043497085571
ALPHA = 0.2
EPS = 1e-06
ROOT = math.sqrt(2.0 / math.pi)
CUBE = 0.044715
F32 = jnp.float32
BF16 = jnp.bfloat16
VMEM_LIMIT = 48 * 1024 * 1024


def act_value(x):
    t = jnp.tanh(ROOT * (x + CUBE * (x * x * x)))
    return (0.5 * GAMMA) * x * (1.0 + t)


def act_slope(x):
    sq = x * x
    t = jnp.tanh(ROOT * (x + CUBE * (sq * x)))
    return (0.5 * GAMMA) * ((1.0 + t) + x * (1.0 - t * t) * (ROOT + (3.0 * CUBE * ROOT) * sq))


def act_both(x):
    sq = x * x
    t = jnp.tanh(ROOT * (x + CUBE * (sq * x)))
    up = 1.0 + t
    value = (0.5 * GAMMA) * x * up
    slope = (0.5 * GAMMA) * (up + x * (1.0 - t * t) * (ROOT + (3.0 * CUBE * ROOT) * sq))
    return value, slope


def params(**kw):
    return pltpu.CompilerParams(vmem_limit_bytes=VMEM_LIMIT, **kw)


def cost(flops, size):
    return pl.CostEstimate(flops=int(flops), bytes_accessed=int(size), transcendentals=0)


def column(gain_ref):
    rows = gain_ref.shape[1]
    first = lax.broadcasted_iota(jnp.int32, (rows, rows), 0)
    second = lax.broadcasted_iota(jnp.int32, (rows, rows), 1)
    spread = jnp.broadcast_to(gain_ref[...], (rows, rows))
    return jnp.sum(jnp.where(first == second, spread, 0.0), axis=1, keepdims=True)


def std_kernel(k1, k2, g1, g2, w1, w2):
    for k, g, w in ((k1, g1, w1), (k2, g2, w2)):
        fan = k.shape[1]
        kern = k[...]
        cent = kern - jnp.mean(kern, axis=1, keepdims=True)
        var = jnp.mean(cent * cent, axis=1, keepdims=True)
        scale = column(g) * lax.rsqrt(var + EPS) * (1.0 / math.sqrt(fan))
        w[...] = (cent * scale).astype(BF16)


def std_rows(k1, k2, g1, g2):
    shape = jax.ShapeDtypeStruct(k1.shape, BF16)
    return pl.pallas_call(
        std_kernel,
        out_shape=(shape, shape),
        name="std_rows",
        compiler_params=params(),
        cost_estimate=cost(1e6, 4e6),
    )(k1, k2, g1, g2)


def pull_kernel(k, g, keep, recv, out):
    fan = k.shape[1]
    kern = k[...]
    grad = keep[...].astype(F32) + recv[...].astype(F32)
    cent = kern - jnp.mean(kern, axis=1, keepdims=True)
    var = jnp.mean(cent * cent, axis=1, keepdims=True)
    inv = lax.rsqrt(var + EPS)
    scale = column(g) * inv * (1.0 / math.sqrt(fan))
    dot = jnp.mean(grad * cent, axis=1, keepdims=True)
    term = scale * (grad - cent * (inv * inv * dot))
    out[...] = term - jnp.mean(term, axis=1, keepdims=True)


def pull_rows(k, g, keep, recv):
    return pl.pallas_call(
        pull_kernel,
        out_shape=jax.ShapeDtypeStruct(k.shape, F32),
        name="pull_rows",
        compiler_params=params(),
        cost_estimate=cost(1e6, 4e6),
    )(k, g, keep, recv)


def pack_kernel(geo, f, c, out):
    cells = f.shape[0]
    group = geo["group"]
    for dst in range(geo["peers"]):
        b, block = dst // geo["blocks"], dst % geo["blocks"]
        for slot in range(geo["slots"]):
            at = (block * geo["per_block"] + slot * geo["nb"] + b) * group
            out[dst, 0, slot] = act_value(f[:, at : at + group].astype(F32)).astype(BF16)
            out[dst, 1, slot] = (ALPHA * c[:, at : at + group].astype(F32)).astype(BF16)


def pack(geo, f, c):
    cells = f.shape[0]
    return pl.pallas_call(
        functools.partial(pack_kernel, geo),
        out_shape=jax.ShapeDtypeStruct((geo["peers"], 2, geo["slots"], cells, geo["group"]), BF16),
        name="pack",
        compiler_params=params(),
        cost_estimate=cost(4e6, 4e6),
    )(f, c)


def merge_kernel(geo, f, c, recv, out, grad):
    group = geo["group"]
    for src in range(geo["peers"]):
        b, block = src // geo["blocks"], src % geo["blocks"]
        for slot in range(geo["slots"]):
            at = (block * geo["per_block"] + slot * geo["nb"] + b) * group
            x = f[:, at : at + group].astype(F32)
            out[:, at : at + group] = (x + recv[src, 0, slot].astype(F32)).astype(BF16)
            grad[:, at : at + group] = (
                c[:, at : at + group].astype(F32) + act_slope(x) * recv[src, 1, slot].astype(F32)
            ).astype(BF16)


def merge(geo, f, c, recv):
    shape = jax.ShapeDtypeStruct(f.shape, BF16)
    return pl.pallas_call(
        functools.partial(merge_kernel, geo),
        out_shape=(shape, shape),
        name="merge",
        compiler_params=params(),
        cost_estimate=cost(4e6, 6e6),
    )(f, c, recv)


def chunks(geo):
    nr, nc, rows, cols, images = (geo[k] for k in ("nr", "nc", "rows", "cols", "images"))
    for b in range(geo["nb"]):
        for i in range(images):
            runs = []
            for r in range(nr):
                for y in range(rows):
                    for c in range(nc):
                        runs.append(((b * nr + r) * nc + c, (i * rows + y) * cols))
            yield runs


def read_maps(geo, recv):
    cols = geo["cols"]
    return [
        jnp.concatenate([recv[peer, 0, 0, at : at + cols, :] for peer, at in runs], axis=0)
        for runs in chunks(geo)
    ]


def write_maps(geo, out, which, maps):
    cols = geo["cols"]
    for value, runs in zip(maps, chunks(geo)):
        for n, (peer, at) in enumerate(runs):
            out[peer, which, 0, at : at + cols, :] = value[n * cols : (n + 1) * cols, :]


def fill_patches(geo, x3, number, value):
    width, group, area = geo["width"], geo["group"], geo["area"]
    x = value.astype(F32)
    at = lax.broadcasted_iota(jnp.int32, (area, group), 0) % width
    left = jnp.where(at == 0, 0.0, pltpu.roll(x, 1, 0))
    right = jnp.where(at == width - 1, 0.0, pltpu.roll(x, area - 1, 0))
    zero = jnp.zeros((width, 3 * group), BF16)
    x3[number, 0:width, :] = zero
    x3[number, width + area : 2 * width + area, :] = zero
    rows = pl.ds(width, area)
    x3[number, rows, 0:group] = left.astype(BF16)
    x3[number, rows, group : 2 * group] = value.astype(BF16)
    x3[number, rows, 2 * group : 3 * group] = right.astype(BF16)


def conv(geo, x3, number, w):
    width, area, span = geo["width"], geo["area"], 3 * geo["group"]
    total = None
    for dy in range(3):
        part = lax.dot_general(
            x3[number, pl.ds(dy * width, area), :],
            w[:, dy * span : (dy + 1) * span],
            (((1,), (1,)), ((), ())),
            preferred_element_type=F32,
        )
        total = part if total is None else total + part
    return total


def adjoint(geo, x3, number, w):
    width, area, span, group = geo["width"], geo["area"], 3 * geo["group"], geo["group"]
    total = None
    for dy in range(3):
        taps = [8 - (3 * dy + s) for s in range(3)]
        rhs = jnp.concatenate([w[:, t * group : (t + 1) * group] for t in taps], axis=0)
        part = jnp.dot(x3[number, pl.ds(dy * width, area), :], rhs, preferred_element_type=F32)
        total = part if total is None else total + part
    return total


def terms(geo, grads, x3, out):
    width, area, span = geo["width"], geo["area"], 3 * geo["group"]
    for dy in range(3):
        total = None
        for number, grad in enumerate(grads):
            part = lax.dot_general(
                grad,
                x3[number, pl.ds(dy * width, area), :],
                (((0,), (0,)), ((), ())),
                preferred_element_type=F32,
            )
            total = part if total is None else total + part
        out[:, dy * span : (dy + 1) * span] = total


def load_weights(geo, refs, w):
    if not geo["pairs"]:
        w[...] = refs[0][0]
        return
    own, far = refs
    e = lax.axis_index("de")
    half = own.shape[1]
    mine = lax.axis_index("da") == pl.program_id(0)

    def put(n):
        w[pl.ds(pl.multiple_of(e * half, half), half), :] = own[n]
        w[pl.ds(pl.multiple_of((1 - e) * half, half), half), :] = far[n]

    pl.when(mine)(lambda: put(0))
    pl.when(jnp.logical_not(mine))(lambda: put(1))


def split_terms(geo, total, refs):
    if not geo["pairs"]:
        refs[0][0] = total[...]
        return
    keep, send = refs
    e = lax.axis_index("de")
    half = keep.shape[1]
    keep[0] = total[pl.ds(pl.multiple_of(e * half, half), half), :]
    send[0] = total[pl.ds(pl.multiple_of((1 - e) * half, half), half), :].astype(BF16)


def weight_specs(geo):
    fan, group = geo["fan"], geo["group"]
    if geo["pairs"]:
        return [pl.BlockSpec((2, group // 2, fan), lambda s: (0, 0, 0))] * 2
    return [pl.BlockSpec((1, group, fan), lambda s: (s, 0, 0))]


def term_out(geo):
    fan, group, slots = geo["fan"], geo["group"], geo["slots"]
    if geo["pairs"]:
        spec = pl.BlockSpec((1, group // 2, fan), lambda s: (s, 0, 0))
        return [spec] * 2, [
            jax.ShapeDtypeStruct((slots, group // 2, fan), F32),
            jax.ShapeDtypeStruct((slots, group // 2, fan), BF16),
        ]
    spec = pl.BlockSpec((1, group, fan), lambda s: (s, 0, 0))
    return [spec], [jax.ShapeDtypeStruct((slots, group, fan), F32)]


def recv_spec(geo, which):
    return pl.BlockSpec(
        (geo["peers"], 1, 1, geo["piece"], geo["group"]), lambda s: (0, which, s, 0, 0)
    )


def map_spec(geo):
    return pl.BlockSpec((1, geo["maps"], geo["area"], geo["group"]), lambda s: (s, 0, 0, 0))


def map_shape(geo):
    return jax.ShapeDtypeStruct((geo["slots"], geo["maps"], geo["area"], geo["group"]), BF16)


def scratch(geo, weights, patches, total):
    fan, group = geo["fan"], geo["group"]
    shapes = [pltpu.VMEM((group, fan), BF16) for _ in range(weights)]
    rows = geo["area"] + 2 * geo["width"]
    shapes += [pltpu.VMEM((geo["maps"], rows, 3 * group), BF16) for _ in range(patches)]
    return shapes + ([pltpu.VMEM((group, fan), F32)] if total else [])


def conv_flops(geo):
    return 2 * geo["slots"] * geo["maps"] * geo["area"] * geo["group"] * geo["fan"]


def first_kernel(geo, *refs):
    nw = 2 if geo["pairs"] else 1
    wrefs, (rec_a, rec_d, h_out, s_out) = refs[:nw], refs[nw : nw + 4]
    t_out, (w, x3, total) = refs[nw + 4 : -3], refs[-3:]
    load_weights(geo, wrefs, w)
    hidden = []
    for n, value in enumerate(read_maps(geo, rec_a)):
        fill_patches(geo, x3, n, value)
        z = conv(geo, x3, n, w).astype(BF16).astype(F32)
        h, slope = act_both(z)
        h = h.astype(BF16)
        h_out[0, n] = h
        s_out[0, n] = slope.astype(BF16)
        hidden.append(h)
    for n, h in enumerate(hidden):
        fill_patches(geo, x3, n, h)
    terms(geo, read_maps(geo, rec_d), x3, total)
    split_terms(geo, total, t_out)


def first(geo, weights, recv):
    specs, shapes = term_out(geo)
    return pl.pallas_call(
        functools.partial(first_kernel, geo),
        grid=(geo["slots"],),
        in_specs=weight_specs(geo) + [recv_spec(geo, 0), recv_spec(geo, 1)],
        out_specs=[map_spec(geo)] * 2 + specs,
        out_shape=[map_shape(geo)] * 2 + shapes,
        scratch_shapes=scratch(geo, 1, 1, True),
        name="first",
        compiler_params=params(),
        cost_estimate=cost(2 * conv_flops(geo), 6e6),
    )(*weights, recv, recv)


def lower_kernel(geo, *refs):
    nw = 2 if geo["pairs"] else 1
    wrefs, (rec_a, rec_d, s_in, l_out) = refs[:nw], refs[nw : nw + 4]
    t_out, (w, x3, y3, total) = refs[nw + 4 : -4], refs[-4:]
    load_weights(geo, wrefs, w)
    lows = []
    for n, value in enumerate(read_maps(geo, rec_d)):
        fill_patches(geo, x3, n, value)
        low = (adjoint(geo, x3, n, w) * s_in[0, n].astype(F32)).astype(BF16)
        l_out[0, n] = low
        lows.append(low)
    for n, value in enumerate(read_maps(geo, rec_a)):
        fill_patches(geo, y3, n, value)
    terms(geo, lows, y3, total)
    split_terms(geo, total, t_out)


def lower(geo, weights, recv, slope):
    specs, shapes = term_out(geo)
    return pl.pallas_call(
        functools.partial(lower_kernel, geo),
        grid=(geo["slots"],),
        in_specs=weight_specs(geo) + [recv_spec(geo, 0), recv_spec(geo, 1), map_spec(geo)],
        out_specs=[map_spec(geo)] + specs,
        out_shape=[map_shape(geo)] + shapes,
        scratch_shapes=scratch(geo, 1, 2, True),
        name="lower",
        compiler_params=params(),
        cost_estimate=cost(2 * conv_flops(geo), 6e6),
    )(*weights, recv, recv, slope)


def last_kernel(geo, *refs):
    nw = 2 if geo["pairs"] else 1
    one, two = refs[:nw], refs[nw : 2 * nw]
    h_in, l_in, out, w, x3 = refs[2 * nw :]
    load_weights(geo, two, w)
    maps = []
    for n in range(geo["maps"]):
        fill_patches(geo, x3, n, h_in[0, n])
        maps.append((ALPHA * conv(geo, x3, n, w)).astype(BF16))
    write_maps(geo, out, 0, maps)
    load_weights(geo, one, w)
    maps = []
    for n in range(geo["maps"]):
        fill_patches(geo, x3, n, l_in[0, n])
        maps.append(adjoint(geo, x3, n, w).astype(BF16))
    write_maps(geo, out, 1, maps)


def last(geo, one, two, hidden, low):
    return pl.pallas_call(
        functools.partial(last_kernel, geo),
        grid=(geo["slots"],),
        in_specs=weight_specs(geo) * 2 + [map_spec(geo)] * 2,
        out_specs=pl.BlockSpec(
            (geo["peers"], 2, 1, geo["piece"], geo["group"]), lambda s: (0, 0, s, 0, 0)
        ),
        out_shape=jax.ShapeDtypeStruct(
            (geo["peers"], 2, geo["slots"], geo["piece"], geo["group"]), BF16
        ),
        scratch_shapes=scratch(geo, 1, 1, False),
        name="last",
        compiler_params=params(),
        cost_estimate=cost(2 * conv_flops(geo), 6e6),
    )(*one, *two, hidden, low)


def fold_kernel(keep, recv, mine, send):
    a = lax.axis_index("da")
    mine[...] = keep[a] + recv[a].astype(F32)
    send[...] = (keep[1 - a] + recv[1 - a].astype(F32)).astype(BF16)


def fold(keep, recv):
    shape = keep.shape[1:]
    return pl.pallas_call(
        fold_kernel,
        out_shape=(jax.ShapeDtypeStruct(shape, F32), jax.ShapeDtypeStruct(shape, BF16)),
        name="fold",
        compiler_params=params(),
        cost_estimate=cost(1e6, 2e6),
    )(keep, recv)


def swap(value, axis):
    return lax.ppermute(value, axis, [(0, 1), (1, 0)])


def gather_rows(geo, rows):
    if not geo["pairs"]:
        return (lax.all_gather(rows, ("da", "de"), axis=0, tiled=True).reshape(
            geo["slots"], geo["group"], geo["fan"]),)
    both = jnp.stack([rows, swap(rows, "da")])
    return (both, swap(both, "de"))


def sum_rows(geo, parts, kern, gain):
    if not geo["pairs"]:
        flat = parts[0].reshape(geo["slots"] * geo["group"], geo["fan"])
        total = lax.psum_scatter(flat, ("da", "de"), scatter_dimension=0, tiled=True)
        return pull_rows(kern, gain, total, jnp.zeros_like(total))
    keep, send = parts
    mine, other = fold(keep, swap(send, "de"))
    return pull_rows(kern, gain, mine, swap(other, "da"))


def local(group, features, cotangent, kernel_one, kernel_two, gain_one, gain_two):
    images, rows, cols, chans = features.shape
    fan = kernel_one.shape[2]
    nr, nc = lax.axis_size("row"), lax.axis_size("col")
    na, nb, ne = lax.axis_size("da"), lax.axis_size("db"), lax.axis_size("de")
    blocks = nr * nc
    geo = dict(
        group=group, fan=fan, nr=nr, nc=nc, nb=nb, blocks=blocks, slots=na,
        per_block=chans // blocks // group, peers=nb * blocks, images=images,
        rows=rows, cols=cols, piece=images * rows * cols, width=nc * cols,
        area=nr * rows * nc * cols, maps=nb * images, pairs=na == 2 and ne == 2,
    )
    flat = (images * rows * cols, chans)
    f, c = features.reshape(flat), cotangent.reshape(flat)
    k1, k2 = kernel_one.reshape(-1, fan), kernel_two.reshape(-1, fan)
    w1, w2 = std_rows(k1, k2, gain_one, gain_two)
    one = gather_rows(geo, w1)
    two = gather_rows(geo, w2)
    peers = ("db", "row", "col")
    recv = lax.all_to_all(pack(geo, f, c), peers, 0, 0, tiled=True)
    hidden, slope, *terms_two = first(geo, one, recv)
    low, *terms_one = lower(geo, two, recv, slope)
    sent = last(geo, one, two, hidden, low)
    back = lax.all_to_all(sent, peers, 0, 0, tiled=True)
    outputs, input_grad = merge(geo, f, c, back)
    grad_one = sum_rows(geo, terms_one, k1, gain_one)
    grad_two = sum_rows(geo, terms_two, k2, gain_two)
    return (
        outputs.reshape(features.shape),
        input_grad.reshape(features.shape),
        grad_one.reshape(kernel_one.shape),
        grad_two.reshape(kernel_two.shape),
    )


def solution(mesh):
    names = ("da", "db", "de", "row", "col")
    nr, nc, dp = mesh.shape["row"], mesh.shape["col"], mesh.shape["dp"]

    def run(features, cotangent, kernel_one, kernel_two, gain_one, gain_two):
        group = kernel_one.shape[2] // 9
        per_block = kernel_one.shape[1] // group
        na = 2 if per_block % 2 == 0 else 1
        nb = per_block // na
        fine = Mesh(mesh.devices.reshape(na, nb, dp // per_block, nr, nc), names)
        dps = ("da", "db", "de")
        cells = P(dps, "row", "col", None)
        rows = P(("row", "col"), dps, None)
        gains = P(("row", "col"), dps)
        return jax.shard_map(
            functools.partial(local, group),
            mesh=fine,
            in_specs=(cells, cells, rows, rows, gains, gains),
            out_specs=(cells, cells, rows, rows),
            check_vma=False,
        )(features, cotangent, kernel_one, kernel_two, gain_one, gain_two)

    return run
```

profile of v0, /device:TPU:0, one launch (start us, length us, event | category | flops | bytes accessed | tf_op | source)
XLA Modules:
  0.0 86.2 jit_solution(11851249379604559345)
XLA Ops:
  0.6 1.0 %copy-done = bf16[1,4,32,2048]{3,2,1,0:T(8,128)(2,1)S(1)} copy-done((bf16[1,4,32,2048]{3,2,1,0:T(8,128)(2,1)S(1)}, bf16[1,4,32,2048]{3,2,1,0:T(8,128)(2,1)}, u32[]{:S(2)}) %copy-start) | copy-done | bytes 524312
  1.7 1.0 %copy-done.2 = bf16[1,4,32,2048]{3,2,1,0:T(8,128)(2,1)S(1)} copy-done((bf16[1,4,32,2048]{3,2,1,0:T(8,128)(2,1)S(1)}, bf16[1,4,32,2048]{3,2,1,0:T(8,128)(2,1)}, u32[]{:S(2)}) %copy-start.2) | copy-done | bytes 524312
  2.7 1.4 %pack.1 = bf16[8,2,2,128,128]{4,3,2,1,0:T(8,128)(2,1)} custom-call(bf16[128,2048]{1,0:T(8,128)(2,1)S(1)} %bitcast.12, bf16[128,2048]{1,0:T(8,128)(2,1)S(1)} %bitcast.14), custom_call_target="tpu_custom_call" | custom-call | flops 4000000 | bytes 4000000 | tf_op jit(solution)/shard_map/pack/pallas_call | solution.py:114
  4.2 5.4 %all-to-all-start = ((bf16[8,2,2,128,128]{4,3,2,1,0:T(8,128)(2,1)}), bf16[8,2,2,128,128]{4,3,2,1,0:T(8,128)(2,1)S(1)}, u32[]{:S(2)}, u32[]{:S(2)}) async-start(bf16[8,2,2,128,128]{4,3,2,1,0:T(8,128)(2,1)} %pack.1), calls=%async_computation | async-start | bytes 2097152 | tf_op jit(solution)/shard_map/all_to_all | solution.py:463
  10.5 2.7 %collective-permute-start = (bf16[64,1152]{1,0:T(8,128)(2,1)S(1)}, bf16[64,1152]{1,0:T(8,128)(2,1)S(1)}, u32[]{:S(2)}, u32[]{:S(2)}) collective-permute-start(bf16[64,1152]{1,0:T(8,128)(2,1)S(1)} %get-tuple-element.19), channel_id=1, source_target_pairs={{0,16},{16,0},{1,17},{17,1},{2,18},{18,2},{3,19},{19,3},{4,20},{20... | collective-permute-start | bytes 442376 | tf_op jit(solution)/shard_map/ppermute | solution.py:423
  13.5 11.8 %collective-permute-done = bf16[64,1152]{1,0:T(8,128)(2,1)S(1)} collective-permute-done((bf16[64,1152]{1,0:T(8,128)(2,1)S(1)}, bf16[64,1152]{1,0:T(8,128)(2,1)S(1)}, u32[]{:S(2)}, u32[]{:S(2)}) %collective-permute-start) | collective-permute-done | bytes 147488 | tf_op jit(solution)/shard_map/ppermute | solution.py:423
  25.3 1.6 %collective-permute-start.1 = (bf16[2,64,1152]{2,1,0:T(8,128)(2,1)S(1)}, bf16[2,64,1152]{2,1,0:T(8,128)(2,1)S(1)}, u32[]{:S(2)}, u32[]{:S(2)}) collective-permute-start(bf16[2,64,1152]{2,1,0:T(8,128)(2,1)S(1)} %pad_maximum_fusion.refs_0_), channel_id=1, source_target_pairs={{0,4},{4,0},{1,5},{5,1},{2,6},{6,2},{3,7},{7,3},{8,12},{12,8},{9,1... | collective-permute-start | bytes 884744 | tf_op jit(solution)/shard_map/ppermute | solution.py:423
  26.9 1.4 %collective-permute-done.2 = bf16[64,1152]{1,0:T(8,128)(2,1)S(1)} collective-permute-done((bf16[64,1152]{1,0:T(8,128)(2,1)S(1)}, bf16[64,1152]{1,0:T(8,128)(2,1)S(1)}, u32[]{:S(2)}, u32[]{:S(2)}) %collective-permute-start.2) | collective-permute-done | bytes 147488 | tf_op jit(solution)/shard_map/ppermute | solution.py:423
  28.3 1.6 %collective-permute-start.3 = (bf16[2,64,1152]{2,1,0:T(8,128)(2,1)S(1)}, bf16[2,64,1152]{2,1,0:T(8,128)(2,1)}, u32[]{:S(2)}, u32[]{:S(2)}) collective-permute-start(bf16[2,64,1152]{2,1,0:T(8,128)(2,1)S(1)} %pad_maximum_fusion.1.refs_0_.refs_2_), channel_id=1, source_target_pairs={{0,4},{4,0},{1,5},{5,1},{2,6},{6,2},{3,7},{7,3},{8,12},{12,8},{9,1... | collective-permute-start | bytes 884744 | tf_op jit(solution)/shard_map/ppermute | solution.py:423
  29.8 5.4 %collective-permute-done.1.refs_1_ = bf16[2,64,1152]{2,1,0:T(8,128)(2,1)S(1)} collective-permute-done((bf16[2,64,1152]{2,1,0:T(8,128)(2,1)S(1)}, bf16[2,64,1152]{2,1,0:T(8,128)(2,1)S(1)}, u32[]{:S(2)}, u32[]{:S(2)}) %collective-permute-start.1) | collective-permute-done | bytes 294944 | tf_op jit(solution)/shard_map/ppermute | solution.py:423
  35.3 3.8 %first.1 = (bf16[2,2,512,128]{3,2,1,0:T(8,128)(2,1)S(1)}, bf16[2,2,512,128]{3,2,1,0:T(8,128)(2,1)S(1)}, f32[2,64,1152]{2,1,0:T(8,128)S(1)}, bf16[2,64,1152]{2,1,0:T(8,128)(2,1)S(1)}) custom-call(bf16[2,64,1152]{2,1,0:T(8,128)(2,1)S(1)} %pad_maximum_fusion.refs_0_, bf16[2,64,1152]{2,1,0:T(8,128)(2,1)S(1)} %collective-permute-done.1.refs_1_, ...), custom_call_target="tpu_custom_call" | custom-call | flops 1207959552 | bytes 6000000 | tf_op jit(solution)/shard_map/first/pallas_call | solution.py:324
  40.5 1.0 %copy-done.7 = bf16[2,64,1152]{2,1,0:T(8,128)(2,1)S(1)} copy-done((bf16[2,64,1152]{2,1,0:T(8,128)(2,1)S(1)}, bf16[2,64,1152]{2,1,0:T(8,128)(2,1)}, u32[]{:S(2)}) %copy-start.7) | copy-done | bytes 294936
  41.4 4.1 %lower.1 = (bf16[2,2,512,128]{3,2,1,0:T(8,128)(2,1)S(1)}, f32[2,64,1152]{2,1,0:T(8,128)S(1)}, bf16[2,64,1152]{2,1,0:T(8,128)(2,1)S(1)}) custom-call(bf16[2,64,1152]{2,1,0:T(8,128)(2,1)S(1)} %copy-done.7, bf16[2,64,1152]{2,1,0:T(8,128)(2,1)} %collective-permute-done.3.refs_1_.refs_3_, bf16[8,2,2,128,128]{4,3,2,1,0:T(8,128)(2,1)S(1)} %all-to-all-done.refs_2_.refs_3_, ...), custom_call_target="tpu_custom_call" | custom-call | flops 1207959552 | bytes 6000000 | tf_op jit(solution)/shard_map/lower/pallas_call | solution.py:356
  45.6 0.7 copy-done.11
  46.3 5.1 %last.1 = bf16[8,2,2,128,128]{4,3,2,1,0:T(8,128)(2,1)} custom-call(bf16[2,64,1152]{2,1,0:T(8,128)(2,1)S(1)} %pad_maximum_fusion.refs_0_, bf16[2,64,1152]{2,1,0:T(8,128)(2,1)S(1)} %copy-done.14, bf16[2,64,1152]{2,1,0:T(8,128)(2,1)S(1)} %copy-done.8, bf16[2,64,1152]{2,1,0:T(8,128)(2,1)} %collective-permute-done.3.refs_1_.refs_3_, ...), custom_call_target="tpu_custom_call" | custom-call | flops 1207959552 | bytes 6000000 | tf_op jit(solution)/shard_map/last/pallas_call | solution.py:388
  51.3 6.7 %all-to-all-start.1 = ((bf16[8,2,2,128,128]{4,3,2,1,0:T(8,128)(2,1)}), bf16[8,2,2,128,128]{4,3,2,1,0:T(8,128)(2,1)S(1)}, u32[]{:S(2)}, u32[]{:S(2)}) async-start(bf16[8,2,2,128,128]{4,3,2,1,0:T(8,128)(2,1)} %last.1), calls=%async_computation.1 | async-start | bytes 2097152 | tf_op jit(solution)/shard_map/all_to_all | solution.py:467
  58.0 1.6 %collective-permute-start.6 = (bf16[2,64,1152]{2,1,0:T(8,128)(2,1)S(1)}, bf16[2,64,1152]{2,1,0:T(8,128)(2,1)S(1)}, u32[]{:S(2)}, u32[]{:S(2)}) collective-permute-start(bf16[2,64,1152]{2,1,0:T(8,128)(2,1)S(1)} %copy-done.16), channel_id=1, source_target_pairs={{0,4},{4,0},{1,5},{5,1},{2,6},{6,2},{3,7},{7,3},{8,12},{12,8},{9,1... | collective-permute-start | bytes 884744 | tf_op jit(solution)/shard_map/ppermute | solution.py:423
  60.1 7.8 %collective-permute-done.6.recv = bf16[2,64,1152]{2,1,0:T(8,128)(2,1)S(1)} collective-permute-done((bf16[2,64,1152]{2,1,0:T(8,128)(2,1)S(1)}, bf16[2,64,1152]{2,1,0:T(8,128)(2,1)S(1)}, u32[]{:S(2)}, u32[]{:S(2)}) %collective-permute-start.6) | collective-permute-done | bytes 294944 | tf_op jit(solution)/shard_map/ppermute | solution.py:423
  68.5 5.3 %collective-permute-done.4.recv = bf16[2,64,1152]{2,1,0:T(8,128)(2,1)S(1)} collective-permute-done((bf16[2,64,1152]{2,1,0:T(8,128)(2,1)S(1)}, bf16[2,64,1152]{2,1,0:T(8,128)(2,1)S(1)}, u32[]{:S(2)}, u32[]{:S(2)}) %collective-permute-start.4) | collective-permute-done | bytes 294944 | tf_op jit(solution)/shard_map/ppermute | solution.py:423
  74.2 2.9 %collective-permute-done.7.recv = bf16[64,1152]{1,0:T(8,128)(2,1)S(1)} collective-permute-done((bf16[64,1152]{1,0:T(8,128)(2,1)S(1)}, bf16[64,1152]{1,0:T(8,128)(2,1)S(1)}, u32[]{:S(2)}, u32[]{:S(2)}) %collective-permute-start.7) | collective-permute-done | bytes 147488 | tf_op jit(solution)/shard_map/ppermute | solution.py:423
  77.1 1.0 %pull_rows.3 = f32[64,1152]{1,0:T(8,128)} custom-call(f32[64,1152]{1,0:T(8,128)S(1)} %bitcast.17, f32[1,64]{1,0:T(1,128)S(1)} %copy-done.9, f32[64,1152]{1,0:T(8,128)S(1)} %get-tuple-element.32.keep, bf16[64,1152]{1,0:T(8,128)(2,1)S(1)} %collective-permute-done.7.recv), custom_call_target="tpu_custom_call" | custom-call | flops 1000000 | bytes 4000000 | tf_op jit(solution)/shard_map/pull_rows/pallas_call | solution.py:92
  78.2 5.3 %collective-permute-done.5.recv = bf16[64,1152]{1,0:T(8,128)(2,1)S(1)} collective-permute-done((bf16[64,1152]{1,0:T(8,128)(2,1)S(1)}, bf16[64,1152]{1,0:T(8,128)(2,1)S(1)}, u32[]{:S(2)}, u32[]{:S(2)}) %collective-permute-start.5) | collective-permute-done | bytes 147488 | tf_op jit(solution)/shard_map/ppermute | solution.py:423
  83.4 1.0 %pull_rows.2 = f32[64,1152]{1,0:T(8,128)} custom-call(f32[64,1152]{1,0:T(8,128)S(1)} %bitcast.19, f32[1,64]{1,0:T(1,128)S(1)} %copy-done.10, f32[64,1152]{1,0:T(8,128)S(1)} %get-tuple-element.28.keep, bf16[64,1152]{1,0:T(8,128)(2,1)S(1)} %collective-permute-done.5.recv), custom_call_target="tpu_custom_call" | custom-call | flops 1000000 | bytes 4000000 | tf_op jit(solution)/shard_map/pull_rows/pallas_call | solution.py:92
  84.5 1.8 %merge.1 = (bf16[128,2048]{1,0:T(8,128)(2,1)}, bf16[128,2048]{1,0:T(8,128)(2,1)}) custom-call(bf16[128,2048]{1,0:T(8,128)(2,1)S(1)} %bitcast.13, bf16[128,2048]{1,0:T(8,128)(2,1)S(1)} %bitcast.15, bf16[8,2,2,128,128]{4,3,2,1,0:T(8,128)(2,1)S(1)} %all-to-all-done.1.recv), custom_call_target="tpu_custom_call" | custom-call | flops 4000000 | bytes 6000000 | tf_op jit(solution)/shard_map/merge/pallas_call | solution.py:138
  (42 shorter events, 4.2 us)
Async XLA Ops:
  0.6 1.0 %copy-start = (bf16[1,4,32,2048]{3,2,1,0:T(8,128)(2,1)S(1)}, bf16[1,4,32,2048]{3,2,1,0:T(8,128)(2,1)}, u32[]{:S(2)}) copy-start(bf16[1,4,32,2048]{3,2,1,0:T(8,128)(2,1)} %param.6) | copy-start | bytes 1572868
  1.7 1.0 %copy-start.2 = (bf16[1,4,32,2048]{3,2,1,0:T(8,128)(2,1)S(1)}, bf16[1,4,32,2048]{3,2,1,0:T(8,128)(2,1)}, u32[]{:S(2)}) copy-start(bf16[1,4,32,2048]{3,2,1,0:T(8,128)(2,1)} %param.7) | copy-start | bytes 1572868
  4.1 5.4 %copy-start.4 = (f32[1,64,1152]{2,1,0:T(8,128)S(1)}, f32[1,64,1152]{2,1,0:T(8,128)}, u32[]{:S(2)}) copy-start(f32[1,64,1152]{2,1,0:T(8,128)} %param.9) | copy-start | bytes 884740
  4.1 5.4 %copy-start.5 = (f32[1,64,1152]{2,1,0:T(8,128)S(1)}, f32[1,64,1152]{2,1,0:T(8,128)}, u32[]{:S(2)}) copy-start(f32[1,64,1152]{2,1,0:T(8,128)} %param.8) | copy-start | bytes 884740
  4.2 31.1 %all-to-all-start = ((bf16[8,2,2,128,128]{4,3,2,1,0:T(8,128)(2,1)}), bf16[8,2,2,128,128]{4,3,2,1,0:T(8,128)(2,1)S(1)}, u32[]{:S(2)}, u32[]{:S(2)}) async-start(bf16[8,2,2,128,128]{4,3,2,1,0:T(8,128)(2,1)} %pack.1), calls=%async_computation | async-start | bytes 2097152 | tf_op jit(solution)/shard_map/all_to_all | solution.py:463
  10.5 14.8 %collective-permute-start = (bf16[64,1152]{1,0:T(8,128)(2,1)S(1)}, bf16[64,1152]{1,0:T(8,128)(2,1)S(1)}, u32[]{:S(2)}, u32[]{:S(2)}) collective-permute-start(bf16[64,1152]{1,0:T(8,128)(2,1)S(1)} %get-tuple-element.19), channel_id=1, source_target_pairs={{0,16},{16,0},{1,17},{17,1},{2,18},{18,2},{3,19},{19,3},{4,20},{20... | collective-permute-start | bytes 442376 | tf_op jit(solution)/shard_map/ppermute | solution.py:423
  13.1 15.1 %collective-permute-start.2 = (bf16[64,1152]{1,0:T(8,128)(2,1)S(1)}, bf16[64,1152]{1,0:T(8,128)(2,1)S(1)}, u32[]{:S(2)}, u32[]{:S(2)}) collective-permute-start(bf16[64,1152]{1,0:T(8,128)(2,1)S(1)} %get-tuple-element.20), channel_id=1, source_target_pairs={{0,16},{16,0},{1,17},{17,1},{2,18},{18,2},{3,19},{19,3},{4,20},{20... | collective-permute-start | bytes 442376 | tf_op jit(solution)/shard_map/ppermute | solution.py:423
  25.3 10.0 %collective-permute-start.1 = (bf16[2,64,1152]{2,1,0:T(8,128)(2,1)S(1)}, bf16[2,64,1152]{2,1,0:T(8,128)(2,1)S(1)}, u32[]{:S(2)}, u32[]{:S(2)}) collective-permute-start(bf16[2,64,1152]{2,1,0:T(8,128)(2,1)S(1)} %pad_maximum_fusion.refs_0_), channel_id=1, source_target_pairs={{0,4},{4,0},{1,5},{5,1},{2,6},{6,2},{3,7},{7,3},{8,12},{12,8},{9,1... | collective-permute-start | bytes 884744 | tf_op jit(solution)/shard_map/ppermute | solution.py:423
  28.3 10.8 %copy-start.6 = (bf16[2,64,1152]{2,1,0:T(8,128)(2,1)}, bf16[2,64,1152]{2,1,0:T(8,128)(2,1)S(1)}, u32[]{:S(2)}) copy-start(bf16[2,64,1152]{2,1,0:T(8,128)(2,1)S(1)} %pad_maximum_fusion.1.refs_0_.refs_2_) | copy-start | bytes 884740
  28.3 12.2 %collective-permute-start.3 = (bf16[2,64,1152]{2,1,0:T(8,128)(2,1)S(1)}, bf16[2,64,1152]{2,1,0:T(8,128)(2,1)}, u32[]{:S(2)}, u32[]{:S(2)}) collective-permute-start(bf16[2,64,1152]{2,1,0:T(8,128)(2,1)S(1)} %pad_maximum_fusion.1.refs_0_.refs_2_), channel_id=1, source_target_pairs={{0,4},{4,0},{1,5},{5,1},{2,6},{6,2},{3,7},{7,3},{8,12},{12,8},{9,1... | collective-permute-start | bytes 884744 | tf_op jit(solution)/shard_map/ppermute | solution.py:423
  35.3 3.8 %copy-start.13 = (bf16[2,64,1152]{2,1,0:T(8,128)(2,1)}, bf16[2,64,1152]{2,1,0:T(8,128)(2,1)S(1)}, u32[]{:S(2)}) copy-start(bf16[2,64,1152]{2,1,0:T(8,128)(2,1)S(1)} %collective-permute-done.1.refs_1_) | copy-start | bytes 884740
  40.5 1.0 %copy-start.7 = (bf16[2,64,1152]{2,1,0:T(8,128)(2,1)S(1)}, bf16[2,64,1152]{2,1,0:T(8,128)(2,1)}, u32[]{:S(2)}) copy-start(bf16[2,64,1152]{2,1,0:T(8,128)(2,1)} %copy-done.6) | copy-start | bytes 884740
  41.4 4.9 %copy-start.8 = (bf16[2,64,1152]{2,1,0:T(8,128)(2,1)S(1)}, bf16[2,64,1152]{2,1,0:T(8,128)(2,1)}, u32[]{:S(2)}) copy-start(bf16[2,64,1152]{2,1,0:T(8,128)(2,1)} %copy-done.6) | copy-start | bytes 884740
  41.4 4.9 %copy-start.14 = (bf16[2,64,1152]{2,1,0:T(8,128)(2,1)S(1)}, bf16[2,64,1152]{2,1,0:T(8,128)(2,1)}, u32[]{:S(2)}) copy-start(bf16[2,64,1152]{2,1,0:T(8,128)(2,1)} %copy-done.13) | copy-start | bytes 884740
  45.6 0.7 copy-start.11
  51.3 6.7 %copy-start.16 = (bf16[2,64,1152]{2,1,0:T(8,128)(2,1)S(1)}, bf16[2,64,1152]{2,1,0:T(8,128)(2,1)}, u32[]{:S(2)}) copy-start(bf16[2,64,1152]{2,1,0:T(8,128)(2,1)} %copy-done.15) | copy-start | bytes 884740
  51.3 8.3 %copy-start.12 = (bf16[2,64,1152]{2,1,0:T(8,128)(2,1)S(1)}, bf16[2,64,1152]{2,1,0:T(8,128)(2,1)}, u32[]{:S(2)}) copy-start(bf16[2,64,1152]{2,1,0:T(8,128)(2,1)} %copy-done.11) | copy-start | bytes 884740
  51.3 33.1 %all-to-all-start.1 = ((bf16[8,2,2,128,128]{4,3,2,1,0:T(8,128)(2,1)}), bf16[8,2,2,128,128]{4,3,2,1,0:T(8,128)(2,1)S(1)}, u32[]{:S(2)}, u32[]{:S(2)}) async-start(bf16[8,2,2,128,128]{4,3,2,1,0:T(8,128)(2,1)} %last.1), calls=%async_computation.1 | async-start | bytes 2097152 | tf_op jit(solution)/shard_map/all_to_all | solution.py:467
  58.0 9.9 %collective-permute-start.6 = (bf16[2,64,1152]{2,1,0:T(8,128)(2,1)S(1)}, bf16[2,64,1152]{2,1,0:T(8,128)(2,1)S(1)}, u32[]{:S(2)}, u32[]{:S(2)}) collective-permute-start(bf16[2,64,1152]{2,1,0:T(8,128)(2,1)S(1)} %copy-done.16), channel_id=1, source_target_pairs={{0,4},{4,0},{1,5},{5,1},{2,6},{6,2},{3,7},{7,3},{8,12},{12,8},{9,1... | collective-permute-start | bytes 884744 | tf_op jit(solution)/shard_map/ppermute | solution.py:423
  59.6 14.2 %collective-permute-start.4 = (bf16[2,64,1152]{2,1,0:T(8,128)(2,1)S(1)}, bf16[2,64,1152]{2,1,0:T(8,128)(2,1)S(1)}, u32[]{:S(2)}, u32[]{:S(2)}) collective-permute-start(bf16[2,64,1152]{2,1,0:T(8,128)(2,1)S(1)} %copy-done.12), channel_id=1, source_target_pairs={{0,4},{4,0},{1,5},{5,1},{2,6},{6,2},{3,7},{7,3},{8,12},{12,8},{9,1... | collective-permute-start | bytes 884744 | tf_op jit(solution)/shard_map/ppermute | solution.py:423
  68.0 9.1 %collective-permute-start.7 = (bf16[64,1152]{1,0:T(8,128)(2,1)S(1)}, bf16[64,1152]{1,0:T(8,128)(2,1)S(1)}, u32[]{:S(2)}, u32[]{:S(2)}) collective-permute-start(bf16[64,1152]{1,0:T(8,128)(2,1)S(1)} %get-tuple-element.33), channel_id=1, source_target_pairs={{0,16},{16,0},{1,17},{17,1},{2,18},{18,2},{3,19},{19,3},{4,20},{20... | collective-permute-start | bytes 442376 | tf_op jit(solution)/shard_map/ppermute | solution.py:423
  73.9 9.6 %collective-permute-start.5 = (bf16[64,1152]{1,0:T(8,128)(2,1)S(1)}, bf16[64,1152]{1,0:T(8,128)(2,1)S(1)}, u32[]{:S(2)}, u32[]{:S(2)}) collective-permute-start(bf16[64,1152]{1,0:T(8,128)(2,1)S(1)} %get-tuple-element.29), channel_id=1, source_target_pairs={{0,16},{16,0},{1,17},{17,1},{2,18},{18,2},{3,19},{19,3},{4,20},{20... | collective-permute-start | bytes 442376 | tf_op jit(solution)/shard_map/ppermute | solution.py:423
  77.1 7.4 %copy-start.3 = (bf16[1,4,32,2048]{3,2,1,0:T(8,128)(2,1)S(1)}, bf16[1,4,32,2048]{3,2,1,0:T(8,128)(2,1)}, u32[]{:S(2)}) copy-start(bf16[1,4,32,2048]{3,2,1,0:T(8,128)(2,1)} %param.7) | copy-start | bytes 1572868
  78.2 6.3 %copy-start.1 = (bf16[1,4,32,2048]{3,2,1,0:T(8,128)(2,1)S(1)}, bf16[1,4,32,2048]{3,2,1,0:T(8,128)(2,1)}, u32[]{:S(2)}) copy-start(bf16[1,4,32,2048]{3,2,1,0:T(8,128)(2,1)} %param.6) | copy-start | bytes 1572868
  (3 other events, 2.0 us)
where the time goes:
time: 86.7 us; the launch traced here: 86.2 us
  waiting for transfers between devices  40.5 us (47%)
  starting transfers between devices  21.1 us (24%)
  Pallas kernels  18.7 us (22%)
  local copies, waits for them, and re-layouts  5.14 us (6%)
    ppermute x8, waiting for transfers between devices, swap(): return lax.ppermute(value, axis, [(0, 1), (1, 0)])  40.5 us
    ppermute x8, starting transfers between devices, swap(): return lax.ppermute(value, axis, [(0, 1), (1, 0)])  9.02 us
    all_to_all x1, starting transfers between devices, local(): back = lax.all_to_all(sent, peers, 0, 0, tiled=True)  6.69 us
    all_to_all x1, starting transfers between devices, local(): recv = lax.all_to_all(pack(geo, f, c), peers, 0, 0, tiled=True)  5.39 us
    unnamed x34, local copies, waits for them, and re-layouts  5.14 us
    pallas_call x1, Pallas kernels, last(): pl.pallas_call(functools.partial(last_kernel, geo), grid=(geo['slots'],),...  5.05 us
    pallas_call x1, Pallas kernels, lower(): pl.pallas_call(functools.partial(lower_kernel, geo), grid=(geo['slots'],)...  4.14 us
    pallas_call x1, Pallas kernels, first(): pl.pallas_call(functools.partial(first_kernel, geo), grid=(geo['slots'],)...  3.79 us
  transfers between devices with their start and end apart: 10, of which 8 were waited for; matrix products, arithmetic and copies ran while one was open for 0% of the time, Pallas kernels for 7%

commit v1 on v0

--- a/solution.py
+++ b/solution.py
@@ -15,7 +15,12 @@
 CUBE = 0.044715
 F32 = jnp.float32
 BF16 = jnp.bfloat16
-VMEM_LIMIT = 48 * 1024 * 1024
+VMEM_LIMIT = 24 * 1024 * 1024
+SMALL = 1
+RELAY = 20_000_000_000
+FIRST = 3_000_000_000
+SECOND = LOWER = RELAY
+PULL = MERGE = SMALL
 
 
 def act_value(x):
@@ -42,8 +47,12 @@
     return pltpu.CompilerParams(vmem_limit_bytes=VMEM_LIMIT, **kw)
 
 
-def cost(flops, size):
-    return pl.CostEstimate(flops=int(flops), bytes_accessed=int(size), transcendentals=0)
+def pin(x):
+    return pltpu.with_memory_space_constraint(x, pltpu.HBM)
+
+
+def cost(flops):
+    return pl.CostEstimate(flops=flops, bytes_accessed=1, transcendentals=0)
 
 
 def column(gain_ref):
@@ -54,31 +63,19 @@
     return jnp.sum(jnp.where(first == second, spread, 0.0), axis=1, keepdims=True)
 
 
-def std_kernel(k1, k2, g1, g2, w1, w2):
-    for k, g, w in ((k1, g1, w1), (k2, g2, w2)):
-        fan = k.shape[1]
-        kern = k[...]
-        cent = kern - jnp.mean(kern, axis=1, keepdims=True)
-        var = jnp.mean(cent * cent, axis=1, keepdims=True)
-        scale = column(g) * lax.rsqrt(var + EPS) * (1.0 / math.sqrt(fan))
-        w[...] = (cent * scale).astype(BF16)
-
-
-def std_rows(k1, k2, g1, g2):
-    shape = jax.ShapeDtypeStruct(k1.shape, BF16)
-    return pl.pallas_call(
-        std_kernel,
-        out_shape=(shape, shape),
-        name="std_rows",
-        compiler_params=params(),
-        cost_estimate=cost(1e6, 4e6),
-    )(k1, k2, g1, g2)
-
-
-def pull_kernel(k, g, keep, recv, out):
+def std_into(k, g, w):
     fan = k.shape[1]
     kern = k[...]
-    grad = keep[...].astype(F32) + recv[...].astype(F32)
+    cent = kern - jnp.mean(kern, axis=1, keepdims=True)
+    var = jnp.mean(cent * cent, axis=1, keepdims=True)
+    scale = column(g) * lax.rsqrt(var + EPS) * (1.0 / math.sqrt(fan))
+    w[...] = (cent * scale).astype(BF16)
+
+
+def pull_kernel(k, g, keep, near, over, out):
+    fan = k.shape[1]
+    kern = k[...]
+    grad = keep[...] + near[...].astype(F32) + over[...].astype(F32)
     cent = kern - jnp.mean(kern, axis=1, keepdims=True)
     var = jnp.mean(cent * cent, axis=1, keepdims=True)
     inv = lax.rsqrt(var + EPS)
@@ -88,36 +85,58 @@
     out[...] = term - jnp.mean(term, axis=1, keepdims=True)
 
 
-def pull_rows(k, g, keep, recv):
+def pull_rows(k, g, sums, flops):
     return pl.pallas_call(
         pull_kernel,
         out_shape=jax.ShapeDtypeStruct(k.shape, F32),
         name="pull_rows",
         compiler_params=params(),
-        cost_estimate=cost(1e6, 4e6),
-    )(k, g, keep, recv)
-
-
-def pack_kernel(geo, f, c, out):
+        cost_estimate=cost(flops),
+    )(k, g, *sums)
+
+
+def prep_kernel(geo, k1, k2, g1, g2, f, c, w1, w2, out, k1_in, k2_in, g1_in, g2_in, f_in, c_in, sems):
+    group = geo["group"]
+    span = geo["per_block"] * group
+    moves = [
+        pltpu.make_async_copy(src, dst, sems.at[n])
+        for n, (src, dst) in enumerate(((k1, k1_in), (g1, g1_in), (k2, k2_in), (g2, g2_in)))
+    ]
+    for n in range(geo["blocks"]):
+        cut = pl.ds(n * span, span)
+        for src, dst in ((f, f_in), (c, c_in)):
+            moves.append(pltpu.make_async_copy(src.at[:, cut], dst.at[:, cut], sems.at[len(moves)]))
+    for move in moves:
+        move.start()
+    for n, (k, g, w) in enumerate(((k1_in, g1_in, w1), (k2_in, g2_in, w2))):
+        moves[2 * n].wait()
+        moves[2 * n + 1].wait()
+        std_into(k, g, w)
+    for block in range(geo["blocks"]):
+        moves[4 + 2 * block].wait()
+        moves[5 + 2 * block].wait()
+        for b in range(geo["nb"]):
+            dst = b * geo["blocks"] + block
+            for slot in range(geo["slots"]):
+                at = (block * geo["per_block"] + slot * geo["nb"] + b) * group
+                out[dst, 0, slot] = act_value(f_in[:, at : at + group].astype(F32)).astype(BF16)
+                out[dst, 1, slot] = (ALPHA * c_in[:, at : at + group].astype(F32)).astype(BF16)
+
+
+def prep(geo, k1, k2, g1, g2, f, c):
     cells = f.shape[0]
-    group = geo["group"]
-    for dst in range(geo["peers"]):
-        b, block = dst // geo["blocks"], dst % geo["blocks"]
-        for slot in range(geo["slots"]):
-            at = (block * geo["per_block"] + slot * geo["nb"] + b) * group
-            out[dst, 0, slot] = act_value(f[:, at : at + group].astype(F32)).astype(BF16)
-            out[dst, 1, slot] = (ALPHA * c[:, at : at + group].astype(F32)).astype(BF16)
-
-
-def pack(geo, f, c):
-    cells = f.shape[0]
+    args = (k1, k2, g1, g2, f, c)
     return pl.pallas_call(
-        functools.partial(pack_kernel, geo),
-        out_shape=jax.ShapeDtypeStruct((geo["peers"], 2, geo["slots"], cells, geo["group"]), BF16),
-        name="pack",
+        functools.partial(prep_kernel, geo),
+        in_specs=[pl.BlockSpec(memory_space=pl.ANY)] * 6,
+        out_shape=[jax.ShapeDtypeStruct(k1.shape, BF16)] * 2
+        + [jax.ShapeDtypeStruct((geo["peers"], 2, geo["slots"], cells, geo["group"]), BF16)],
+        scratch_shapes=[pltpu.VMEM(x.shape, x.dtype) for x in args]
+        + [pltpu.SemaphoreType.DMA((4 + 2 * geo["blocks"],))],
+        name="prep",
         compiler_params=params(),
-        cost_estimate=cost(4e6, 4e6),
-    )(f, c)
+        cost_estimate=cost(SMALL),
+    )(*[pin(x) for x in args])
 
 
 def merge_kernel(geo, f, c, recv, out, grad):
@@ -140,7 +159,7 @@
         out_shape=(shape, shape),
         name="merge",
         compiler_params=params(),
-        cost_estimate=cost(4e6, 6e6),
+        cost_estimate=cost(MERGE),
     )(f, c, recv)
 
 
@@ -247,11 +266,17 @@
     if not geo["pairs"]:
         refs[0][0] = total[...]
         return
-    keep, send = refs
+    keep_near, keep_far, send_near, send_far = refs
     e = lax.axis_index("de")
-    half = keep.shape[1]
-    keep[0] = total[pl.ds(pl.multiple_of(e * half, half), half), :]
-    send[0] = total[pl.ds(pl.multiple_of((1 - e) * half, half), half), :].astype(BF16)
+    half = keep_near.shape[0]
+    mine = lax.axis_index("da") == pl.program_id(0)
+
+    def put(keep, send):
+        keep[...] = total[pl.ds(pl.multiple_of(e * half, half), half), :]
+        send[...] = total[pl.ds(pl.multiple_of((1 - e) * half, half), half), :].astype(BF16)
+
+    pl.when(mine)(lambda: put(keep_near, send_near))
+    pl.when(jnp.logical_not(mine))(lambda: put(keep_far, send_far))
 
 
 def weight_specs(geo):
@@ -264,19 +289,26 @@
 def term_out(geo):
     fan, group, slots = geo["fan"], geo["group"], geo["slots"]
     if geo["pairs"]:
-        spec = pl.BlockSpec((1, group // 2, fan), lambda s: (s, 0, 0))
-        return [spec] * 2, [
-            jax.ShapeDtypeStruct((slots, group // 2, fan), F32),
-            jax.ShapeDtypeStruct((slots, group // 2, fan), BF16),
-        ]
+        shape = (group // 2, fan)
+        return [pl.BlockSpec(shape, lambda s: (0, 0))] * 4, [
+            jax.ShapeDtypeStruct(shape, t) for t in (F32, F32, BF16, BF16)]
     spec = pl.BlockSpec((1, group, fan), lambda s: (s, 0, 0))
     return [spec], [jax.ShapeDtypeStruct((slots, group, fan), F32)]
 
 
 def recv_spec(geo, which):
-    return pl.BlockSpec(
-        (geo["peers"], 1, 1, geo["piece"], geo["group"]), lambda s: (0, which, s, 0, 0)
-    )
+    dims = (geo["peers"], 1, 1, geo["piece"], geo["group"])
+    return pl.BlockSpec(dims, lambda s: (0, which, s, 0, 0))
+
+
+def send_spec(geo):
+    dims = (geo["peers"], 2, 1, geo["piece"], geo["group"])
+    return pl.BlockSpec(dims, lambda s: (0, 0, s, 0, 0))
+
+
+def send_shape(geo):
+    return jax.ShapeDtypeStruct(
+        (geo["peers"], 2, geo["slots"], geo["piece"], geo["group"]), BF16)
 
 
 def map_spec(geo):
@@ -299,123 +331,103 @@
     return 2 * geo["slots"] * geo["maps"] * geo["area"] * geo["group"] * geo["fan"]
 
 
+def call(geo, body, name, args, in_specs, out_specs, out_shape, scratch_shapes, flops):
+    return pl.pallas_call(
+        functools.partial(body, geo),
+        grid=(geo["slots"],),
+        in_specs=in_specs,
+        out_specs=out_specs,
+        out_shape=out_shape,
+        scratch_shapes=scratch_shapes,
+        name=name,
+        compiler_params=params(),
+        cost_estimate=cost(flops),
+    )(*args)
+
+
 def first_kernel(geo, *refs):
     nw = 2 if geo["pairs"] else 1
-    wrefs, (rec_a, rec_d, h_out, s_out) = refs[:nw], refs[nw : nw + 4]
+    rec_a, rec_d, h_out, s_out = refs[nw : nw + 4]
     t_out, (w, x3, total) = refs[nw + 4 : -3], refs[-3:]
-    load_weights(geo, wrefs, w)
+    load_weights(geo, refs[:nw], w)
     hidden = []
     for n, value in enumerate(read_maps(geo, rec_a)):
         fill_patches(geo, x3, n, value)
         z = conv(geo, x3, n, w).astype(BF16).astype(F32)
         h, slope = act_both(z)
-        h = h.astype(BF16)
-        h_out[0, n] = h
+        hidden.append(h.astype(BF16))
+        h_out[0, n] = hidden[n]
         s_out[0, n] = slope.astype(BF16)
-        hidden.append(h)
     for n, h in enumerate(hidden):
         fill_patches(geo, x3, n, h)
     terms(geo, read_maps(geo, rec_d), x3, total)
     split_terms(geo, total, t_out)
 
 
-def first(geo, weights, recv):
+def first(geo, one, recv):
     specs, shapes = term_out(geo)
-    return pl.pallas_call(
-        functools.partial(first_kernel, geo),
-        grid=(geo["slots"],),
-        in_specs=weight_specs(geo) + [recv_spec(geo, 0), recv_spec(geo, 1)],
-        out_specs=[map_spec(geo)] * 2 + specs,
-        out_shape=[map_shape(geo)] * 2 + shapes,
-        scratch_shapes=scratch(geo, 1, 1, True),
-        name="first",
-        compiler_params=params(),
-        cost_estimate=cost(2 * conv_flops(geo), 6e6),
-    )(*weights, recv, recv)
-
-
-def lower_kernel(geo, *refs):
-    nw = 2 if geo["pairs"] else 1
-    wrefs, (rec_a, rec_d, s_in, l_out) = refs[:nw], refs[nw : nw + 4]
-    t_out, (w, x3, y3, total) = refs[nw + 4 : -4], refs[-4:]
-    load_weights(geo, wrefs, w)
-    lows = []
-    for n, value in enumerate(read_maps(geo, rec_d)):
-        fill_patches(geo, x3, n, value)
-        low = (adjoint(geo, x3, n, w) * s_in[0, n].astype(F32)).astype(BF16)
-        l_out[0, n] = low
-        lows.append(low)
-    for n, value in enumerate(read_maps(geo, rec_a)):
-        fill_patches(geo, y3, n, value)
-    terms(geo, lows, y3, total)
-    split_terms(geo, total, t_out)
-
-
-def lower(geo, weights, recv, slope):
-    specs, shapes = term_out(geo)
-    return pl.pallas_call(
-        functools.partial(lower_kernel, geo),
-        grid=(geo["slots"],),
-        in_specs=weight_specs(geo) + [recv_spec(geo, 0), recv_spec(geo, 1), map_spec(geo)],
-        out_specs=[map_spec(geo)] + specs,
-        out_shape=[map_shape(geo)] + shapes,
-        scratch_shapes=scratch(geo, 1, 2, True),
-        name="lower",
-        compiler_params=params(),
-        cost_estimate=cost(2 * conv_flops(geo), 6e6),
-    )(*weights, recv, recv, slope)
-
-
-def last_kernel(geo, *refs):
+    return call(
+        geo, first_kernel, "first", (*one, recv, recv),
+        weight_specs(geo) + [recv_spec(geo, 0), recv_spec(geo, 1)],
+        [map_spec(geo)] * 2 + specs, [map_shape(geo)] * 2 + shapes,
+        scratch(geo, 1, 1, True), FIRST)
+
+
+def second_kernel(geo, *refs):
     nw = 2 if geo["pairs"] else 1
     one, two = refs[:nw], refs[nw : 2 * nw]
-    h_in, l_in, out, w, x3 = refs[2 * nw :]
-    load_weights(geo, two, w)
+    rec_d, h_in, s_in, l_out, out, w1, w2, x3 = refs[2 * nw :]
+    load_weights(geo, two, w2)
     maps = []
     for n in range(geo["maps"]):
         fill_patches(geo, x3, n, h_in[0, n])
-        maps.append((ALPHA * conv(geo, x3, n, w)).astype(BF16))
+        maps.append((ALPHA * conv(geo, x3, n, w2)).astype(BF16))
     write_maps(geo, out, 0, maps)
-    load_weights(geo, one, w)
+    load_weights(geo, one, w1)
     maps = []
-    for n in range(geo["maps"]):
-        fill_patches(geo, x3, n, l_in[0, n])
-        maps.append(adjoint(geo, x3, n, w).astype(BF16))
+    for n, value in enumerate(read_maps(geo, rec_d)):
+        fill_patches(geo, x3, n, value)
+        low = (adjoint(geo, x3, n, w2) * s_in[0, n].astype(F32)).astype(BF16)
+        l_out[0, n] = low
+        fill_patches(geo, x3, n, low)
+        maps.append(adjoint(geo, x3, n, w1).astype(BF16))
     write_maps(geo, out, 1, maps)
 
 
-def last(geo, one, two, hidden, low):
-    return pl.pallas_call(
-        functools.partial(last_kernel, geo),
-        grid=(geo["slots"],),
-        in_specs=weight_specs(geo) * 2 + [map_spec(geo)] * 2,
-        out_specs=pl.BlockSpec(
-            (geo["peers"], 2, 1, geo["piece"], geo["group"]), lambda s: (0, 0, s, 0, 0)
-        ),
-        out_shape=jax.ShapeDtypeStruct(
-            (geo["peers"], 2, geo["slots"], geo["piece"], geo["group"]), BF16
-        ),
-        scratch_shapes=scratch(geo, 1, 1, False),
-        name="last",
-        compiler_params=params(),
-        cost_estimate=cost(2 * conv_flops(geo), 6e6),
-    )(*one, *two, hidden, low)
-
-
-def fold_kernel(keep, recv, mine, send):
-    a = lax.axis_index("da")
-    mine[...] = keep[a] + recv[a].astype(F32)
-    send[...] = (keep[1 - a] + recv[1 - a].astype(F32)).astype(BF16)
+def second(geo, one, two, recv, hidden, slope):
+    return call(
+        geo, second_kernel, "second", (*one, *two, recv, hidden, slope),
+        weight_specs(geo) * 2 + [recv_spec(geo, 1)] + [map_spec(geo)] * 2,
+        [map_spec(geo), send_spec(geo)], [map_shape(geo), send_shape(geo)],
+        scratch(geo, 2, 1, False), SECOND)
+
+
+def lower_kernel(geo, rec_a, l_in, *refs):
+    t_out, (x3, total) = refs[:-2], refs[-2:]
+    for n, value in enumerate(read_maps(geo, rec_a)):
+        fill_patches(geo, x3, n, value)
+    terms(geo, [l_in[0, n] for n in range(geo["maps"])], x3, total)
+    split_terms(geo, total, t_out)
+
+
+def lower(geo, recv, low):
+    specs, shapes = term_out(geo)
+    return call(
+        geo, lower_kernel, "lower", (recv, low),
+        [recv_spec(geo, 0), map_spec(geo)], specs, shapes, scratch(geo, 0, 1, True), LOWER)
+
+
+def fold_kernel(keep, recv, send):
+    send[...] = (keep[...] + recv[...].astype(F32)).astype(BF16)
 
 
 def fold(keep, recv):
-    shape = keep.shape[1:]
     return pl.pallas_call(
         fold_kernel,
-        out_shape=(jax.ShapeDtypeStruct(shape, F32), jax.ShapeDtypeStruct(shape, BF16)),
+        out_shape=jax.ShapeDtypeStruct(keep.shape, BF16),
         name="fold",
         compiler_params=params(),
-        cost_estimate=cost(1e6, 2e6),
+        cost_estimate=cost(SMALL),
     )(keep, recv)
 
 
@@ -423,22 +435,30 @@
     return lax.ppermute(value, axis, [(0, 1), (1, 0)])
 
 
-def gather_rows(geo, rows):
+def relay_kernel(rows, over, out):
+    out[0] = rows[...]
+    out[1] = over[...]
+
+
+def relay(rows, over):
+    return pl.pallas_call(
+        relay_kernel,
+        out_shape=jax.ShapeDtypeStruct((2,) + rows.shape, rows.dtype),
+        name="relay",
+        compiler_params=params(),
+        cost_estimate=cost(RELAY),
+    )(rows, over)
+
+
+def gather_rows(geo, one, two):
     if not geo["pairs"]:
-        return (lax.all_gather(rows, ("da", "de"), axis=0, tiled=True).reshape(
-            geo["slots"], geo["group"], geo["fan"]),)
-    both = jnp.stack([rows, swap(rows, "da")])
-    return (both, swap(both, "de"))
-
-
-def sum_rows(geo, parts, kern, gain):
-    if not geo["pairs"]:
-        flat = parts[0].reshape(geo["slots"] * geo["group"], geo["fan"])
-        total = lax.psum_scatter(flat, ("da", "de"), scatter_dimension=0, tiled=True)
-        return pull_rows(kern, gain, total, jnp.zeros_like(total))
-    keep, send = parts
-    mine, other = fold(keep, swap(send, "de"))
-    return pull_rows(kern, gain, mine, swap(other, "da"))
+        full = [lax.all_gather(w, ("da", "de"), axis=0, tiled=True) for w in (one, two)]
+        return [(w.reshape(geo["slots"], geo["group"], geo["fan"]),) for w in full]
+    over = swap(one, "da")
+    two, over = lax.optimization_barrier((two, over))
+    one = relay(one, over)
+    two = relay(two, swap(two, "da"))
+    return (one, swap(one, "de")), (two, swap(two, "de"))
 
 
 def local(group, features, cotangent, kernel_one, kernel_two, gain_one, gain_two):
@@ -456,18 +476,34 @@
     flat = (images * rows * cols, chans)
     f, c = features.reshape(flat), cotangent.reshape(flat)
     k1, k2 = kernel_one.reshape(-1, fan), kernel_two.reshape(-1, fan)
-    w1, w2 = std_rows(k1, k2, gain_one, gain_two)
-    one = gather_rows(geo, w1)
-    two = gather_rows(geo, w2)
-    peers = ("db", "row", "col")
-    recv = lax.all_to_all(pack(geo, f, c), peers, 0, 0, tiled=True)
-    hidden, slope, *terms_two = first(geo, one, recv)
-    low, *terms_one = lower(geo, two, recv, slope)
-    sent = last(geo, one, two, hidden, low)
-    back = lax.all_to_all(sent, peers, 0, 0, tiled=True)
+    w1, w2, pieces = prep(geo, k1, k2, gain_one, gain_two, f, c)
+
+    def exchange(x):
+        return lax.all_to_all(x, ("db", "row", "col"), 0, 0, tiled=True)
+
+    recv = exchange(pieces)
+    one, two = gather_rows(geo, w1, w2)
+    hidden, slope, *parts_two = first(geo, one, recv)
+    if geo["pairs"]:
+        keep2, far2, send2, away2 = parts_two
+        low, out = second(geo, one, two, recv, hidden, slope)
+        far2 = fold(far2, swap(away2, "de"))
+        out, far2 = lax.optimization_barrier((out, far2))
+        back = exchange(out)
+        keep1, far1, send1, away1 = lower(geo, recv, low)
+        far1 = fold(far1, swap(away1, "de"))
+        grad_two = pull_rows(k2, gain_two, (keep2, swap(send2, "de"), swap(far2, "da")), PULL)
+        grad_one = pull_rows(k1, gain_one, (keep1, swap(send1, "de"), swap(far1, "da")), SMALL)
+    else:
+        low, out = second(geo, one, two, recv, hidden, slope)
+        back = exchange(out)
+        parts_one = lower(geo, recv, low)
+        flat = jnp.stack([x[0].reshape(geo["slots"] * group, fan) for x in (parts_one, parts_two)])
+        sums = lax.psum_scatter(flat, ("da", "de"), scatter_dimension=1, tiled=True)
+        none = jnp.zeros(k1.shape, BF16)
+        grad_one = pull_rows(k1, gain_one, (sums[0], none, none), SMALL)
+        grad_two = pull_rows(k2, gain_two, (sums[1], none, none), SMALL)
     outputs, input_grad = merge(geo, f, c, back)
-    grad_one = sum_rows(geo, terms_one, k1, gain_one)
-    grad_two = sum_rows(geo, terms_two, k2, gain_two)
     return (
         outputs.reshape(features.shape),
         input_grad.reshape(features.shape),

time: 86.7 us -> 71.3 us (0.82)
  waiting for transfers between devices: 40.5 us -> 25.1 us
  local copies, waits for them, and re-layouts: 5.14 us -> 0.02 us
  starting transfers between devices: 21.1 us -> 26.1 us
    ppermute x8 -> x10, waiting for transfers between devices: 40.5 us -> 23.7 us  [swap(): return lax.ppermute(value, axis, [(0, 1), (1, 0)])]
    ppermute x8 -> x10, starting transfers between devices: 9.02 us -> 17.5 us  [swap(): return lax.ppermute(value, axis, [(0, 1), (1, 0)])]
    unnamed x34 -> x12, local copies, waits for them, and re-layouts: 5.14 us -> 0.02 us
    all_to_all x2, starting transfers between devices: 12.1 us -> 8.59 us  [exchange(): return lax.all_to_all(x, ('db', 'row', 'col'), 0, 0, tiled=True)]
    all_to_all x2, waiting for transfers between devices: 0.01 us -> 1.46 us  [exchange(): return lax.all_to_all(x, ('db', 'row', 'col'), 0, 0, tiled=True)]
    pallas_call x7 -> x8, Pallas kernels: 14.8 us -> 14.7 us  [the longest x3 11.6 us: call(): pl.pallas_call(functools.partial(body, geo), grid=(geo['slots'],), in_spe...]
  transfers between devices with their start and end apart: 10 -> 12, of which waited for: 8 -> 9; matrix products, arithmetic and copies ran while one was open for 0% -> 0% of each run, Pallas kernels for 7% -> 20%
where the time goes in v1:
time: 71.3 us; the launch traced here: 70.5 us
  starting transfers between devices  26.1 us (37%)
  waiting for transfers between devices  25.1 us (35%)
  Pallas kernels  18.5 us (26%)
    ppermute x10, waiting for transfers between devices, swap(): return lax.ppermute(value, axis, [(0, 1), (1, 0)])  23.7 us
    ppermute x10, starting transfers between devices, swap(): return lax.ppermute(value, axis, [(0, 1), (1, 0)])  17.5 us
    pallas_call x3, Pallas kernels, call(): pl.pallas_call(functools.partial(body, geo), grid=(geo['slots'],), in_spe...  11.6 us
    all_to_all x2, starting transfers between devices, exchange(): return lax.all_to_all(x, ('db', 'row', 'col'), 0, 0, tiled=True)  8.59 us
    pallas_call x1, Pallas kernels, prep(): pl.pallas_call(functools.partial(prep_kernel, geo), in_specs=[pl.BlockSpe...  2.97 us
    pallas_call x2, Pallas kernels, pull_rows(): pl.pallas_call(pull_kernel, out_shape=jax.ShapeDtypeStruct(k.shape, F32),...  2.1 us
    pallas_call x1, Pallas kernels, merge(): pl.pallas_call(functools.partial(merge_kernel, geo), out_shape=(shape, sh...  1.75 us
    all_to_all x2, waiting for transfers between devices, exchange(): return lax.all_to_all(x, ('db', 'row', 'col'), 0, 0, tiled=True)  1.46 us
  transfers between devices with their start and end apart: 12, of which 9 were waited for; matrix products, arithmetic and copies ran while one was open for 0% of the time, Pallas kernels for 20%

profile of v1, /device:TPU:0, one launch (start us, length us, event | category | flops | bytes accessed | tf_op | source)
XLA Modules:
  0.0 70.5 jit_solution(16789859842764089069)
XLA Ops:
  0.6 3.0 %prep.1 = (bf16[64,1152]{1,0:T(8,128)(2,1)S(1)}, bf16[64,1152]{1,0:T(8,128)(2,1)S(1)}, bf16[8,2,2,128,128]{4,3,2,1,0:T(8,128)(2,1)}) custom-call(f32[64,1152]{1,0:T(8,128)} %bitcast.14, f32[64,1152]{1,0:T(8,128)} %bitcast.12, f32[1,64]{1,0:T(1,128)} %g.2, f32[1,64]{1,0:T(1,128)} %g.3, bf16[128,2048]{1,0:T(8,128)(2,1)} %bitcast.8, bf16[128,2048]{1,0:T(8,128)(2,1)} %bitcast.10), custom_call_target="tpu_custom_call" | custom-call | flops 1 | bytes 1 | tf_op jit(solution)/shard_map/prep/pallas_call | solution.py:129
  3.6 4.1 %collective-permute-start = (bf16[64,1152]{1,0:T(8,128)(2,1)S(1)}, bf16[64,1152]{1,0:T(8,128)(2,1)S(1)}, u32[]{:S(2)}, u32[]{:S(2)}) collective-permute-start(bf16[64,1152]{1,0:T(8,128)(2,1)S(1)} %get-tuple-element.25.rows), channel_id=1, source_target_pairs={{0,16},{16,0},{1,17},{17,1},{2,18},{18,2},{3,19},{19,3},{4,20},{20... | collective-permute-start | bytes 442376 | tf_op jit(solution)/shard_map/ppermute | solution.py:435
  7.7 3.8 %all-to-all-start = ((bf16[8,2,2,128,128]{4,3,2,1,0:T(8,128)(2,1)}), bf16[8,2,2,128,128]{4,3,2,1,0:T(8,128)(2,1)S(1)}, u32[]{:S(2)}, u32[]{:S(2)}) async-start(bf16[8,2,2,128,128]{4,3,2,1,0:T(8,128)(2,1)} %get-tuple-element.29), calls=%async_computation | async-start | bytes 2097152 | tf_op jit(solution)/shard_map/all_to_all | solution.py:482
  11.5 3.2 %collective-permute-done.over = bf16[64,1152]{1,0:T(8,128)(2,1)S(1)} collective-permute-done((bf16[64,1152]{1,0:T(8,128)(2,1)S(1)}, bf16[64,1152]{1,0:T(8,128)(2,1)S(1)}, u32[]{:S(2)}, u32[]{:S(2)}) %collective-permute-start) | collective-permute-done | bytes 147488 | tf_op jit(solution)/shard_map/ppermute | solution.py:435
  14.8 1.6 %collective-permute-start.1 = (bf16[2,64,1152]{2,1,0:T(8,128)(2,1)S(1)}, bf16[2,64,1152]{2,1,0:T(8,128)(2,1)S(1)}, u32[]{:S(2)}, u32[]{:S(2)}) collective-permute-start(bf16[2,64,1152]{2,1,0:T(8,128)(2,1)S(1)} %relay.2.refs_0_), channel_id=1, source_target_pairs={{0,4},{4,0},{1,5},{5,1},{2,6},{6,2},{3,7},{7,3},{8,12},{12,8},{9,1... | collective-permute-start | bytes 884744 | tf_op jit(solution)/shard_map/ppermute | solution.py:435
  16.4 10.7 %collective-permute-done.2.over = bf16[64,1152]{1,0:T(8,128)(2,1)S(1)} collective-permute-done((bf16[64,1152]{1,0:T(8,128)(2,1)S(1)}, bf16[64,1152]{1,0:T(8,128)(2,1)S(1)}, u32[]{:S(2)}, u32[]{:S(2)}) %collective-permute-start.2) | collective-permute-done | bytes 147488 | tf_op jit(solution)/shard_map/ppermute | solution.py:435
  27.1 1.6 %collective-permute-start.3 = (bf16[2,64,1152]{2,1,0:T(8,128)(2,1)S(1)}, bf16[2,64,1152]{2,1,0:T(8,128)(2,1)S(1)}, u32[]{:S(2)}, u32[]{:S(2)}) collective-permute-start(bf16[2,64,1152]{2,1,0:T(8,128)(2,1)S(1)} %relay.3.refs_2_), channel_id=1, source_target_pairs={{0,4},{4,0},{1,5},{5,1},{2,6},{6,2},{3,7},{7,3},{8,12},{12,8},{9,1... | collective-permute-start | bytes 884744 | tf_op jit(solution)/shard_map/ppermute | solution.py:435
  29.1 3.7 %first.1 = (bf16[2,2,512,128]{3,2,1,0:T(8,128)(2,1)S(1)}, bf16[2,2,512,128]{3,2,1,0:T(8,128)(2,1)S(1)}, f32[64,1152]{1,0:T(8,128)S(1)}, f32[64,1152]{1,0:T(8,128...) custom-call(bf16[2,64,1152]{2,1,0:T(8,128)(2,1)S(1)} %relay.2.refs_0_, ...), custom_call_target="tpu_custom_call" | custom-call | flops 3000000000 | bytes 1 | tf_op jit(solution)/shard_map/first/pallas_call | solution.py:335
  32.9 1.6 %collective-permute-start.4 = (bf16[64,1152]{1,0:T(8,128)(2,1)S(1)}, bf16[64,1152]{1,0:T(8,128)(2,1)S(1)}, u32[]{:S(2)}, u32[]{:S(2)}) collective-permute-start(bf16[64,1152]{1,0:T(8,128)(2,1)S(1)} %get-tuple-element.34), channel_id=1, source_target_pairs={{0,4},{4,0},{1,5},{5,1},{2,6},{6,2},{3,7},{7,3},{8,12},{12,8},{9,1... | collective-permute-start | bytes 442376 | tf_op jit(solution)/shard_map/ppermute | solution.py:435
  34.5 2.3 %collective-permute-done.3.refs_3_ = bf16[2,64,1152]{2,1,0:T(8,128)(2,1)S(1)} collective-permute-done((bf16[2,64,1152]{2,1,0:T(8,128)(2,1)S(1)}, bf16[2,64,1152]{2,1,0:T(8,128)(2,1)S(1)}, u32[]{:S(2)}, u32[]{:S(2)}) %collective-permute-start.3) | collective-permute-done | bytes 294944 | tf_op jit(solution)/shard_map/ppermute | solution.py:435
  36.7 6.4 %second.1 = (bf16[2,2,512,128]{3,2,1,0:T(8,128)(2,1)S(1)}, bf16[8,2,2,128,128]{4,3,2,1,0:T(8,128)(2,1)}) custom-call(bf16[2,64,1152]{2,1,0:T(8,128)(2,1)S(1)} %relay.2.refs_0_, bf16[2,64,1152]{2,1,0:T(8,128)(2,1)S(1)} %collective-permute-done.1.refs_1_, bf16[2,64,1152]{2,1,0:T(8,128)(2,1)S(1)} %relay.3.refs_2_, ...), custom_call_target="tpu_custom_call" | custom-call | flops 20000000000 | bytes 1 | tf_op jit(solution)/shard_map/second/pallas_call | solution.py:335
  43.1 4.8 %all-to-all-start.1 = ((bf16[8,2,2,128,128]{4,3,2,1,0:T(8,128)(2,1)}), bf16[8,2,2,128,128]{4,3,2,1,0:T(8,128)(2,1)S(1)}, u32[]{:S(2)}, u32[]{:S(2)}) async-start(bf16[8,2,2,128,128]{4,3,2,1,0:T(8,128)(2,1)} %get-tuple-element.35), calls=%async_computation.1 | async-start | bytes 2097152 | tf_op jit(solution)/shard_map/all_to_all | solution.py:482
  47.9 1.5 %lower.1 = (f32[64,1152]{1,0:T(8,128)S(1)}, f32[64,1152]{1,0:T(8,128)S(1)}, bf16[64,1152]{1,0:T(8,128)(2,1)S(1)}, bf16[64,1152]{1,0:T(8,128)(2,1)S(1)}) custom-call(bf16[8,2,2,128,128]{4,3,2,1,0:T(8,128)(2,1)S(1)} %all-to-all-done.refs_2_.refs_3_.refs_4_.rec_a, bf16[2,2,512,128]{3,2,1,0:T(8,128)(2,1)S(1)} %get-tuple-element.38.l_in), custom_call_target="tpu_custom_call" | custom-call | flops 20000000000 | bytes 1 | tf_op jit(solution)/shard_map/lower/pallas_call | solution.py:335
  49.4 1.7 %collective-permute-start.6 = (bf16[64,1152]{1,0:T(8,128)(2,1)S(1)}, bf16[64,1152]{1,0:T(8,128)(2,1)S(1)}, u32[]{:S(2)}, u32[]{:S(2)}) collective-permute-start(bf16[64,1152]{1,0:T(8,128)(2,1)S(1)} %get-tuple-element.42), channel_id=1, source_target_pairs={{0,4},{4,0},{1,5},{5,1},{2,6},{6,2},{3,7},{7,3},{8,12},{12,8},{9,1... | collective-permute-start | bytes 442376 | tf_op jit(solution)/shard_map/ppermute | solution.py:435
  51.5 1.6 %collective-permute-start.5 = (bf16[64,1152]{1,0:T(8,128)(2,1)S(1)}, bf16[64,1152]{1,0:T(8,128)(2,1)S(1)}, u32[]{:S(2)}, u32[]{:S(2)}) collective-permute-start(bf16[64,1152]{1,0:T(8,128)(2,1)S(1)} %get-tuple-element.40), channel_id=1, source_target_pairs={{0,4},{4,0},{1,5},{5,1},{2,6},{6,2},{3,7},{7,3},{8,12},{12,8},{9,1... | collective-permute-start | bytes 442376 | tf_op jit(solution)/shard_map/ppermute | solution.py:435
  53.2 2.3 %collective-permute-start.9 = (bf16[64,1152]{1,0:T(8,128)(2,1)S(1)}, bf16[64,1152]{1,0:T(8,128)(2,1)S(1)}, u32[]{:S(2)}, u32[]{:S(2)}) collective-permute-start(bf16[64,1152]{1,0:T(8,128)(2,1)S(1)} %fold.2), channel_id=1, source_target_pairs={{0,16},{16,0},{1,17},{17,1},{2,18},{18,2},{3,19},{19,3},{4,20},{20... | collective-permute-start | bytes 442376 | tf_op jit(solution)/shard_map/ppermute | solution.py:435
  55.5 0.6 collective-permute-done.6.recv
  56.2 2.6 %collective-permute-start.7 = (bf16[64,1152]{1,0:T(8,128)(2,1)S(1)}, bf16[64,1152]{1,0:T(8,128)(2,1)S(1)}, u32[]{:S(2)}, u32[]{:S(2)}) collective-permute-start(bf16[64,1152]{1,0:T(8,128)(2,1)S(1)} %fold.3), channel_id=1, source_target_pairs={{0,16},{16,0},{1,17},{17,1},{2,18},{18,2},{3,19},{19,3},{4,20},{20... | collective-permute-start | bytes 442376 | tf_op jit(solution)/shard_map/ppermute | solution.py:435
  59.3 4.4 %collective-permute-done.9.over = bf16[64,1152]{1,0:T(8,128)(2,1)S(1)} collective-permute-done((bf16[64,1152]{1,0:T(8,128)(2,1)S(1)}, bf16[64,1152]{1,0:T(8,128)(2,1)S(1)}, u32[]{:S(2)}, u32[]{:S(2)}) %collective-permute-start.9) | collective-permute-done | bytes 147488 | tf_op jit(solution)/shard_map/ppermute | solution.py:435
  63.7 1.1 %pull_rows.3 = f32[64,1152]{1,0:T(8,128)} custom-call(f32[64,1152]{1,0:T(8,128)S(1)} %bitcast.13, f32[1,64]{1,0:T(1,128)S(1)} %copy-done.4, f32[64,1152]{1,0:T(8,128)S(1)} %get-tuple-element.43.keep, bf16[64,1152]{1,0:T(8,128)(2,1)S(1)} %collective-permute-done.8.near, bf16[64,1152]{1,0:T(8,128)(2,1)S(1)} %collective-permute-done.9.over), custom_call_target="tpu_custom_call" | custom-call | flops 1 | bytes 1 | tf_op jit(solution)/shard_map/pull_rows/pallas_call | solution.py:89
  64.8 1.9 %collective-permute-done.7.over = bf16[64,1152]{1,0:T(8,128)(2,1)S(1)} collective-permute-done((bf16[64,1152]{1,0:T(8,128)(2,1)S(1)}, bf16[64,1152]{1,0:T(8,128)(2,1)S(1)}, u32[]{:S(2)}, u32[]{:S(2)}) %collective-permute-start.7) | collective-permute-done | bytes 147488 | tf_op jit(solution)/shard_map/ppermute | solution.py:435
  66.7 1.1 %pull_rows.2 = f32[64,1152]{1,0:T(8,128)} custom-call(f32[64,1152]{1,0:T(8,128)S(1)} %bitcast.15, f32[1,64]{1,0:T(1,128)S(1)} %copy-done.5, f32[64,1152]{1,0:T(8,128)S(1)} %get-tuple-element.39.keep, bf16[64,1152]{1,0:T(8,128)(2,1)S(1)} %collective-permute-done.5.near, bf16[64,1152]{1,0:T(8,128)(2,1)S(1)} %collective-permute-done.7.over), custom_call_target="tpu_custom_call" | custom-call | flops 1 | bytes 1 | tf_op jit(solution)/shard_map/pull_rows/pallas_call | solution.py:89
  67.7 1.0 %all-to-all-done.1.recv = bf16[8,2,2,128,128]{4,3,2,1,0:T(8,128)(2,1)S(1)} async-done(((bf16[8,2,2,128,128]{4,3,2,1,0:T(8,128)(2,1)}), bf16[8,2,2,128,128]{4,3,2,1,0:T(8,128)(2,1)S(1)}, u32[]{:S(2)}, u32[]{:S(2)}) %all-to-all-start.1) | async-done | bytes 1048608 | tf_op jit(solution)/shard_map/all_to_all | solution.py:482
  68.7 1.8 %merge.1 = (bf16[128,2048]{1,0:T(8,128)(2,1)}, bf16[128,2048]{1,0:T(8,128)(2,1)}) custom-call(bf16[128,2048]{1,0:T(8,128)(2,1)S(1)} %bitcast.9, bf16[128,2048]{1,0:T(8,128)(2,1)S(1)} %bitcast.11, bf16[8,2,2,128,128]{4,3,2,1,0:T(8,128)(2,1)S(1)} %all-to-all-done.1.recv), custom_call_target="tpu_custom_call" | custom-call | flops 1 | bytes 1 | tf_op jit(solution)/shard_map/merge/pallas_call | solution.py:157
  (23 shorter events, 1.5 us)
Async XLA Ops:
  3.6 11.1 %collective-permute-start = (bf16[64,1152]{1,0:T(8,128)(2,1)S(1)}, bf16[64,1152]{1,0:T(8,128)(2,1)S(1)}, u32[]{:S(2)}, u32[]{:S(2)}) collective-permute-start(bf16[64,1152]{1,0:T(8,128)(2,1)S(1)} %get-tuple-element.25.rows), channel_id=1, source_target_pairs={{0,16},{16,0},{1,17},{17,1},{2,18},{18,2},{3,19},{19,3},{4,20},{20... | collective-permute-start | bytes 442376 | tf_op jit(solution)/shard_map/ppermute | solution.py:435
  7.7 21.4 %all-to-all-start = ((bf16[8,2,2,128,128]{4,3,2,1,0:T(8,128)(2,1)}), bf16[8,2,2,128,128]{4,3,2,1,0:T(8,128)(2,1)S(1)}, u32[]{:S(2)}, u32[]{:S(2)}) async-start(bf16[8,2,2,128,128]{4,3,2,1,0:T(8,128)(2,1)} %get-tuple-element.29), calls=%async_computation | async-start | bytes 2097152 | tf_op jit(solution)/shard_map/all_to_all | solution.py:482
  14.7 12.3 %collective-permute-start.2 = (bf16[64,1152]{1,0:T(8,128)(2,1)S(1)}, bf16[64,1152]{1,0:T(8,128)(2,1)S(1)}, u32[]{:S(2)}, u32[]{:S(2)}) collective-permute-start(bf16[64,1152]{1,0:T(8,128)(2,1)S(1)} %get-tuple-element.28.rows), channel_id=1, source_target_pairs={{0,16},{16,0},{1,17},{17,1},{2,18},{18,2},{3,19},{19,3},{4,20},{20... | collective-permute-start | bytes 442376 | tf_op jit(solution)/shard_map/ppermute | solution.py:435
  14.8 13.9 %collective-permute-start.1 = (bf16[2,64,1152]{2,1,0:T(8,128)(2,1)S(1)}, bf16[2,64,1152]{2,1,0:T(8,128)(2,1)S(1)}, u32[]{:S(2)}, u32[]{:S(2)}) collective-permute-start(bf16[2,64,1152]{2,1,0:T(8,128)(2,1)S(1)} %relay.2.refs_0_), channel_id=1, source_target_pairs={{0,4},{4,0},{1,5},{5,1},{2,6},{6,2},{3,7},{7,3},{8,12},{12,8},{9,1... | collective-permute-start | bytes 884744 | tf_op jit(solution)/shard_map/ppermute | solution.py:435
  27.1 9.7 %collective-permute-start.3 = (bf16[2,64,1152]{2,1,0:T(8,128)(2,1)S(1)}, bf16[2,64,1152]{2,1,0:T(8,128)(2,1)S(1)}, u32[]{:S(2)}, u32[]{:S(2)}) collective-permute-start(bf16[2,64,1152]{2,1,0:T(8,128)(2,1)S(1)} %relay.3.refs_2_), channel_id=1, source_target_pairs={{0,4},{4,0},{1,5},{5,1},{2,6},{6,2},{3,7},{7,3},{8,12},{12,8},{9,1... | collective-permute-start | bytes 884744 | tf_op jit(solution)/shard_map/ppermute | solution.py:435
  32.9 10.2 %collective-permute-start.4 = (bf16[64,1152]{1,0:T(8,128)(2,1)S(1)}, bf16[64,1152]{1,0:T(8,128)(2,1)S(1)}, u32[]{:S(2)}, u32[]{:S(2)}) collective-permute-start(bf16[64,1152]{1,0:T(8,128)(2,1)S(1)} %get-tuple-element.34), channel_id=1, source_target_pairs={{0,4},{4,0},{1,5},{5,1},{2,6},{6,2},{3,7},{7,3},{8,12},{12,8},{9,1... | collective-permute-start | bytes 442376 | tf_op jit(solution)/shard_map/ppermute | solution.py:435
  43.1 25.6 %all-to-all-start.1 = ((bf16[8,2,2,128,128]{4,3,2,1,0:T(8,128)(2,1)}), bf16[8,2,2,128,128]{4,3,2,1,0:T(8,128)(2,1)S(1)}, u32[]{:S(2)}, u32[]{:S(2)}) async-start(bf16[8,2,2,128,128]{4,3,2,1,0:T(8,128)(2,1)} %get-tuple-element.35), calls=%async_computation.1 | async-start | bytes 2097152 | tf_op jit(solution)/shard_map/all_to_all | solution.py:482
  49.4 6.7 %collective-permute-start.6 = (bf16[64,1152]{1,0:T(8,128)(2,1)S(1)}, bf16[64,1152]{1,0:T(8,128)(2,1)S(1)}, u32[]{:S(2)}, u32[]{:S(2)}) collective-permute-start(bf16[64,1152]{1,0:T(8,128)(2,1)S(1)} %get-tuple-element.42), channel_id=1, source_target_pairs={{0,4},{4,0},{1,5},{5,1},{2,6},{6,2},{3,7},{7,3},{8,12},{12,8},{9,1... | collective-permute-start | bytes 442376 | tf_op jit(solution)/shard_map/ppermute | solution.py:435
  51.1 8.2 %collective-permute-start.8 = (bf16[64,1152]{1,0:T(8,128)(2,1)S(1)}, bf16[64,1152]{1,0:T(8,128)(2,1)S(1)}, u32[]{:S(2)}, u32[]{:S(2)}) collective-permute-start(bf16[64,1152]{1,0:T(8,128)(2,1)S(1)} %get-tuple-element.44), channel_id=1, source_target_pairs={{0,4},{4,0},{1,5},{5,1},{2,6},{6,2},{3,7},{7,3},{8,12},{12,8},{9,1... | collective-permute-start | bytes 442376 | tf_op jit(solution)/shard_map/ppermute | solution.py:435
  51.5 13.2 %collective-permute-start.5 = (bf16[64,1152]{1,0:T(8,128)(2,1)S(1)}, bf16[64,1152]{1,0:T(8,128)(2,1)S(1)}, u32[]{:S(2)}, u32[]{:S(2)}) collective-permute-start(bf16[64,1152]{1,0:T(8,128)(2,1)S(1)} %get-tuple-element.40), channel_id=1, source_target_pairs={{0,4},{4,0},{1,5},{5,1},{2,6},{6,2},{3,7},{7,3},{8,12},{12,8},{9,1... | collective-permute-start | bytes 442376 | tf_op jit(solution)/shard_map/ppermute | solution.py:435
  53.2 10.5 %collective-permute-start.9 = (bf16[64,1152]{1,0:T(8,128)(2,1)S(1)}, bf16[64,1152]{1,0:T(8,128)(2,1)S(1)}, u32[]{:S(2)}, u32[]{:S(2)}) collective-permute-start(bf16[64,1152]{1,0:T(8,128)(2,1)S(1)} %fold.2), channel_id=1, source_target_pairs={{0,16},{16,0},{1,17},{17,1},{2,18},{18,2},{3,19},{19,3},{4,20},{20... | collective-permute-start | bytes 442376 | tf_op jit(solution)/shard_map/ppermute | solution.py:435
  56.1 7.6 %copy-start.2 = (f32[1,64,1152]{2,1,0:T(8,128)S(1)}, f32[1,64,1152]{2,1,0:T(8,128)}, u32[]{:S(2)}) copy-start(f32[1,64,1152]{2,1,0:T(8,128)} %param.9) | copy-start | bytes 884740
  56.2 7.5 %copy-start.4 = (f32[1,64]{1,0:T(1,128)S(1)}, f32[1,64]{1,0:T(1,128)}, u32[]{:S(2)}) copy-start(f32[1,64]{1,0:T(1,128)} %g.3) | copy-start | bytes 772
  56.2 10.5 %collective-permute-start.7 = (bf16[64,1152]{1,0:T(8,128)(2,1)S(1)}, bf16[64,1152]{1,0:T(8,128)(2,1)S(1)}, u32[]{:S(2)}, u32[]{:S(2)}) collective-permute-start(bf16[64,1152]{1,0:T(8,128)(2,1)S(1)} %fold.3), channel_id=1, source_target_pairs={{0,16},{16,0},{1,17},{17,1},{2,18},{18,2},{3,19},{19,3},{4,20},{20... | collective-permute-start | bytes 442376 | tf_op jit(solution)/shard_map/ppermute | solution.py:435
  63.7 3.0 %copy-start.3 = (f32[1,64,1152]{2,1,0:T(8,128)S(1)}, f32[1,64,1152]{2,1,0:T(8,128)}, u32[]{:S(2)}) copy-start(f32[1,64,1152]{2,1,0:T(8,128)} %param.8) | copy-start | bytes 884740
  64.7 1.9 %copy-start.5 = (f32[1,64]{1,0:T(1,128)S(1)}, f32[1,64]{1,0:T(1,128)}, u32[]{:S(2)}) copy-start(f32[1,64]{1,0:T(1,128)} %g.2) | copy-start | bytes 772
  66.7 2.0 %copy-start = (bf16[1,4,32,2048]{3,2,1,0:T(8,128)(2,1)S(1)}, bf16[1,4,32,2048]{3,2,1,0:T(8,128)(2,1)}, u32[]{:S(2)}) copy-start(bf16[1,4,32,2048]{3,2,1,0:T(8,128)(2,1)} %param.6) | copy-start | bytes 1572868
  66.7 2.0 %copy-start.1 = (bf16[1,4,32,2048]{3,2,1,0:T(8,128)(2,1)S(1)}, bf16[1,4,32,2048]{3,2,1,0:T(8,128)(2,1)}, u32[]{:S(2)}) copy-start(bf16[1,4,32,2048]{3,2,1,0:T(8,128)(2,1)} %param.7) | copy-start | bytes 1572868

commit v2 on v1

v2 whole, which is shorter than its diff:
```python
import functools
import math

import jax
import jax.numpy as jnp
from jax import lax
from jax.experimental import pallas as pl
from jax.experimental.pallas import tpu as pltpu
from jax.sharding import Mesh, PartitionSpec as P

GAMMA = 1.7015043497085571
ALPHA = 0.2
EPS = 1e-06
ROOT = math.sqrt(2.0 / math.pi)
CUBE = 0.044715
F32 = jnp.float32
BF16 = jnp.bfloat16
VMEM_LIMIT = 24 * 1024 * 1024
SMALL = 1
RELAY = 20_000_000_000
FIRST = 3_000_000_000
LOWER = RELAY
SECOND = FOLD = RELAY
PULL = MERGE = SMALL
STRIP = 4


def act_value(x):
    t = jnp.tanh(ROOT * (x + CUBE * (x * x * x)))
    return (0.5 * GAMMA) * x * (1.0 + t)


def act_slope(x):
    sq = x * x
    t = jnp.tanh(ROOT * (x + CUBE * (sq * x)))
    return (0.5 * GAMMA) * ((1.0 + t) + x * (1.0 - t * t) * (ROOT + (3.0 * CUBE * ROOT) * sq))


def act_both(x):
    sq = x * x
    t = jnp.tanh(ROOT * (x + CUBE * (sq * x)))
    up = 1.0 + t
    value = (0.5 * GAMMA) * x * up
    slope = (0.5 * GAMMA) * (up + x * (1.0 - t * t) * (ROOT + (3.0 * CUBE * ROOT) * sq))
    return value, slope


def params(**kw):
    return pltpu.CompilerParams(vmem_limit_bytes=VMEM_LIMIT, **kw)


def pin(x):
    return pltpu.with_memory_space_constraint(x, pltpu.HBM)


def cost(flops):
    return pl.CostEstimate(flops=flops, bytes_accessed=1, transcendentals=0)


def column(gain_ref):
    rows = gain_ref.shape[1]
    first = lax.broadcasted_iota(jnp.int32, (rows, rows), 0)
    second = lax.broadcasted_iota(jnp.int32, (rows, rows), 1)
    spread = jnp.broadcast_to(gain_ref[...], (rows, rows))
    return jnp.sum(jnp.where(first == second, spread, 0.0), axis=1, keepdims=True)


def std_into(k, g, w):
    fan = k.shape[1]
    kern = k[...]
    cent = kern - jnp.mean(kern, axis=1, keepdims=True)
    var = jnp.mean(cent * cent, axis=1, keepdims=True)
    scale = column(g) * lax.rsqrt(var + EPS) * (1.0 / math.sqrt(fan))
    w[...] = (cent * scale).astype(BF16)


def pull_kernel(k, g, *refs):
    out = refs[-1]
    fan = k.shape[1]
    kern = k[...]
    grad = sum(ref[...].astype(F32) for ref in refs[:-1])
    cent = kern - jnp.mean(kern, axis=1, keepdims=True)
    var = jnp.mean(cent * cent, axis=1, keepdims=True)
    inv = lax.rsqrt(var + EPS)
    scale = column(g) * inv * (1.0 / math.sqrt(fan))
    dot = jnp.mean(grad * cent, axis=1, keepdims=True)
    term = scale * (grad - cent * (inv * inv * dot))
    out[...] = term - jnp.mean(term, axis=1, keepdims=True)


def pull_rows(k, g, sums, flops):
    return pl.pallas_call(
        pull_kernel,
        out_shape=jax.ShapeDtypeStruct(k.shape, F32),
        name="pull_rows",
        compiler_params=params(),
        cost_estimate=cost(flops),
    )(k, g, *sums)


def prep_kernel(geo, k1, k2, g1, g2, f, c, w1, w2, out, *scratch):
    k1_in, k2_in, g1_in, g2_in, f_in, c_in, stage, sems, sent = scratch
    group, blocks = geo["group"], geo["blocks"]
    span = geo["per_block"] * group

    def bring(src, dst):
        move = pltpu.make_async_copy(src, dst, sems.at[len(moves)])
        moves.append(move)
        move.start()
        return move

    moves, cells = [], []
    for n in range(blocks):
        cut = pl.ds(n * span, span)
        cells.append((bring(f.at[:, cut], f_in.at[:, cut]), bring(c.at[:, cut], c_in.at[:, cut])))
        if n == 0:
            rows = [bring(*pair) for pair in ((k1, k1_in), (g1, g1_in), (k2, k2_in), (g2, g2_in))]
    leaves = []
    for block in range(blocks):
        for move in cells[block]:
            move.wait()
        for b in range(geo["nb"]):
            dst = b * blocks + block
            for slot in range(geo["slots"]):
                at = (block * geo["per_block"] + slot * geo["nb"] + b) * group
                stage[dst, 0, slot] = act_value(f_in[:, at : at + group].astype(F32)).astype(BF16)
                stage[dst, 1, slot] = (ALPHA * c_in[:, at : at + group].astype(F32)).astype(BF16)
            leaves.append(pltpu.make_async_copy(stage.at[dst], out.at[dst], sent.at[dst]))
            leaves[-1].start()
        if block == 0:
            for move in rows[:2]:
                move.wait()
            std_into(k1_in, g1_in, w1)
            for move in rows[2:]:
                move.wait()
            std_into(k2_in, g2_in, w2)
    for move in leaves:
        move.wait()


def prep(geo, k1, k2, g1, g2, f, c):
    args = (k1, k2, g1, g2, f, c)
    dims = (geo["peers"], 2, geo["slots"], f.shape[0], geo["group"])
    vmem, hbm = (pl.BlockSpec(memory_space=m) for m in (pltpu.VMEM, pl.ANY))
    return pl.pallas_call(
        functools.partial(prep_kernel, geo),
        in_specs=[hbm] * 6,
        out_specs=[vmem, vmem, hbm],
        out_shape=[jax.ShapeDtypeStruct(k1.shape, BF16)] * 2 + [jax.ShapeDtypeStruct(dims, BF16)],
        scratch_shapes=[pltpu.VMEM(x.shape, x.dtype) for x in args] + [
            pltpu.VMEM(dims, BF16),
            pltpu.SemaphoreType.DMA((4 + 2 * geo["blocks"],)),
            pltpu.SemaphoreType.DMA((geo["peers"],))],
        name="prep",
        compiler_params=params(),
        cost_estimate=cost(SMALL),
    )(*[pin(x) for x in args])


def merge_kernel(geo, f, c, recv, out, grad, out_in, grad_in, sems):
    group, blocks = geo["group"], geo["blocks"]
    span = geo["per_block"] * group
    moves = []
    for block in range(blocks):
        for b in range(geo["nb"]):
            src = b * blocks + block
            for slot in range(geo["slots"]):
                at = (block * geo["per_block"] + slot * geo["nb"] + b) * group
                x = f[:, at : at + group].astype(F32)
                out_in[:, at : at + group] = (x + recv[src, 0, slot].astype(F32)).astype(BF16)
                grad_in[:, at : at + group] = (
                    c[:, at : at + group].astype(F32)
                    + act_slope(x) * recv[src, 1, slot].astype(F32)
                ).astype(BF16)
        cut = pl.ds(block * span, span)
        for n, (src, dst) in enumerate(((out_in, out), (grad_in, grad))):
            moves.append(pltpu.make_async_copy(
                src.at[:, cut], dst.at[:, cut], sems.at[n, block]))
            moves[-1].start()
    for move in moves:
        move.wait()


def merge(geo, f, c, recv):
    shape = jax.ShapeDtypeStruct(f.shape, BF16)
    return pl.pallas_call(
        functools.partial(merge_kernel, geo),
        out_specs=[pl.BlockSpec(memory_space=pl.ANY)] * 2,
        out_shape=(shape, shape),
        scratch_shapes=[pltpu.VMEM(f.shape, BF16)] * 2 + [
            pltpu.SemaphoreType.DMA((2, geo["blocks"]))],
        name="merge",
        compiler_params=params(),
        cost_estimate=cost(MERGE),
    )(f, c, recv)


def runs(geo, number, at, size):
    rows, cols, width = geo["rows"], geo["cols"], geo["width"]
    b, i = number // geo["images"], number % geo["images"]
    for cell in range(at, at + size, cols):
        line, c = cell // width, cell % width // cols
        r, y = line // rows, line % rows
        yield (b * geo["nr"] + r) * geo["nc"] + c, (i * rows + y) * cols


def read_strip(geo, recv, which, slot, number, at, size):
    cols = geo["cols"]
    return jnp.concatenate([
        recv[peer, which, slot, p : p + cols, :] for peer, p in runs(geo, number, at, size)], axis=0)


def write_strip(geo, out, number, at, value):
    cols = geo["cols"]
    for n, (peer, p) in enumerate(runs(geo, number, at, value.shape[0])):
        out[peer, p : p + cols, :] = value[n * cols : (n + 1) * cols, :]


def strips(geo):
    size = STRIP * geo["width"]
    return [(at, size) for at in range(0, geo["area"], size)]


def column_is(geo, shape, place):
    return lax.broadcasted_iota(jnp.int32, shape, 0) % geo["width"] == place


def clear_rim(geo, x2):
    width, group, area = geo["width"], geo["group"], geo["area"]
    zero = jnp.zeros((width, 2 * group), BF16)
    for n in range(geo["maps"]):
        x2[n, 0:width, :] = zero
        x2[n, width + area : 2 * width + area, :] = zero


def fill_strip(geo, x2, number, at, value):
    width, group, size = geo["width"], geo["group"], value.shape[0]
    right = pltpu.roll(value.astype(F32), size - 1, 0)
    right = jnp.where(column_is(geo, right.shape, width - 1), 0.0, right)
    rows = pl.ds(width + at, size)
    x2[number, rows, 0:group] = value.astype(BF16)
    x2[number, rows, group : 2 * group] = right.astype(BF16)


def around(geo, x2, number):
    width, area = geo["width"], geo["area"]
    return jnp.concatenate([x2[number, pl.ds(dy * width, area), :] for dy in range(3)], axis=1)


def join(geo, pair):
    group = geo["group"]
    left = pltpu.roll(pair[:, group:], 1, 0)
    return pair[:, :group] + jnp.where(column_is(geo, left.shape, 0), 0.0, left)


def forward_weights(geo, w, out):
    group = geo["group"]
    for dy in range(3):
        at = dy * 2 * group
        out[0:group, at : at + 2 * group] = w[:, (3 * dy + 1) * group : (3 * dy + 3) * group]
        out[group : 2 * group, at : at + group] = w[:, 3 * dy * group : (3 * dy + 1) * group]
        out[group : 2 * group, at + group : at + 2 * group] = jnp.zeros((group, group), BF16)


def adjoint_weights(geo, w, out):
    group = geo["group"]
    for row in range(3):
        dy, at = 2 - row, row * 2 * group
        out[at : at + group, :] = w[:, (3 * dy + 1) * group : (3 * dy + 3) * group]
        out[at + group : at + 2 * group, 0:group] = w[:, 3 * dy * group : (3 * dy + 1) * group]
        out[at + group : at + 2 * group, group : 2 * group] = jnp.zeros((group, group), BF16)


def conv(geo, x2, number, at, size, weights, turned):
    span, width = 2 * geo["group"], geo["width"]
    total = None
    for dy in range(3):
        rows = x2[number, pl.ds(at + dy * width, size), :]
        if turned:
            part = jnp.dot(
                rows, weights[dy * span : (dy + 1) * span, :], preferred_element_type=F32)
        else:
            part = lax.dot_general(
                rows, weights[:, dy * span : (dy + 1) * span], (((1,), (1,)), ((), ())),
                preferred_element_type=F32)
        total = part if total is None else total + part
    return join(geo, total)


def terms(geo, g2, x2, out):
    width, area, group = geo["width"], geo["area"], geo["group"]
    total = None
    for n in range(geo["maps"]):
        part = lax.dot_general(
            g2[n, pl.ds(width, area), :], around(geo, x2, n), (((0,), (0,)), ((), ())),
            preferred_element_type=F32)
        total = part if total is None else total + part
    for dy in range(3):
        at, to = dy * 2 * group, dy * 3 * group
        out[:, to + group : to + 3 * group] = total[0:group, at : at + 2 * group]
        out[:, to : to + group] = total[group : 2 * group, at : at + group]


def load_weights(geo, slot, refs, w):
    if not geo["pairs"]:
        w[...] = refs[0][slot]
        return
    e = lax.axis_index("de")
    half = w.shape[0] // 2
    mine = lax.axis_index("da") == slot

    def put(here, there):
        w[pl.ds(pl.multiple_of(e * half, half), half), :] = here[...]
        w[pl.ds(pl.multiple_of((1 - e) * half, half), half), :] = there[...]

    if len(refs) == 2:
        refs = [ref.at[n] for n in range(2) for ref in refs]
    pl.when(mine)(lambda: put(refs[0], refs[1]))
    pl.when(jnp.logical_not(mine))(lambda: put(refs[2], refs[3]))


def split_terms(geo, slot, total, refs):
    if not geo["pairs"]:
        refs[0][slot] = total[...]
        return
    keep_near, keep_far, send_near, send_far = refs
    e = lax.axis_index("de")
    half = keep_near.shape[0]
    mine = lax.axis_index("da") == slot

    def put(keep, send):
        keep[...] = total[pl.ds(pl.multiple_of(e * half, half), half), :]
        send[...] = total[pl.ds(pl.multiple_of((1 - e) * half, half), half), :].astype(BF16)

    pl.when(mine)(lambda: put(keep_near, send_near))
    pl.when(jnp.logical_not(mine))(lambda: put(keep_far, send_far))


def split_slots(geo, slot, total, refs):
    if not geo["pairs"]:
        refs[0][slot] = total[...]
        return
    keep, send = refs
    mine = lax.axis_index("da") == slot

    @pl.when(mine)
    def _():
        keep[...] = total[...]

    @pl.when(jnp.logical_not(mine))
    def _():
        send[...] = total[...].astype(BF16)


def term_out(geo):
    if not geo["pairs"]:
        return [jax.ShapeDtypeStruct((geo["slots"], geo["group"], geo["fan"]), F32)]
    shape = (geo["group"] // 2, geo["fan"])
    return [jax.ShapeDtypeStruct(shape, t) for t in (F32, F32, BF16, BF16)]


def slot_out(geo):
    if not geo["pairs"]:
        return term_out(geo)
    return [jax.ShapeDtypeStruct((geo["group"], geo["fan"]), t) for t in (F32, BF16)]


def map_shape(geo):
    return jax.ShapeDtypeStruct((geo["slots"], geo["maps"], geo["area"], geo["group"]), BF16)


def send_shape(geo):
    return jax.ShapeDtypeStruct(
        (geo["peers"], 2, geo["slots"], geo["piece"], geo["group"]), BF16)


def scratch(geo, pairs, total, *weights):
    fan, group, slots = geo["fan"], geo["group"], geo["slots"]
    rows = geo["area"] + 2 * geo["width"]
    shapes = [pltpu.VMEM((slots, geo["maps"], rows, 2 * group), BF16) for _ in range(pairs)]
    shapes += [pltpu.VMEM((slots,) + dims, BF16) for dims in weights]
    return shapes + ([pltpu.VMEM((slots, group, fan), F32)] if total else [])


def weight_shapes(geo):
    group = geo["group"]
    return (group, geo["fan"]), (2 * group, 6 * group), (6 * group, 2 * group)


def conv_flops(geo):
    return 2 * geo["slots"] * geo["maps"] * geo["area"] * geo["group"] * geo["fan"]


def call(geo, body, name, args, out_shape, scratch_shapes, flops):
    return pl.pallas_call(
        functools.partial(body, geo),
        out_shape=out_shape,
        scratch_shapes=scratch_shapes,
        name=name,
        compiler_params=params(),
        cost_estimate=cost(flops),
    )(*args)


def first_kernel(geo, *refs):
    nw = 2 if geo["pairs"] else 1
    recv, h_out, s_out = refs[nw : nw + 3]
    t_out, buffers = refs[nw + 3 : -6], refs[-6:]
    for slot in range(geo["slots"]):
        x2, y2, g2, w, fw, total = [ref.at[slot] for ref in buffers]
        for buffer in (x2, y2, g2):
            clear_rim(geo, buffer)
        load_weights(geo, slot, refs[:nw], w)
        forward_weights(geo, w, fw)
        for n in range(geo["maps"]):
            for at, size in strips(geo):
                fill_strip(geo, x2, n, at, read_strip(geo, recv, 0, slot, n, at, size))
                fill_strip(geo, g2, n, at, read_strip(geo, recv, 1, slot, n, at, size))
        for n in range(geo["maps"]):
            for at, size in strips(geo):
                z = conv(geo, x2, n, at, size, fw, False).astype(BF16).astype(F32)
                h, slope = act_both(z)
                h = h.astype(BF16)
                h_out[slot, n, at : at + size, :] = h
                s_out[slot, n, at : at + size, :] = slope.astype(BF16)
                fill_strip(geo, y2, n, at, h)
        terms(geo, g2, y2, total)
        split_slots(geo, slot, total, t_out)


def first(geo, one, recv):
    return call(
        geo, first_kernel, "first", (*one, recv),
        [map_shape(geo)] * 2 + slot_out(geo),
        scratch(geo, 3, True, *weight_shapes(geo)[:2]), FIRST)


def second_kernel(geo, nw, *refs):
    one, two = refs[: nw[0]], refs[nw[0] : sum(nw)]
    recv, h_in, s_in, l_out, out, *buffers, stage, sems = refs[sum(nw) :]
    moves = []

    def leave(which, slot):
        move = pltpu.make_async_copy(
            stage.at[which, slot], out.at[:, which, slot], sems.at[which, slot])
        move.start()
        moves.append(move)

    for slot in range(geo["slots"]):
        x2, y2, z2, w, fw2, aw2, aw1 = [ref.at[slot] for ref in buffers]
        for buffer in (x2, y2, z2):
            clear_rim(geo, buffer)
        load_weights(geo, slot, two, w)
        forward_weights(geo, w, fw2)
        adjoint_weights(geo, w, aw2)
        load_weights(geo, slot, one, w)
        adjoint_weights(geo, w, aw1)
        for n in range(geo["maps"]):
            for at, size in strips(geo):
                fill_strip(geo, x2, n, at, h_in[slot, n, at : at + size, :])
                fill_strip(geo, y2, n, at, read_strip(geo, recv, 1, slot, n, at, size))
        for n in range(geo["maps"]):
            for at, size in strips(geo):
                value = ALPHA * conv(geo, x2, n, at, size, fw2, False)
                write_strip(geo, stage.at[0, slot], n, at, value.astype(BF16))
        leave(0, slot)
        for n in range(geo["maps"]):
            for at, size in strips(geo):
                low = conv(geo, y2, n, at, size, aw2, True)
                low = (low * s_in[slot, n, at : at + size, :].astype(F32)).astype(BF16)
                l_out[slot, n, at : at + size, :] = low
                fill_strip(geo, z2, n, at, low)
        for n in range(geo["maps"]):
            for at, size in strips(geo):
                value = conv(geo, z2, n, at, size, aw1, True)
                write_strip(geo, stage.at[1, slot], n, at, value.astype(BF16))
        leave(1, slot)
    for move in moves:
        move.wait()


def second(geo, one, two, recv, hidden, slope):
    nw = (len(one), len(two))
    shapes = weight_shapes(geo)
    sent = send_shape(geo)
    args = (*one, *two, recv, hidden, slope)
    return pl.pallas_call(
        functools.partial(second_kernel, geo, nw),
        out_shape=[map_shape(geo), sent],
        out_specs=[
            pl.BlockSpec(memory_space=pltpu.VMEM), pl.BlockSpec(memory_space=pl.ANY)],
        scratch_shapes=scratch(geo, 3, False, *shapes, shapes[2]) + [
            pltpu.VMEM((2, geo["slots"], geo["peers"], geo["piece"], geo["group"]), BF16),
            pltpu.SemaphoreType.DMA((2, geo["slots"]))],
        name="second",
        compiler_params=params(),
        cost_estimate=cost(SECOND),
    )(*args)


def lower_kernel(geo, recv, l_in, *refs):
    t_out, buffers = refs[:-3], refs[-3:]
    for slot in range(geo["slots"]):
        x2, g2, total = [ref.at[slot] for ref in buffers]
        clear_rim(geo, x2)
        clear_rim(geo, g2)
        for n in range(geo["maps"]):
            for at, size in strips(geo):
                fill_strip(geo, x2, n, at, read_strip(geo, recv, 0, slot, n, at, size))
                fill_strip(geo, g2, n, at, l_in[slot, n, at : at + size, :])
        terms(geo, g2, x2, total)
        split_terms(geo, slot, total, t_out)


def lower(geo, recv, low):
    return call(
        geo, lower_kernel, "lower", (recv, low), term_out(geo), scratch(geo, 2, True), LOWER)


def fold_kernel(keep, recv, send):
    send[...] = (keep[...] + recv[...].astype(F32)).astype(BF16)


def fold(keep, recv):
    return pl.pallas_call(
        fold_kernel,
        out_shape=jax.ShapeDtypeStruct(keep.shape, BF16),
        name="fold",
        compiler_params=params(),
        cost_estimate=cost(FOLD),
    )(keep, recv)


def halve_kernel(keep, recv, mine, send):
    e = lax.axis_index("de")
    half = mine.shape[0]
    here = pl.ds(pl.multiple_of(e * half, half), half)
    there = pl.ds(pl.multiple_of((1 - e) * half, half), half)
    mine[...] = keep[here, :] + recv[here, :].astype(F32)
    send[...] = (keep[there, :] + recv[there, :].astype(F32)).astype(BF16)


def halve(keep, recv):
    shape = (keep.shape[0] // 2, keep.shape[1])
    return pl.pallas_call(
        halve_kernel,
        out_shape=[jax.ShapeDtypeStruct(shape, F32), jax.ShapeDtypeStruct(shape, BF16)],
        name="halve",
        compiler_params=params(),
        cost_estimate=cost(FOLD),
    )(keep, recv)


def swap(value, axis):
    return lax.ppermute(value, axis, [(0, 1), (1, 0)])


def relay_kernel(rows, over, out):
    out[0] = rows[...]
    out[1] = over[...]


def relay(rows, over):
    return pl.pallas_call(
        relay_kernel,
        out_shape=jax.ShapeDtypeStruct((2,) + rows.shape, rows.dtype),
        name="relay",
        compiler_params=params(),
        cost_estimate=cost(RELAY),
    )(rows, over)


def gather_rows(geo, one, two):
    if not geo["pairs"]:
        full = [lax.all_gather(w, ("da", "de"), axis=0, tiled=True) for w in (one, two)]
        return [(w.reshape(geo["slots"], geo["group"], geo["fan"]),) for w in full]
    over = swap(one, "da")
    two, over = lax.optimization_barrier((two, over))
    one = relay(one, over)
    near, over = swap(two, "de"), swap(two, "da")
    return (one, swap(one, "de")), (two, near, over, swap(over, "de"))


def local(group, features, cotangent, kernel_one, kernel_two, gain_one, gain_two):
    images, rows, cols, chans = features.shape
    fan = kernel_one.shape[2]
    nr, nc = lax.axis_size("row"), lax.axis_size("col")
    na, nb, ne = lax.axis_size("da"), lax.axis_size("db"), lax.axis_size("de")
    blocks = nr * nc
    geo = dict(
        group=group, fan=fan, nr=nr, nc=nc, nb=nb, blocks=blocks, slots=na,
        per_block=chans // blocks // group, peers=nb * blocks, images=images,
        rows=rows, cols=cols, piece=images * rows * cols, width=nc * cols,
        area=nr * rows * nc * cols, maps=nb * images, pairs=na == 2 and ne == 2,
    )
    flat = (images * rows * cols, chans)
    f, c = features.reshape(flat), cotangent.reshape(flat)
    k1, k2 = kernel_one.reshape(-1, fan), kernel_two.reshape(-1, fan)
    w1, w2, pieces = prep(geo, k1, k2, gain_one, gain_two, f, c)

    def exchange(x):
        return lax.all_to_all(x, ("db", "row", "col"), 0, 0, tiled=True)

    recv = exchange(pieces)
    one, two = gather_rows(geo, w1, w2)
    hidden, slope, *parts_two = first(geo, one, recv)
    low, out = second(geo, one, two, recv, hidden, slope)
    parts_one = lower(geo, recv, low)
    if geo["pairs"]:
        keep2, send2 = parts_two
        mine2, half2 = halve(keep2, swap(send2, "da"))
        keep1, far1, send1, away1 = parts_one
        back = exchange(out)
        away1, half2 = lax.optimization_barrier((swap(away1, "de"), half2))
        far1, send1 = lax.optimization_barrier((fold(far1, away1), send1))
        grad_two = pull_rows(k2, gain_two, (mine2, swap(half2, "de")), PULL)
        grad_one = pull_rows(k1, gain_one, (keep1, swap(send1, "de"), swap(far1, "da")), PULL)
    else:
        back = exchange(out)
        flat = jnp.stack([x[0].reshape(geo["slots"] * group, fan) for x in (parts_one, parts_two)])
        sums = lax.psum_scatter(flat, ("da", "de"), scatter_dimension=1, tiled=True)
        grad_one = pull_rows(k1, gain_one, (sums[0],), SMALL)
        grad_two = pull_rows(k2, gain_two, (sums[1],), SMALL)
    outputs, input_grad = merge(geo, f, c, back)
    return (
        outputs.reshape(features.shape),
        input_grad.reshape(features.shape),
        grad_one.reshape(kernel_one.shape),
        grad_two.reshape(kernel_two.shape),
    )


def solution(mesh):
    names = ("da", "db", "de", "row", "col")
    nr, nc, dp = mesh.shape["row"], mesh.shape["col"], mesh.shape["dp"]

    def run(features, cotangent, kernel_one, kernel_two, gain_one, gain_two):
        group = kernel_one.shape[2] // 9
        per_block = kernel_one.shape[1] // group
        na = 2 if per_block % 2 == 0 else 1
        nb = per_block // na
        fine = Mesh(mesh.devices.reshape(na, nb, dp // per_block, nr, nc), names)
        dps = ("da", "db", "de")
        cells = P(dps, "row", "col", None)
        rows = P(("row", "col"), dps, None)
        gains = P(("row", "col"), dps)
        return jax.shard_map(
            functools.partial(local, group),
            mesh=fine,
            in_specs=(cells, cells, rows, rows, gains, gains),
            out_specs=(cells, cells, rows, rows),
            check_vma=False,
        )(features, cotangent, kernel_one, kernel_two, gain_one, gain_two)

    return run
```

time: 71.3 us -> 65.1 us (0.913)
  starting transfers between devices: 26.1 us -> 21.5 us
  Pallas kernels: 18.5 us -> 15.4 us
  waiting for transfers between devices: 25.1 us -> 27.2 us
    ppermute x10, starting transfers between devices: 17.5 us -> 13.3 us  [swap(): return lax.ppermute(value, axis, [(0, 1), (1, 0)])]
    pallas_call x5 -> x6, Pallas kernels: 16.3 us -> 13.3 us  [the longest x2 4.99 us: call(): pl.pallas_call(functools.partial(body, geo), out_shape=out_shape, scratch...]
    ppermute x10, waiting for transfers between devices: 23.7 us -> 25.6 us  [swap(): return lax.ppermute(value, axis, [(0, 1), (1, 0)])]
  transfers between devices with their start and end apart: 12 -> 12, of which waited for: 9 -> 8; matrix products, arithmetic and copies ran while one was open for 0% -> 0% of each run, Pallas kernels for 20% -> 17%
where the time goes in v2:
time: 65.1 us; the launch traced here: 64.9 us
  waiting for transfers between devices  27.2 us (42%)
  starting transfers between devices  21.5 us (33%)
  Pallas kernels  15.4 us (24%)
  between operations  0.71 us (1%)
    ppermute x10, waiting for transfers between devices, swap(): return lax.ppermute(value, axis, [(0, 1), (1, 0)])  25.6 us
    ppermute x10, starting transfers between devices, swap(): return lax.ppermute(value, axis, [(0, 1), (1, 0)])  13.3 us
    all_to_all x2, starting transfers between devices, exchange(): return lax.all_to_all(x, ('db', 'row', 'col'), 0, 0, tiled=True)  8.14 us
    pallas_call x2, Pallas kernels, call(): pl.pallas_call(functools.partial(body, geo), out_shape=out_shape, scratch...  4.99 us
    pallas_call x1, Pallas kernels, second(): pl.pallas_call(functools.partial(second_kernel, geo, nw), out_shape=[map_...  3.91 us
    pallas_call x1, Pallas kernels, prep(): pl.pallas_call(functools.partial(prep_kernel, geo), in_specs=[hbm] * 6, o...  2.74 us
    pallas_call x2, Pallas kernels, pull_rows(): pl.pallas_call(pull_kernel, out_shape=jax.ShapeDtypeStruct(k.shape, F32),...  2.1 us
    all_to_all x2, waiting for transfers between devices, exchange(): return lax.all_to_all(x, ('db', 'row', 'col'), 0, 0, tiled=True)  1.59 us
  transfers between devices with their start and end apart: 12, of which 8 were waited for; matrix products, arithmetic and copies ran while one was open for 0% of the time, Pallas kernels for 17%

profile of v2, /device:TPU:0, one launch (start us, length us, event | category | flops | bytes accessed | tf_op | source)
XLA Modules:
  0.0 64.9 jit_solution(15690850853263055771)
XLA Ops:
  0.6 2.7 %prep.1 = (bf16[64,1152]{1,0:T(8,128)(2,1)S(1)}, bf16[64,1152]{1,0:T(8,128)(2,1)S(1)}, bf16[8,2,2,128,128]{4,3,2,1,0:T(8,128)(2,1)}) custom-call(f32[64,1152]{1,0:T(8,128)} %bitcast.14, f32[64,1152]{1,0:T(8,128)} %bitcast.12, f32[1,64]{1,0:T(1,128)} %g.2, f32[1,64]{1,0:T(1,128)} %g.3, bf16[128,2048]{1,0:T(8,128)(2,1)} %bitcast.8, bf16[128,2048]{1,0:T(8,128)(2,1)} %bitcast.10), custom_call_target="tpu_custom_call" | custom-call | flops 1 | bytes 1 | tf_op jit(solution)/shard_map/prep/pallas_call | solution.py:145
  3.4 4.1 %collective-permute-start = (bf16[64,1152]{1,0:T(8,128)(2,1)S(1)}, bf16[64,1152]{1,0:T(8,128)(2,1)S(1)}, u32[]{:S(2)}, u32[]{:S(2)}) collective-permute-start(bf16[64,1152]{1,0:T(8,128)(2,1)S(1)} %get-tuple-element.27.rows), channel_id=1, source_target_pairs={{0,16},{16,0},{1,17},{17,1},{2,18},{18,2},{3,19},{19,3},{4,20},{20... | collective-permute-start | bytes 442376 | tf_op jit(solution)/shard_map/ppermute | solution.py:555
  7.5 3.8 %all-to-all-start = ((bf16[8,2,2,128,128]{4,3,2,1,0:T(8,128)(2,1)}), bf16[8,2,2,128,128]{4,3,2,1,0:T(8,128)(2,1)S(1)}, u32[]{:S(2)}, u32[]{:S(2)}) async-start(bf16[8,2,2,128,128]{4,3,2,1,0:T(8,128)(2,1)} %get-tuple-element.31), calls=%async_computation | async-start | bytes 2097152 | tf_op jit(solution)/shard_map/all_to_all | solution.py:602
  11.3 3.2 %collective-permute-done.over = bf16[64,1152]{1,0:T(8,128)(2,1)S(1)} collective-permute-done((bf16[64,1152]{1,0:T(8,128)(2,1)S(1)}, bf16[64,1152]{1,0:T(8,128)(2,1)S(1)}, u32[]{:S(2)}, u32[]{:S(2)}) %collective-permute-start) | collective-permute-done | bytes 147488 | tf_op jit(solution)/shard_map/ppermute | solution.py:555
  14.5 1.6 %collective-permute-start.1 = (bf16[2,64,1152]{2,1,0:T(8,128)(2,1)S(1)}, bf16[2,64,1152]{2,1,0:T(8,128)(2,1)S(1)}, u32[]{:S(2)}, u32[]{:S(2)}) collective-permute-start(bf16[2,64,1152]{2,1,0:T(8,128)(2,1)S(1)} %relay.1.refs_0_), channel_id=1, source_target_pairs={{0,4},{4,0},{1,5},{5,1},{2,6},{6,2},{3,7},{7,3},{8,12},{12,8},{9,1... | collective-permute-start | bytes 884744 | tf_op jit(solution)/shard_map/ppermute | solution.py:555
  16.6 10.2 %collective-permute-done.3.refs_4_ = bf16[64,1152]{1,0:T(8,128)(2,1)S(1)} collective-permute-done((bf16[64,1152]{1,0:T(8,128)(2,1)S(1)}, bf16[64,1152]{1,0:T(8,128)(2,1)S(1)}, u32[]{:S(2)}, u32[]{:S(2)}) %collective-permute-start.3) | collective-permute-done | bytes 147488 | tf_op jit(solution)/shard_map/ppermute | solution.py:555
  26.8 1.5 %collective-permute-start.4 = (bf16[64,1152]{1,0:T(8,128)(2,1)S(1)}, bf16[64,1152]{1,0:T(8,128)(2,1)S(1)}, u32[]{:S(2)}, u32[]{:S(2)}) collective-permute-start(bf16[64,1152]{1,0:T(8,128)(2,1)S(1)} %collective-permute-done.3.refs_4_), channel_id=1, source_target_pairs={{0,4},{4,0},{1,5},{5,1},{2,6},{6,2},{3,7},{7,3},{8,12},{12,8},{9,1... | collective-permute-start | bytes 442376 | tf_op jit(solution)/shard_map/ppermute | solution.py:555
  28.3 0.6 all-to-all-done.refs_2_.refs_6_.recv
  28.9 3.4 %first.1 = (bf16[2,2,512,128]{3,2,1,0:T(8,128)(2,1)S(1)}, bf16[2,2,512,128]{3,2,1,0:T(8,128)(2,1)S(1)}, f32[128,1152]{1,0:T(8,128)S(1)}, bf16[128,1152]{1,0:T(8,128)(2,1)S(1)}) custom-call(bf16[2,64,1152]{2,1,0:T(8,128)(2,1)S(1)} %relay.1.refs_0_, bf16[2,64,1152]{2,1,0:T(8,128)(2,1)S(1)} %collective-permute-done.1.refs_1_, ...), custom_call_target="tpu_custom_call" | custom-call | flops 3000000000 | bytes 1 | tf_op jit(solution)/shard_map/first/pallas_call | solution.py:395
  32.3 2.9 %collective-permute-start.6 = (bf16[128,1152]{1,0:T(8,128)(2,1)S(1)}, bf16[128,1152]{1,0:T(8,128)(2,1)S(1)}, u32[]{:S(2)}, u32[]{:S(2)}) collective-permute-start(bf16[128,1152]{1,0:T(8,128)(2,1)S(1)} %get-tuple-element.42), channel_id=1, source_target_pairs={{0,16},{16,0},{1,17},{17,1},{2,18},{18,2},{3,19},{19,3},{4,20},{20... | collective-permute-start | bytes 884744 | tf_op jit(solution)/shard_map/ppermute | solution.py:555
  35.2 3.9 %second.1 = (bf16[2,2,512,128]{3,2,1,0:T(8,128)(2,1)S(1)}, bf16[8,2,2,128,128]{4,3,2,1,0:T(8,128)(2,1)}) custom-call(bf16[2,64,1152]{2,1,0:T(8,128)(2,1)S(1)} %relay.1.refs_0_, bf16[2,64,1152]{2,1,0:T(8,128)(2,1)S(1)} %collective-permute-done.1.refs_1_, bf16[64,1152]{1,0:T(8,128)(2,1)S(1)} %get-tuple-element.30.refs_2_, ...), custom_call_target="tpu_custom_call" | custom-call | flops 20000000000 | bytes 1 | tf_op jit(solution)/shard_map/second/pallas_call | solution.py:487
  39.1 1.6 %lower.1 = (f32[64,1152]{1,0:T(8,128)S(1)}, f32[64,1152]{1,0:T(8,128)S(1)}, bf16[64,1152]{1,0:T(8,128)(2,1)S(1)}, bf16[64,1152]{1,0:T(8,128)(2,1)S(1)}) custom-call(bf16[8,2,2,128,128]{4,3,2,1,0:T(8,128)(2,1)S(1)} %all-to-all-done.refs_2_.refs_6_.recv, bf16[2,2,512,128]{3,2,1,0:T(8,128)(2,1)S(1)} %get-tuple-element.37.l_in), custom_call_target="tpu_custom_call" | custom-call | flops 20000000000 | bytes 1 | tf_op jit(solution)/shard_map/lower/pallas_call | solution.py:395
  40.7 0.6 collective-permute-start.5
  41.3 4.3 %all-to-all-start.1 = ((bf16[8,2,2,128,128]{4,3,2,1,0:T(8,128)(2,1)}), bf16[8,2,2,128,128]{4,3,2,1,0:T(8,128)(2,1)S(1)}, u32[]{:S(2)}, u32[]{:S(2)}) async-start(bf16[8,2,2,128,128]{4,3,2,1,0:T(8,128)(2,1)} %get-tuple-element.34), calls=%async_computation.1 | async-start | bytes 2097152 | tf_op jit(solution)/shard_map/all_to_all | solution.py:602
  45.6 2.7 %collective-permute-done.6.recv = bf16[128,1152]{1,0:T(8,128)(2,1)S(1)} collective-permute-done((bf16[128,1152]{1,0:T(8,128)(2,1)S(1)}, bf16[128,1152]{1,0:T(8,128)(2,1)S(1)}, u32[]{:S(2)}, u32[]{:S(2)}) %collective-permute-start.6) | collective-permute-done | bytes 294944 | tf_op jit(solution)/shard_map/ppermute | solution.py:555
  48.4 1.4 %collective-permute-start.9 = (bf16[64,1152]{1,0:T(8,128)(2,1)S(1)}, bf16[64,1152]{1,0:T(8,128)(2,1)S(1)}, u32[]{:S(2)}, u32[]{:S(2)}) collective-permute-start(bf16[64,1152]{1,0:T(8,128)(2,1)S(1)} %get-tuple-element.49), channel_id=1, source_target_pairs={{0,4},{4,0},{1,5},{5,1},{2,6},{6,2},{3,7},{7,3},{8,12},{12,8},{9,1... | collective-permute-start | bytes 442376 | tf_op jit(solution)/shard_map/ppermute | solution.py:555
  49.8 0.7 %collective-permute-start.7 = (bf16[64,1152]{1,0:T(8,128)(2,1)S(1)}, bf16[64,1152]{1,0:T(8,128)(2,1)S(1)}, u32[]{:S(2)}, u32[]{:S(2)}) collective-permute-start(bf16[64,1152]{1,0:T(8,128)(2,1)S(1)} %get-tuple-element.46), channel_id=1, source_target_pairs={{0,4},{4,0},{1,5},{5,1},{2,6},{6,2},{3,7},{7,3},{8,12},{12,8},{9,1... | collective-permute-start | bytes 442376 | tf_op jit(solution)/shard_map/ppermute | solution.py:555
  50.6 4.4 %collective-permute-done.9.refs_1_ = bf16[64,1152]{1,0:T(8,128)(2,1)S(1)} collective-permute-done((bf16[64,1152]{1,0:T(8,128)(2,1)S(1)}, bf16[64,1152]{1,0:T(8,128)(2,1)S(1)}, u32[]{:S(2)}, u32[]{:S(2)}) %collective-permute-start.9) | collective-permute-done | bytes 147488 | tf_op jit(solution)/shard_map/ppermute | solution.py:555
  54.9 1.0 %pull_rows.3 = f32[64,1152]{1,0:T(8,128)} custom-call(f32[64,1152]{1,0:T(8,128)S(1)} %bitcast.13, f32[1,64]{1,0:T(1,128)S(1)} %copy-done.4, f32[64,1152]{1,0:T(8,128)S(1)} %get-tuple-element.48.refs_0_, bf16[64,1152]{1,0:T(8,128)(2,1)S(1)} %collective-permute-done.9.refs_1_), custom_call_target="tpu_custom_call" | custom-call | flops 1 | bytes 1 | tf_op jit(solution)/shard_map/pull_rows/pallas_call | solution.py:92
  56.0 0.5 collective-permute-done.7.refs_1_
  56.5 4.7 %collective-permute-done.8.refs_2_ = bf16[64,1152]{1,0:T(8,128)(2,1)S(1)} collective-permute-done((bf16[64,1152]{1,0:T(8,128)(2,1)S(1)}, bf16[64,1152]{1,0:T(8,128)(2,1)S(1)}, u32[]{:S(2)}, u32[]{:S(2)}) %collective-permute-start.8) | collective-permute-done | bytes 147488 | tf_op jit(solution)/shard_map/ppermute | solution.py:555
  61.2 1.1 %pull_rows.2 = f32[64,1152]{1,0:T(8,128)} custom-call(f32[64,1152]{1,0:T(8,128)S(1)} %bitcast.15, f32[1,64]{1,0:T(1,128)S(1)} %copy-done.5, f32[64,1152]{1,0:T(8,128)S(1)} %get-tuple-element.38.refs_0_, bf16[64,1152]{1,0:T(8,128)(2,1)S(1)} %collective-permute-done.7.refs_1_, bf16[64,1152]{1,0:T(8,128)(2,1)S(1)} %collective-permute-done.8.refs_2_), custom_call_target="tpu_custom_call" | custom-call | flops 1 | bytes 1 | tf_op jit(solution)/shard_map/pull_rows/pallas_call | solution.py:92
  62.3 1.0 %all-to-all-done.1.recv = bf16[8,2,2,128,128]{4,3,2,1,0:T(8,128)(2,1)S(1)} async-done(((bf16[8,2,2,128,128]{4,3,2,1,0:T(8,128)(2,1)}), bf16[8,2,2,128,128]{4,3,2,1,0:T(8,128)(2,1)S(1)}, u32[]{:S(2)}, u32[]{:S(2)}) %all-to-all-start.1) | async-done | bytes 1048608 | tf_op jit(solution)/shard_map/all_to_all | solution.py:602
  63.3 1.6 %merge.1 = (bf16[128,2048]{1,0:T(8,128)(2,1)}, bf16[128,2048]{1,0:T(8,128)(2,1)}) custom-call(bf16[128,2048]{1,0:T(8,128)(2,1)S(1)} %bitcast.9, bf16[128,2048]{1,0:T(8,128)(2,1)S(1)} %bitcast.11, bf16[8,2,2,128,128]{4,3,2,1,0:T(8,128)(2,1)S(1)} %all-to-all-done.1.recv), custom_call_target="tpu_custom_call" | custom-call | flops 1 | bytes 1 | tf_op jit(solution)/shard_map/merge/pallas_call | solution.py:186
  (22 shorter events, 0.6 us)
Async XLA Ops:
  3.4 11.1 %collective-permute-start = (bf16[64,1152]{1,0:T(8,128)(2,1)S(1)}, bf16[64,1152]{1,0:T(8,128)(2,1)S(1)}, u32[]{:S(2)}, u32[]{:S(2)}) collective-permute-start(bf16[64,1152]{1,0:T(8,128)(2,1)S(1)} %get-tuple-element.27.rows), channel_id=1, source_target_pairs={{0,16},{16,0},{1,17},{17,1},{2,18},{18,2},{3,19},{19,3},{4,20},{20... | collective-permute-start | bytes 442376 | tf_op jit(solution)/shard_map/ppermute | solution.py:555
  7.5 21.4 %all-to-all-start = ((bf16[8,2,2,128,128]{4,3,2,1,0:T(8,128)(2,1)}), bf16[8,2,2,128,128]{4,3,2,1,0:T(8,128)(2,1)S(1)}, u32[]{:S(2)}, u32[]{:S(2)}) async-start(bf16[8,2,2,128,128]{4,3,2,1,0:T(8,128)(2,1)} %get-tuple-element.31), calls=%async_computation | async-start | bytes 2097152 | tf_op jit(solution)/shard_map/all_to_all | solution.py:602
  14.5 13.8 %collective-permute-start.1 = (bf16[2,64,1152]{2,1,0:T(8,128)(2,1)S(1)}, bf16[2,64,1152]{2,1,0:T(8,128)(2,1)S(1)}, u32[]{:S(2)}, u32[]{:S(2)}) collective-permute-start(bf16[2,64,1152]{2,1,0:T(8,128)(2,1)S(1)} %relay.1.refs_0_), channel_id=1, source_target_pairs={{0,4},{4,0},{1,5},{5,1},{2,6},{6,2},{3,7},{7,3},{8,12},{12,8},{9,1... | collective-permute-start | bytes 884744 | tf_op jit(solution)/shard_map/ppermute | solution.py:555
  16.1 10.7 %collective-permute-start.3 = (bf16[64,1152]{1,0:T(8,128)(2,1)S(1)}, bf16[64,1152]{1,0:T(8,128)(2,1)S(1)}, u32[]{:S(2)}, u32[]{:S(2)}) collective-permute-start(bf16[64,1152]{1,0:T(8,128)(2,1)S(1)} %get-tuple-element.30.refs_2_), channel_id=1, source_target_pairs={{0,16},{16,0},{1,17},{17,1},{2,18},{18,2},{3,19},{19,3},{4,20},{20... | collective-permute-start | bytes 442376 | tf_op jit(solution)/shard_map/ppermute | solution.py:555
  16.1 19.0 %collective-permute-start.2 = (bf16[64,1152]{1,0:T(8,128)(2,1)S(1)}, bf16[64,1152]{1,0:T(8,128)(2,1)S(1)}, u32[]{:S(2)}, u32[]{:S(2)}) collective-permute-start(bf16[64,1152]{1,0:T(8,128)(2,1)S(1)} %get-tuple-element.30.refs_2_), channel_id=1, source_target_pairs={{0,4},{4,0},{1,5},{5,1},{2,6},{6,2},{3,7},{7,3},{8,12},{12,8},{9,1... | collective-permute-start | bytes 442376 | tf_op jit(solution)/shard_map/ppermute | solution.py:555
  26.8 8.3 %collective-permute-start.4 = (bf16[64,1152]{1,0:T(8,128)(2,1)S(1)}, bf16[64,1152]{1,0:T(8,128)(2,1)S(1)}, u32[]{:S(2)}, u32[]{:S(2)}) collective-permute-start(bf16[64,1152]{1,0:T(8,128)(2,1)S(1)} %collective-permute-done.3.refs_4_), channel_id=1, source_target_pairs={{0,4},{4,0},{1,5},{5,1},{2,6},{6,2},{3,7},{7,3},{8,12},{12,8},{9,1... | collective-permute-start | bytes 442376 | tf_op jit(solution)/shard_map/ppermute | solution.py:555
  32.3 16.0 %collective-permute-start.6 = (bf16[128,1152]{1,0:T(8,128)(2,1)S(1)}, bf16[128,1152]{1,0:T(8,128)(2,1)S(1)}, u32[]{:S(2)}, u32[]{:S(2)}) collective-permute-start(bf16[128,1152]{1,0:T(8,128)(2,1)S(1)} %get-tuple-element.42), channel_id=1, source_target_pairs={{0,16},{16,0},{1,17},{17,1},{2,18},{18,2},{3,19},{19,3},{4,20},{20... | collective-permute-start | bytes 884744 | tf_op jit(solution)/shard_map/ppermute | solution.py:555
  40.7 7.6 %collective-permute-start.5 = (bf16[64,1152]{1,0:T(8,128)(2,1)S(1)}, bf16[64,1152]{1,0:T(8,128)(2,1)S(1)}, u32[]{:S(2)}, u32[]{:S(2)}) collective-permute-start(bf16[64,1152]{1,0:T(8,128)(2,1)S(1)} %get-tuple-element.40), channel_id=1, source_target_pairs={{0,4},{4,0},{1,5},{5,1},{2,6},{6,2},{3,7},{7,3},{8,12},{12,8},{9,1... | collective-permute-start | bytes 442376 | tf_op jit(solution)/shard_map/ppermute | solution.py:555
  41.3 22.0 %all-to-all-start.1 = ((bf16[8,2,2,128,128]{4,3,2,1,0:T(8,128)(2,1)}), bf16[8,2,2,128,128]{4,3,2,1,0:T(8,128)(2,1)S(1)}, u32[]{:S(2)}, u32[]{:S(2)}) async-start(bf16[8,2,2,128,128]{4,3,2,1,0:T(8,128)(2,1)} %get-tuple-element.34), calls=%async_computation.1 | async-start | bytes 2097152 | tf_op jit(solution)/shard_map/all_to_all | solution.py:602
  48.4 6.6 %collective-permute-start.9 = (bf16[64,1152]{1,0:T(8,128)(2,1)S(1)}, bf16[64,1152]{1,0:T(8,128)(2,1)S(1)}, u32[]{:S(2)}, u32[]{:S(2)}) collective-permute-start(bf16[64,1152]{1,0:T(8,128)(2,1)S(1)} %get-tuple-element.49), channel_id=1, source_target_pairs={{0,4},{4,0},{1,5},{5,1},{2,6},{6,2},{3,7},{7,3},{8,12},{12,8},{9,1... | collective-permute-start | bytes 442376 | tf_op jit(solution)/shard_map/ppermute | solution.py:555
  49.8 5.1 %copy-start.2 = (f32[1,64,1152]{2,1,0:T(8,128)S(1)}, f32[1,64,1152]{2,1,0:T(8,128)}, u32[]{:S(2)}) copy-start(f32[1,64,1152]{2,1,0:T(8,128)} %param.9) | copy-start | bytes 884740
  49.8 5.1 %copy-start.4 = (f32[1,64]{1,0:T(1,128)S(1)}, f32[1,64]{1,0:T(1,128)}, u32[]{:S(2)}) copy-start(f32[1,64]{1,0:T(1,128)} %g.3) | copy-start | bytes 772
  49.8 6.7 %collective-permute-start.7 = (bf16[64,1152]{1,0:T(8,128)(2,1)S(1)}, bf16[64,1152]{1,0:T(8,128)(2,1)S(1)}, u32[]{:S(2)}, u32[]{:S(2)}) collective-permute-start(bf16[64,1152]{1,0:T(8,128)(2,1)S(1)} %get-tuple-element.46), channel_id=1, source_target_pairs={{0,4},{4,0},{1,5},{5,1},{2,6},{6,2},{3,7},{7,3},{8,12},{12,8},{9,1... | collective-permute-start | bytes 442376 | tf_op jit(solution)/shard_map/ppermute | solution.py:555
  50.6 10.6 %collective-permute-start.8 = (bf16[64,1152]{1,0:T(8,128)(2,1)S(1)}, bf16[64,1152]{1,0:T(8,128)(2,1)S(1)}, u32[]{:S(2)}, u32[]{:S(2)}) collective-permute-start(bf16[64,1152]{1,0:T(8,128)(2,1)S(1)} %fold.1), channel_id=1, source_target_pairs={{0,16},{16,0},{1,17},{17,1},{2,18},{18,2},{3,19},{19,3},{4,20},{20... | collective-permute-start | bytes 442376 | tf_op jit(solution)/shard_map/ppermute | solution.py:555
  54.9 6.2 %copy-start.3 = (f32[1,64,1152]{2,1,0:T(8,128)S(1)}, f32[1,64,1152]{2,1,0:T(8,128)}, u32[]{:S(2)}) copy-start(f32[1,64,1152]{2,1,0:T(8,128)} %param.8) | copy-start | bytes 884740
  56.0 5.2 %copy-start.5 = (f32[1,64]{1,0:T(1,128)S(1)}, f32[1,64]{1,0:T(1,128)}, u32[]{:S(2)}) copy-start(f32[1,64]{1,0:T(1,128)} %g.2) | copy-start | bytes 772
  61.2 2.1 %copy-start = (bf16[1,4,32,2048]{3,2,1,0:T(8,128)(2,1)S(1)}, bf16[1,4,32,2048]{3,2,1,0:T(8,128)(2,1)}, u32[]{:S(2)}) copy-start(bf16[1,4,32,2048]{3,2,1,0:T(8,128)(2,1)} %param.6) | copy-start | bytes 1572868
  61.2 2.1 %copy-start.1 = (bf16[1,4,32,2048]{3,2,1,0:T(8,128)(2,1)S(1)}, bf16[1,4,32,2048]{3,2,1,0:T(8,128)(2,1)}, u32[]{:S(2)}) copy-start(bf16[1,4,32,2048]{3,2,1,0:T(8,128)(2,1)} %param.7) | copy-start | bytes 1572868

commit v3 on v2

--- a/solution.py
+++ b/solution.py
@@ -26,23 +26,23 @@
 
 
 def act_value(x):
-    t = jnp.tanh(ROOT * (x + CUBE * (x * x * x)))
+    t = jnp.tanh(x * (ROOT + (CUBE * ROOT) * (x * x)))
     return (0.5 * GAMMA) * x * (1.0 + t)
 
 
 def act_slope(x):
     sq = x * x
-    t = jnp.tanh(ROOT * (x + CUBE * (sq * x)))
+    t = jnp.tanh(x * (ROOT + (CUBE * ROOT) * sq))
     return (0.5 * GAMMA) * ((1.0 + t) + x * (1.0 - t * t) * (ROOT + (3.0 * CUBE * ROOT) * sq))
 
 
 def act_both(x):
     sq = x * x
-    t = jnp.tanh(ROOT * (x + CUBE * (sq * x)))
+    t = jnp.tanh(x * (ROOT + (CUBE * ROOT) * sq))
     up = 1.0 + t
     value = (0.5 * GAMMA) * x * up
-    slope = (0.5 * GAMMA) * (up + x * (1.0 - t * t) * (ROOT + (3.0 * CUBE * ROOT) * sq))
-    return value, slope
+    bend = x * (1.0 - t * t) * (ROOT + (3.0 * CUBE * ROOT) * sq)
+    return value, (0.5 * GAMMA * ALPHA) * (up + bend)
 
 
 def params(**kw):
@@ -74,7 +74,7 @@
     w[...] = (cent * scale).astype(BF16)
 
 
-def pull_kernel(k, g, *refs):
+def pull_kernel(factor, k, g, *refs):
     out = refs[-1]
     fan = k.shape[1]
     kern = k[...]
@@ -82,19 +82,19 @@
     cent = kern - jnp.mean(kern, axis=1, keepdims=True)
     var = jnp.mean(cent * cent, axis=1, keepdims=True)
     inv = lax.rsqrt(var + EPS)
-    scale = column(g) * inv * (1.0 / math.sqrt(fan))
+    scale = column(g) * inv * (factor / math.sqrt(fan))
     dot = jnp.mean(grad * cent, axis=1, keepdims=True)
     term = scale * (grad - cent * (inv * inv * dot))
     out[...] = term - jnp.mean(term, axis=1, keepdims=True)
 
 
-def pull_rows(k, g, sums, flops):
-    return pl.pallas_call(
-        pull_kernel,
+def pull_rows(k, g, sums, factor):
+    return pl.pallas_call(
+        functools.partial(pull_kernel, factor),
         out_shape=jax.ShapeDtypeStruct(k.shape, F32),
         name="pull_rows",
         compiler_params=params(),
-        cost_estimate=cost(flops),
+        cost_estimate=cost(PULL),
     )(k, g, *sums)
 
 
@@ -124,7 +124,7 @@
             for slot in range(geo["slots"]):
                 at = (block * geo["per_block"] + slot * geo["nb"] + b) * group
                 stage[dst, 0, slot] = act_value(f_in[:, at : at + group].astype(F32)).astype(BF16)
-                stage[dst, 1, slot] = (ALPHA * c_in[:, at : at + group].astype(F32)).astype(BF16)
+                stage[dst, 1, slot] = c_in[:, at : at + group]
             leaves.append(pltpu.make_async_copy(stage.at[dst], out.at[dst], sent.at[dst]))
             leaves[-1].start()
         if block == 0:
@@ -613,14 +613,14 @@
         back = exchange(out)
         away1, half2 = lax.optimization_barrier((swap(away1, "de"), half2))
         far1, send1 = lax.optimization_barrier((fold(far1, away1), send1))
-        grad_two = pull_rows(k2, gain_two, (mine2, swap(half2, "de")), PULL)
-        grad_one = pull_rows(k1, gain_one, (keep1, swap(send1, "de"), swap(far1, "da")), PULL)
+        grad_two = pull_rows(k2, gain_two, (mine2, swap(half2, "de")), ALPHA)
+        grad_one = pull_rows(k1, gain_one, (keep1, swap(send1, "de"), swap(far1, "da")), 1.0)
     else:
         back = exchange(out)
         flat = jnp.stack([x[0].reshape(geo["slots"] * group, fan) for x in (parts_one, parts_two)])
         sums = lax.psum_scatter(flat, ("da", "de"), scatter_dimension=1, tiled=True)
-        grad_one = pull_rows(k1, gain_one, (sums[0],), SMALL)
-        grad_two = pull_rows(k2, gain_two, (sums[1],), SMALL)
+        grad_one = pull_rows(k1, gain_one, (sums[0],), 1.0)
+        grad_two = pull_rows(k2, gain_two, (sums[1],), ALPHA)
     outputs, input_grad = merge(geo, f, c, back)
     return (
         outputs.reshape(features.shape),

time: 65.1 us -> 65 us (level)
  no operation moved by 1% of the time
where the time goes in v3:
time: 65 us; the launch traced here: 64.8 us
  waiting for transfers between devices  27.2 us (42%)
  starting transfers between devices  21.5 us (33%)
  Pallas kernels  15.3 us (24%)
  between operations  0.71 us (1%)
    ppermute x10, waiting for transfers between devices, swap(): return lax.ppermute(value, axis, [(0, 1), (1, 0)])  25.6 us
    ppermute x10, starting transfers between devices, swap(): return lax.ppermute(value, axis, [(0, 1), (1, 0)])  13.3 us
    all_to_all x2, starting transfers between devices, exchange(): return lax.all_to_all(x, ('db', 'row', 'col'), 0, 0, tiled=True)  8.15 us
    pallas_call x2, Pallas kernels, call(): pl.pallas_call(functools.partial(body, geo), out_shape=out_shape, scratch...  4.97 us
    pallas_call x1, Pallas kernels, second(): pl.pallas_call(functools.partial(second_kernel, geo, nw), out_shape=[map_...  3.91 us
    pallas_call x1, Pallas kernels, prep(): pl.pallas_call(functools.partial(prep_kernel, geo), in_specs=[hbm] * 6, o...  2.71 us
    pallas_call x2, Pallas kernels, pull_rows(): pl.pallas_call(functools.partial(pull_kernel, factor), out_shape=jax.Shap...  2.1 us
    all_to_all x2, waiting for transfers between devices, exchange(): return lax.all_to_all(x, ('db', 'row', 'col'), 0, 0, tiled=True)  1.59 us
  transfers between devices with their start and end apart: 12, of which 8 were waited for; matrix products, arithmetic and copies ran while one was open for 0% of the time, Pallas kernels for 17%

profile of v3, /device:TPU:0, one launch (start us, length us, event | category | flops | bytes accessed | tf_op | source)
XLA Modules:
  0.0 64.8 jit_solution(16716203336664494249)
XLA Ops:
  0.6 2.7 %prep.1 = (bf16[64,1152]{1,0:T(8,128)(2,1)S(1)}, bf16[64,1152]{1,0:T(8,128)(2,1)S(1)}, bf16[8,2,2,128,128]{4,3,2,1,0:T(8,128)(2,1)}) custom-call(f32[64,1152]{1,0:T(8,128)} %bitcast.14, f32[64,1152]{1,0:T(8,128)} %bitcast.12, f32[1,64]{1,0:T(1,128)} %g.2, f32[1,64]{1,0:T(1,128)} %g.3, bf16[128,2048]{1,0:T(8,128)(2,1)} %bitcast.8, bf16[128,2048]{1,0:T(8,128)(2,1)} %bitcast.10), custom_call_target="tpu_custom_call" | custom-call | flops 1 | bytes 1 | tf_op jit(solution)/shard_map/prep/pallas_call | solution.py:145
  3.3 4.1 %collective-permute-start = (bf16[64,1152]{1,0:T(8,128)(2,1)S(1)}, bf16[64,1152]{1,0:T(8,128)(2,1)S(1)}, u32[]{:S(2)}, u32[]{:S(2)}) collective-permute-start(bf16[64,1152]{1,0:T(8,128)(2,1)S(1)} %get-tuple-element.27.rows), channel_id=1, source_target_pairs={{0,16},{16,0},{1,17},{17,1},{2,18},{18,2},{3,19},{19,3},{4,20},{20... | collective-permute-start | bytes 442376 | tf_op jit(solution)/shard_map/ppermute | solution.py:555
  7.4 3.8 %all-to-all-start = ((bf16[8,2,2,128,128]{4,3,2,1,0:T(8,128)(2,1)}), bf16[8,2,2,128,128]{4,3,2,1,0:T(8,128)(2,1)S(1)}, u32[]{:S(2)}, u32[]{:S(2)}) async-start(bf16[8,2,2,128,128]{4,3,2,1,0:T(8,128)(2,1)} %get-tuple-element.31), calls=%async_computation | async-start | bytes 2097152 | tf_op jit(solution)/shard_map/all_to_all | solution.py:602
  11.3 3.2 %collective-permute-done.over = bf16[64,1152]{1,0:T(8,128)(2,1)S(1)} collective-permute-done((bf16[64,1152]{1,0:T(8,128)(2,1)S(1)}, bf16[64,1152]{1,0:T(8,128)(2,1)S(1)}, u32[]{:S(2)}, u32[]{:S(2)}) %collective-permute-start) | collective-permute-done | bytes 147488 | tf_op jit(solution)/shard_map/ppermute | solution.py:555
  14.5 1.6 %collective-permute-start.1 = (bf16[2,64,1152]{2,1,0:T(8,128)(2,1)S(1)}, bf16[2,64,1152]{2,1,0:T(8,128)(2,1)S(1)}, u32[]{:S(2)}, u32[]{:S(2)}) collective-permute-start(bf16[2,64,1152]{2,1,0:T(8,128)(2,1)S(1)} %relay.1.refs_0_), channel_id=1, source_target_pairs={{0,4},{4,0},{1,5},{5,1},{2,6},{6,2},{3,7},{7,3},{8,12},{12,8},{9,1... | collective-permute-start | bytes 884744 | tf_op jit(solution)/shard_map/ppermute | solution.py:555
  16.6 10.2 %collective-permute-done.3.refs_4_ = bf16[64,1152]{1,0:T(8,128)(2,1)S(1)} collective-permute-done((bf16[64,1152]{1,0:T(8,128)(2,1)S(1)}, bf16[64,1152]{1,0:T(8,128)(2,1)S(1)}, u32[]{:S(2)}, u32[]{:S(2)}) %collective-permute-start.3) | collective-permute-done | bytes 147488 | tf_op jit(solution)/shard_map/ppermute | solution.py:555
  26.8 1.5 %collective-permute-start.4 = (bf16[64,1152]{1,0:T(8,128)(2,1)S(1)}, bf16[64,1152]{1,0:T(8,128)(2,1)S(1)}, u32[]{:S(2)}, u32[]{:S(2)}) collective-permute-start(bf16[64,1152]{1,0:T(8,128)(2,1)S(1)} %collective-permute-done.3.refs_4_), channel_id=1, source_target_pairs={{0,4},{4,0},{1,5},{5,1},{2,6},{6,2},{3,7},{7,3},{8,12},{12,8},{9,1... | collective-permute-start | bytes 442376 | tf_op jit(solution)/shard_map/ppermute | solution.py:555
  28.3 0.6 all-to-all-done.refs_2_.refs_6_.recv
  28.9 3.3 %first.1 = (bf16[2,2,512,128]{3,2,1,0:T(8,128)(2,1)S(1)}, bf16[2,2,512,128]{3,2,1,0:T(8,128)(2,1)S(1)}, f32[128,1152]{1,0:T(8,128)S(1)}, bf16[128,1152]{1,0:T(8,128)(2,1)S(1)}) custom-call(bf16[2,64,1152]{2,1,0:T(8,128)(2,1)S(1)} %relay.1.refs_0_, bf16[2,64,1152]{2,1,0:T(8,128)(2,1)S(1)} %collective-permute-done.1.refs_1_, ...), custom_call_target="tpu_custom_call" | custom-call | flops 3000000000 | bytes 1 | tf_op jit(solution)/shard_map/first/pallas_call | solution.py:395
  32.2 2.9 %collective-permute-start.6 = (bf16[128,1152]{1,0:T(8,128)(2,1)S(1)}, bf16[128,1152]{1,0:T(8,128)(2,1)S(1)}, u32[]{:S(2)}, u32[]{:S(2)}) collective-permute-start(bf16[128,1152]{1,0:T(8,128)(2,1)S(1)} %get-tuple-element.42), channel_id=1, source_target_pairs={{0,16},{16,0},{1,17},{17,1},{2,18},{18,2},{3,19},{19,3},{4,20},{20... | collective-permute-start | bytes 884744 | tf_op jit(solution)/shard_map/ppermute | solution.py:555
  35.1 3.9 %second.1 = (bf16[2,2,512,128]{3,2,1,0:T(8,128)(2,1)S(1)}, bf16[8,2,2,128,128]{4,3,2,1,0:T(8,128)(2,1)}) custom-call(bf16[2,64,1152]{2,1,0:T(8,128)(2,1)S(1)} %relay.1.refs_0_, bf16[2,64,1152]{2,1,0:T(8,128)(2,1)S(1)} %collective-permute-done.1.refs_1_, bf16[64,1152]{1,0:T(8,128)(2,1)S(1)} %get-tuple-element.30.refs_2_, ...), custom_call_target="tpu_custom_call" | custom-call | flops 20000000000 | bytes 1 | tf_op jit(solution)/shard_map/second/pallas_call | solution.py:487
  39.0 1.6 %lower.1 = (f32[64,1152]{1,0:T(8,128)S(1)}, f32[64,1152]{1,0:T(8,128)S(1)}, bf16[64,1152]{1,0:T(8,128)(2,1)S(1)}, bf16[64,1152]{1,0:T(8,128)(2,1)S(1)}) custom-call(bf16[8,2,2,128,128]{4,3,2,1,0:T(8,128)(2,1)S(1)} %all-to-all-done.refs_2_.refs_6_.recv, bf16[2,2,512,128]{3,2,1,0:T(8,128)(2,1)S(1)} %get-tuple-element.37.l_in), custom_call_target="tpu_custom_call" | custom-call | flops 20000000000 | bytes 1 | tf_op jit(solution)/shard_map/lower/pallas_call | solution.py:395
  40.7 0.6 collective-permute-start.5
  41.3 4.3 %all-to-all-start.1 = ((bf16[8,2,2,128,128]{4,3,2,1,0:T(8,128)(2,1)}), bf16[8,2,2,128,128]{4,3,2,1,0:T(8,128)(2,1)S(1)}, u32[]{:S(2)}, u32[]{:S(2)}) async-start(bf16[8,2,2,128,128]{4,3,2,1,0:T(8,128)(2,1)} %get-tuple-element.34), calls=%async_computation.1 | async-start | bytes 2097152 | tf_op jit(solution)/shard_map/all_to_all | solution.py:602
  45.6 2.6 %collective-permute-done.6.recv = bf16[128,1152]{1,0:T(8,128)(2,1)S(1)} collective-permute-done((bf16[128,1152]{1,0:T(8,128)(2,1)S(1)}, bf16[128,1152]{1,0:T(8,128)(2,1)S(1)}, u32[]{:S(2)}, u32[]{:S(2)}) %collective-permute-start.6) | collective-permute-done | bytes 294944 | tf_op jit(solution)/shard_map/ppermute | solution.py:555
  48.3 1.4 %collective-permute-start.9 = (bf16[64,1152]{1,0:T(8,128)(2,1)S(1)}, bf16[64,1152]{1,0:T(8,128)(2,1)S(1)}, u32[]{:S(2)}, u32[]{:S(2)}) collective-permute-start(bf16[64,1152]{1,0:T(8,128)(2,1)S(1)} %get-tuple-element.49), channel_id=1, source_target_pairs={{0,4},{4,0},{1,5},{5,1},{2,6},{6,2},{3,7},{7,3},{8,12},{12,8},{9,1... | collective-permute-start | bytes 442376 | tf_op jit(solution)/shard_map/ppermute | solution.py:555
  49.8 0.7 %collective-permute-start.7 = (bf16[64,1152]{1,0:T(8,128)(2,1)S(1)}, bf16[64,1152]{1,0:T(8,128)(2,1)S(1)}, u32[]{:S(2)}, u32[]{:S(2)}) collective-permute-start(bf16[64,1152]{1,0:T(8,128)(2,1)S(1)} %get-tuple-element.46), channel_id=1, source_target_pairs={{0,4},{4,0},{1,5},{5,1},{2,6},{6,2},{3,7},{7,3},{8,12},{12,8},{9,1... | collective-permute-start | bytes 442376 | tf_op jit(solution)/shard_map/ppermute | solution.py:555
  50.5 4.4 %collective-permute-done.9.refs_1_ = bf16[64,1152]{1,0:T(8,128)(2,1)S(1)} collective-permute-done((bf16[64,1152]{1,0:T(8,128)(2,1)S(1)}, bf16[64,1152]{1,0:T(8,128)(2,1)S(1)}, u32[]{:S(2)}, u32[]{:S(2)}) %collective-permute-start.9) | collective-permute-done | bytes 147488 | tf_op jit(solution)/shard_map/ppermute | solution.py:555
  54.9 1.0 %pull_rows.3 = f32[64,1152]{1,0:T(8,128)} custom-call(f32[64,1152]{1,0:T(8,128)S(1)} %bitcast.13, f32[1,64]{1,0:T(1,128)S(1)} %copy-done.4, f32[64,1152]{1,0:T(8,128)S(1)} %get-tuple-element.48.refs_0_, bf16[64,1152]{1,0:T(8,128)(2,1)S(1)} %collective-permute-done.9.refs_1_), custom_call_target="tpu_custom_call" | custom-call | flops 1 | bytes 1 | tf_op jit(solution)/shard_map/pull_rows/pallas_call | solution.py:92
  55.9 0.5 collective-permute-done.7.refs_1_
  56.5 4.7 %collective-permute-done.8.refs_2_ = bf16[64,1152]{1,0:T(8,128)(2,1)S(1)} collective-permute-done((bf16[64,1152]{1,0:T(8,128)(2,1)S(1)}, bf16[64,1152]{1,0:T(8,128)(2,1)S(1)}, u32[]{:S(2)}, u32[]{:S(2)}) %collective-permute-start.8) | collective-permute-done | bytes 147488 | tf_op jit(solution)/shard_map/ppermute | solution.py:555
  61.2 1.1 %pull_rows.2 = f32[64,1152]{1,0:T(8,128)} custom-call(f32[64,1152]{1,0:T(8,128)S(1)} %bitcast.15, f32[1,64]{1,0:T(1,128)S(1)} %copy-done.5, f32[64,1152]{1,0:T(8,128)S(1)} %get-tuple-element.38.refs_0_, bf16[64,1152]{1,0:T(8,128)(2,1)S(1)} %collective-permute-done.7.refs_1_, bf16[64,1152]{1,0:T(8,128)(2,1)S(1)} %collective-permute-done.8.refs_2_), custom_call_target="tpu_custom_call" | custom-call | flops 1 | bytes 1 | tf_op jit(solution)/shard_map/pull_rows/pallas_call | solution.py:92
  62.2 1.0 %all-to-all-done.1.recv = bf16[8,2,2,128,128]{4,3,2,1,0:T(8,128)(2,1)S(1)} async-done(((bf16[8,2,2,128,128]{4,3,2,1,0:T(8,128)(2,1)}), bf16[8,2,2,128,128]{4,3,2,1,0:T(8,128)(2,1)S(1)}, u32[]{:S(2)}, u32[]{:S(2)}) %all-to-all-start.1) | async-done | bytes 1048608 | tf_op jit(solution)/shard_map/all_to_all | solution.py:602
  63.2 1.6 %merge.1 = (bf16[128,2048]{1,0:T(8,128)(2,1)}, bf16[128,2048]{1,0:T(8,128)(2,1)}) custom-call(bf16[128,2048]{1,0:T(8,128)(2,1)S(1)} %bitcast.9, bf16[128,2048]{1,0:T(8,128)(2,1)S(1)} %bitcast.11, bf16[8,2,2,128,128]{4,3,2,1,0:T(8,128)(2,1)S(1)} %all-to-all-done.1.recv), custom_call_target="tpu_custom_call" | custom-call | flops 1 | bytes 1 | tf_op jit(solution)/shard_map/merge/pallas_call | solution.py:186
  (22 shorter events, 0.6 us)
Async XLA Ops:
  3.3 11.1 %collective-permute-start = (bf16[64,1152]{1,0:T(8,128)(2,1)S(1)}, bf16[64,1152]{1,0:T(8,128)(2,1)S(1)}, u32[]{:S(2)}, u32[]{:S(2)}) collective-permute-start(bf16[64,1152]{1,0:T(8,128)(2,1)S(1)} %get-tuple-element.27.rows), channel_id=1, source_target_pairs={{0,16},{16,0},{1,17},{17,1},{2,18},{18,2},{3,19},{19,3},{4,20},{20... | collective-permute-start | bytes 442376 | tf_op jit(solution)/shard_map/ppermute | solution.py:555
  7.4 21.4 %all-to-all-start = ((bf16[8,2,2,128,128]{4,3,2,1,0:T(8,128)(2,1)}), bf16[8,2,2,128,128]{4,3,2,1,0:T(8,128)(2,1)S(1)}, u32[]{:S(2)}, u32[]{:S(2)}) async-start(bf16[8,2,2,128,128]{4,3,2,1,0:T(8,128)(2,1)} %get-tuple-element.31), calls=%async_computation | async-start | bytes 2097152 | tf_op jit(solution)/shard_map/all_to_all | solution.py:602
  14.5 13.8 %collective-permute-start.1 = (bf16[2,64,1152]{2,1,0:T(8,128)(2,1)S(1)}, bf16[2,64,1152]{2,1,0:T(8,128)(2,1)S(1)}, u32[]{:S(2)}, u32[]{:S(2)}) collective-permute-start(bf16[2,64,1152]{2,1,0:T(8,128)(2,1)S(1)} %relay.1.refs_0_), channel_id=1, source_target_pairs={{0,4},{4,0},{1,5},{5,1},{2,6},{6,2},{3,7},{7,3},{8,12},{12,8},{9,1... | collective-permute-start | bytes 884744 | tf_op jit(solution)/shard_map/ppermute | solution.py:555
  16.1 10.7 %collective-permute-start.3 = (bf16[64,1152]{1,0:T(8,128)(2,1)S(1)}, bf16[64,1152]{1,0:T(8,128)(2,1)S(1)}, u32[]{:S(2)}, u32[]{:S(2)}) collective-permute-start(bf16[64,1152]{1,0:T(8,128)(2,1)S(1)} %get-tuple-element.30.refs_2_), channel_id=1, source_target_pairs={{0,16},{16,0},{1,17},{17,1},{2,18},{18,2},{3,19},{19,3},{4,20},{20... | collective-permute-start | bytes 442376 | tf_op jit(solution)/shard_map/ppermute | solution.py:555
  16.1 19.0 %collective-permute-start.2 = (bf16[64,1152]{1,0:T(8,128)(2,1)S(1)}, bf16[64,1152]{1,0:T(8,128)(2,1)S(1)}, u32[]{:S(2)}, u32[]{:S(2)}) collective-permute-start(bf16[64,1152]{1,0:T(8,128)(2,1)S(1)} %get-tuple-element.30.refs_2_), channel_id=1, source_target_pairs={{0,4},{4,0},{1,5},{5,1},{2,6},{6,2},{3,7},{7,3},{8,12},{12,8},{9,1... | collective-permute-start | bytes 442376 | tf_op jit(solution)/shard_map/ppermute | solution.py:555
  26.8 8.3 %collective-permute-start.4 = (bf16[64,1152]{1,0:T(8,128)(2,1)S(1)}, bf16[64,1152]{1,0:T(8,128)(2,1)S(1)}, u32[]{:S(2)}, u32[]{:S(2)}) collective-permute-start(bf16[64,1152]{1,0:T(8,128)(2,1)S(1)} %collective-permute-done.3.refs_4_), channel_id=1, source_target_pairs={{0,4},{4,0},{1,5},{5,1},{2,6},{6,2},{3,7},{7,3},{8,12},{12,8},{9,1... | collective-permute-start | bytes 442376 | tf_op jit(solution)/shard_map/ppermute | solution.py:555
  32.2 16.0 %collective-permute-start.6 = (bf16[128,1152]{1,0:T(8,128)(2,1)S(1)}, bf16[128,1152]{1,0:T(8,128)(2,1)S(1)}, u32[]{:S(2)}, u32[]{:S(2)}) collective-permute-start(bf16[128,1152]{1,0:T(8,128)(2,1)S(1)} %get-tuple-element.42), channel_id=1, source_target_pairs={{0,16},{16,0},{1,17},{17,1},{2,18},{18,2},{3,19},{19,3},{4,20},{20... | collective-permute-start | bytes 884744 | tf_op jit(solution)/shard_map/ppermute | solution.py:555
  40.7 7.6 %collective-permute-start.5 = (bf16[64,1152]{1,0:T(8,128)(2,1)S(1)}, bf16[64,1152]{1,0:T(8,128)(2,1)S(1)}, u32[]{:S(2)}, u32[]{:S(2)}) collective-permute-start(bf16[64,1152]{1,0:T(8,128)(2,1)S(1)} %get-tuple-element.40), channel_id=1, source_target_pairs={{0,4},{4,0},{1,5},{5,1},{2,6},{6,2},{3,7},{7,3},{8,12},{12,8},{9,1... | collective-permute-start | bytes 442376 | tf_op jit(solution)/shard_map/ppermute | solution.py:555
  41.3 22.0 %all-to-all-start.1 = ((bf16[8,2,2,128,128]{4,3,2,1,0:T(8,128)(2,1)}), bf16[8,2,2,128,128]{4,3,2,1,0:T(8,128)(2,1)S(1)}, u32[]{:S(2)}, u32[]{:S(2)}) async-start(bf16[8,2,2,128,128]{4,3,2,1,0:T(8,128)(2,1)} %get-tuple-element.34), calls=%async_computation.1 | async-start | bytes 2097152 | tf_op jit(solution)/shard_map/all_to_all | solution.py:602
  48.3 6.6 %collective-permute-start.9 = (bf16[64,1152]{1,0:T(8,128)(2,1)S(1)}, bf16[64,1152]{1,0:T(8,128)(2,1)S(1)}, u32[]{:S(2)}, u32[]{:S(2)}) collective-permute-start(bf16[64,1152]{1,0:T(8,128)(2,1)S(1)} %get-tuple-element.49), channel_id=1, source_target_pairs={{0,4},{4,0},{1,5},{5,1},{2,6},{6,2},{3,7},{7,3},{8,12},{12,8},{9,1... | collective-permute-start | bytes 442376 | tf_op jit(solution)/shard_map/ppermute | solution.py:555
  49.7 5.1 %copy-start.2 = (f32[1,64,1152]{2,1,0:T(8,128)S(1)}, f32[1,64,1152]{2,1,0:T(8,128)}, u32[]{:S(2)}) copy-start(f32[1,64,1152]{2,1,0:T(8,128)} %param.9) | copy-start | bytes 884740
  49.8 5.1 %copy-start.4 = (f32[1,64]{1,0:T(1,128)S(1)}, f32[1,64]{1,0:T(1,128)}, u32[]{:S(2)}) copy-start(f32[1,64]{1,0:T(1,128)} %g.3) | copy-start | bytes 772
  49.8 6.7 %collective-permute-start.7 = (bf16[64,1152]{1,0:T(8,128)(2,1)S(1)}, bf16[64,1152]{1,0:T(8,128)(2,1)S(1)}, u32[]{:S(2)}, u32[]{:S(2)}) collective-permute-start(bf16[64,1152]{1,0:T(8,128)(2,1)S(1)} %get-tuple-element.46), channel_id=1, source_target_pairs={{0,4},{4,0},{1,5},{5,1},{2,6},{6,2},{3,7},{7,3},{8,12},{12,8},{9,1... | collective-permute-start | bytes 442376 | tf_op jit(solution)/shard_map/ppermute | solution.py:555
  50.5 10.6 %collective-permute-start.8 = (bf16[64,1152]{1,0:T(8,128)(2,1)S(1)}, bf16[64,1152]{1,0:T(8,128)(2,1)S(1)}, u32[]{:S(2)}, u32[]{:S(2)}) collective-permute-start(bf16[64,1152]{1,0:T(8,128)(2,1)S(1)} %fold.1), channel_id=1, source_target_pairs={{0,16},{16,0},{1,17},{17,1},{2,18},{18,2},{3,19},{19,3},{4,20},{20... | collective-permute-start | bytes 442376 | tf_op jit(solution)/shard_map/ppermute | solution.py:555
  54.9 6.3 %copy-start.3 = (f32[1,64,1152]{2,1,0:T(8,128)S(1)}, f32[1,64,1152]{2,1,0:T(8,128)}, u32[]{:S(2)}) copy-start(f32[1,64,1152]{2,1,0:T(8,128)} %param.8) | copy-start | bytes 884740
  55.9 5.2 %copy-start.5 = (f32[1,64]{1,0:T(1,128)S(1)}, f32[1,64]{1,0:T(1,128)}, u32[]{:S(2)}) copy-start(f32[1,64]{1,0:T(1,128)} %g.2) | copy-start | bytes 772
  61.1 2.1 %copy-start = (bf16[1,4,32,2048]{3,2,1,0:T(8,128)(2,1)S(1)}, bf16[1,4,32,2048]{3,2,1,0:T(8,128)(2,1)}, u32[]{:S(2)}) copy-start(bf16[1,4,32,2048]{3,2,1,0:T(8,128)(2,1)} %param.6) | copy-start | bytes 1572868
  61.1 2.1 %copy-start.1 = (bf16[1,4,32,2048]{3,2,1,0:T(8,128)(2,1)S(1)}, bf16[1,4,32,2048]{3,2,1,0:T(8,128)(2,1)}, u32[]{:S(2)}) copy-start(bf16[1,4,32,2048]{3,2,1,0:T(8,128)(2,1)} %param.7) | copy-start | bytes 1572868

commit v4 on v3

--- a/solution.py
+++ b/solution.py
@@ -20,7 +20,10 @@
 RELAY = 20_000_000_000
 FIRST = 3_000_000_000
 LOWER = RELAY
-SECOND = FOLD = RELAY
+SECOND = RELAY
+FOLD = 1
+HALVE = 1
+ADD = 500_000_000
 PULL = MERGE = SMALL
 STRIP = 4
 
@@ -74,28 +77,31 @@
     w[...] = (cent * scale).astype(BF16)
 
 
-def pull_kernel(factor, k, g, *refs):
-    out = refs[-1]
-    fan = k.shape[1]
-    kern = k[...]
-    grad = sum(ref[...].astype(F32) for ref in refs[:-1])
-    cent = kern - jnp.mean(kern, axis=1, keepdims=True)
-    var = jnp.mean(cent * cent, axis=1, keepdims=True)
-    inv = lax.rsqrt(var + EPS)
-    scale = column(g) * inv * (factor / math.sqrt(fan))
-    dot = jnp.mean(grad * cent, axis=1, keepdims=True)
-    term = scale * (grad - cent * (inv * inv * dot))
-    out[...] = term - jnp.mean(term, axis=1, keepdims=True)
-
-
-def pull_rows(k, g, sums, factor):
-    return pl.pallas_call(
-        functools.partial(pull_kernel, factor),
-        out_shape=jax.ShapeDtypeStruct(k.shape, F32),
+def pull_kernel(k1, k2, g1, g2, *refs):
+    *sums, out1, out2 = refs
+    half = len(sums) // 2
+    for k, g, parts, out, factor in (
+            (k1, g1, sums[:half], out1, 1.0), (k2, g2, sums[half:], out2, ALPHA)):
+        fan = k.shape[1]
+        kern = k[...]
+        grad = sum(ref[...].astype(F32) for ref in parts)
+        cent = kern - jnp.mean(kern, axis=1, keepdims=True)
+        var = jnp.mean(cent * cent, axis=1, keepdims=True)
+        inv = lax.rsqrt(var + EPS)
+        scale = column(g) * inv * (factor / math.sqrt(fan))
+        dot = jnp.mean(grad * cent, axis=1, keepdims=True)
+        term = scale * (grad - cent * (inv * inv * dot))
+        out[...] = term - jnp.mean(term, axis=1, keepdims=True)
+
+
+def pull_rows(k1, k2, g1, g2, *sums):
+    return pl.pallas_call(
+        pull_kernel,
+        out_shape=[jax.ShapeDtypeStruct(k1.shape, F32)] * 2,
         name="pull_rows",
         compiler_params=params(),
         cost_estimate=cost(PULL),
-    )(k, g, *sums)
+    )(k1, k2, g1, g2, *sums)
 
 
 def prep_kernel(geo, k1, k2, g1, g2, f, c, w1, w2, out, *scratch):
@@ -437,7 +443,7 @@
 
 def second_kernel(geo, nw, *refs):
     one, two = refs[: nw[0]], refs[nw[0] : sum(nw)]
-    recv, h_in, s_in, l_out, out, *buffers, stage, sems = refs[sum(nw) :]
+    recv, h_in, s_in, l_out, out, *buffers, low_in, stage, sems, low_sems = refs[sum(nw) :]
     moves = []
 
     def leave(which, slot):
@@ -468,8 +474,10 @@
             for at, size in strips(geo):
                 low = conv(geo, y2, n, at, size, aw2, True)
                 low = (low * s_in[slot, n, at : at + size, :].astype(F32)).astype(BF16)
-                l_out[slot, n, at : at + size, :] = low
+                low_in[slot, n, at : at + size, :] = low
                 fill_strip(geo, z2, n, at, low)
+        moves.append(pltpu.make_async_copy(low_in.at[slot], l_out.at[slot], low_sems.at[slot]))
+        moves[-1].start()
         for n in range(geo["maps"]):
             for at, size in strips(geo):
                 value = conv(geo, z2, n, at, size, aw1, True)
@@ -486,35 +494,59 @@
     args = (*one, *two, recv, hidden, slope)
     return pl.pallas_call(
         functools.partial(second_kernel, geo, nw),
-        out_shape=[map_shape(geo), sent],
-        out_specs=[
-            pl.BlockSpec(memory_space=pltpu.VMEM), pl.BlockSpec(memory_space=pl.ANY)],
+        out_shape=[pltpu.HBM(map_shape(geo).shape, BF16), sent],
+        out_specs=[pl.BlockSpec(memory_space=pl.ANY)] * 2,
         scratch_shapes=scratch(geo, 3, False, *shapes, shapes[2]) + [
+            pltpu.VMEM(map_shape(geo).shape, BF16),
             pltpu.VMEM((2, geo["slots"], geo["peers"], geo["piece"], geo["group"]), BF16),
-            pltpu.SemaphoreType.DMA((2, geo["slots"]))],
+            pltpu.SemaphoreType.DMA((2, geo["slots"])),
+            pltpu.SemaphoreType.DMA((geo["slots"],))],
         name="second",
         compiler_params=params(),
         cost_estimate=cost(SECOND),
     )(*args)
 
 
-def lower_kernel(geo, recv, l_in, *refs):
-    t_out, buffers = refs[:-3], refs[-3:]
-    for slot in range(geo["slots"]):
-        x2, g2, total = [ref.at[slot] for ref in buffers]
+def lower_kernel(geo, recv, low, k1, k2, g1, g2, *refs):
+    t_out, (*buffers, l_in, sems, k_sems) = refs[:-6], refs[-6:]
+    t_out, held = t_out[:-4], t_out[-4:]
+    brought = [pltpu.make_async_copy(src, dst, k_sems.at[n])
+               for n, (src, dst) in enumerate(zip((k1, k2, g1, g2), held))]
+    slots = range(geo["slots"])
+    moves = [pltpu.make_async_copy(low.at[slot], l_in.at[slot], sems.at[slot]) for slot in slots]
+    for move in moves + brought:
+        move.start()
+    for slot in slots:
+        x2 = buffers[0].at[slot]
         clear_rim(geo, x2)
-        clear_rim(geo, g2)
         for n in range(geo["maps"]):
             for at, size in strips(geo):
                 fill_strip(geo, x2, n, at, read_strip(geo, recv, 0, slot, n, at, size))
+    for slot in slots:
+        x2, g2, total = [ref.at[slot] for ref in buffers]
+        moves[slot].wait()
+        for n in range(geo["maps"]):
+            for at, size in strips(geo):
                 fill_strip(geo, g2, n, at, l_in[slot, n, at : at + size, :])
         terms(geo, g2, x2, total)
         split_terms(geo, slot, total, t_out)
-
-
-def lower(geo, recv, low):
-    return call(
-        geo, lower_kernel, "lower", (recv, low), term_out(geo), scratch(geo, 2, True), LOWER)
+    for move in brought:
+        move.wait()
+
+
+def lower(geo, recv, low, *kernels):
+    vmem, hbm = (pl.BlockSpec(memory_space=m) for m in (pltpu.VMEM, pl.ANY))
+    return pl.pallas_call(
+        functools.partial(lower_kernel, geo),
+        in_specs=[vmem] + [hbm] * 5,
+        out_shape=term_out(geo) + [jax.ShapeDtypeStruct(x.shape, F32) for x in kernels],
+        scratch_shapes=scratch(geo, 2, True) + [
+            pltpu.VMEM(map_shape(geo).shape, BF16), pltpu.SemaphoreType.DMA((geo["slots"],)),
+            pltpu.SemaphoreType.DMA((4,))],
+        name="lower",
+        compiler_params=params(),
+        cost_estimate=cost(LOWER),
+    )(recv, pin(low), *[pin(x) for x in kernels])
 
 
 def fold_kernel(keep, recv, send):
@@ -547,7 +579,21 @@
         out_shape=[jax.ShapeDtypeStruct(shape, F32), jax.ShapeDtypeStruct(shape, BF16)],
         name="halve",
         compiler_params=params(),
-        cost_estimate=cost(FOLD),
+        cost_estimate=cost(HALVE),
+    )(keep, recv)
+
+
+def add_kernel(keep, recv, out):
+    out[...] = keep[...] + recv[...].astype(F32)
+
+
+def add(keep, recv):
+    return pl.pallas_call(
+        add_kernel,
+        out_shape=jax.ShapeDtypeStruct(keep.shape, F32),
+        name="add",
+        compiler_params=params(),
+        cost_estimate=cost(ADD),
     )(keep, recv)
 
 
@@ -605,7 +651,8 @@
     one, two = gather_rows(geo, w1, w2)
     hidden, slope, *parts_two = first(geo, one, recv)
     low, out = second(geo, one, two, recv, hidden, slope)
-    parts_one = lower(geo, recv, low)
+    *parts_one, k1v, k2v, g1v, g2v = lower(geo, recv, low, k1, k2, gain_one, gain_two)
+    kernels = k1v, k2v, g1v, g2v
     if geo["pairs"]:
         keep2, send2 = parts_two
         mine2, half2 = halve(keep2, swap(send2, "da"))
@@ -613,14 +660,14 @@
         back = exchange(out)
         away1, half2 = lax.optimization_barrier((swap(away1, "de"), half2))
         far1, send1 = lax.optimization_barrier((fold(far1, away1), send1))
-        grad_two = pull_rows(k2, gain_two, (mine2, swap(half2, "de")), ALPHA)
-        grad_one = pull_rows(k1, gain_one, (keep1, swap(send1, "de"), swap(far1, "da")), 1.0)
+        mine1 = add(keep1, swap(far1, "da"))
+        grad_one, grad_two = pull_rows(
+            *kernels, mine1, swap(send1, "de"), mine2, swap(half2, "de"))
     else:
         back = exchange(out)
         flat = jnp.stack([x[0].reshape(geo["slots"] * group, fan) for x in (parts_one, parts_two)])
         sums = lax.psum_scatter(flat, ("da", "de"), scatter_dimension=1, tiled=True)
-        grad_one = pull_rows(k1, gain_one, (sums[0],), 1.0)
-        grad_two = pull_rows(k2, gain_two, (sums[1],), ALPHA)
+        grad_one, grad_two = pull_rows(*kernels, sums[0], sums[1])
     outputs, input_grad = merge(geo, f, c, back)
     return (
         outputs.reshape(features.shape),

time: 65 us -> 64.5 us (level)
  waiting for transfers between devices: 27.2 us -> 25.7 us
    pallas_call x3 -> x4, Pallas kernels: 6.01 us -> 8 us  [the longest x1 3.98 us: second(): pl.pallas_call(functools.partial(second_kernel, geo, nw), out_shape=[pltp...]
    pallas_call x2 -> x1, Pallas kernels: 4.97 us -> 3.35 us  [call(): pl.pallas_call(functools.partial(body, geo), out_shape=out_shape, scratch...]
    ppermute x10, starting transfers between devices: 13.3 us -> 14.7 us  [swap(): return lax.ppermute(value, axis, [(0, 1), (1, 0)])]
    all_to_all x2, waiting for transfers between devices: 1.59 us -> 0.58 us  [exchange(): return lax.all_to_all(x, ('db', 'row', 'col'), 0, 0, tiled=True)]
    all_to_all x2, starting transfers between devices: 8.15 us -> 7.38 us  [exchange(): return lax.all_to_all(x, ('db', 'row', 'col'), 0, 0, tiled=True)]
  transfers between devices with their start and end apart: 12 -> 12, of which waited for: 8 -> 6; matrix products, arithmetic and copies ran while one was open for 0% -> 0% of each run, Pallas kernels for 17% -> 18%
where the time goes in v4:
time: 64.5 us; the launch traced here: 64.3 us
  waiting for transfers between devices  25.7 us (40%)
  starting transfers between devices  22.1 us (34%)
  Pallas kernels  15.7 us (24%)
  between operations  0.73 us (1%)
    ppermute x10, waiting for transfers between devices, swap(): return lax.ppermute(value, axis, [(0, 1), (1, 0)])  25.1 us
    ppermute x10, starting transfers between devices, swap(): return lax.ppermute(value, axis, [(0, 1), (1, 0)])  14.7 us
    all_to_all x2, starting transfers between devices, exchange(): return lax.all_to_all(x, ('db', 'row', 'col'), 0, 0, tiled=True)  7.38 us
    pallas_call x1, Pallas kernels, second(): pl.pallas_call(functools.partial(second_kernel, geo, nw), out_shape=[pltp...  3.98 us
    pallas_call x1, Pallas kernels, call(): pl.pallas_call(functools.partial(body, geo), out_shape=out_shape, scratch...  3.35 us
    pallas_call x1, Pallas kernels, lower(): pl.pallas_call(functools.partial(lower_kernel, geo), in_specs=[vmem] + [h...  2.78 us
    pallas_call x1, Pallas kernels, prep(): pl.pallas_call(functools.partial(prep_kernel, geo), in_specs=[hbm] * 6, o...  2.7 us
    pallas_call x1, Pallas kernels, merge(): pl.pallas_call(functools.partial(merge_kernel, geo), out_specs=[pl.BlockS...  1.55 us
  transfers between devices with their start and end apart: 12, of which 6 were waited for; matrix products, arithmetic and copies ran while one was open for 0% of the time, Pallas kernels for 18%

profile of v4, /device:TPU:0, one launch (start us, length us, event | category | flops | bytes accessed | tf_op | source)
XLA Modules:
  0.0 64.3 jit_solution(7869985452322197927)
XLA Ops:
  0.6 2.7 %prep.1 = (bf16[64,1152]{1,0:T(8,128)(2,1)S(1)}, bf16[64,1152]{1,0:T(8,128)(2,1)S(1)}, bf16[8,2,2,128,128]{4,3,2,1,0:T(8,128)(2,1)}) custom-call(f32[64,1152]{1,0:T(8,128)} %bitcast.12, f32[64,1152]{1,0:T(8,128)} %bitcast.14, f32[1,64]{1,0:T(1,128)} %g1.3, f32[1,64]{1,0:T(1,128)} %g2.3, bf16[128,2048]{1,0:T(8,128)(2,1)} %bitcast.8, bf16[128,2048]{1,0:T(8,128)(2,1)} %bitcast.10), custom_call_target="tpu_custom_call" | custom-call | flops 1 | bytes 1 | tf_op jit(solution)/shard_map/prep/pallas_call | solution.py:151
  3.3 4.1 %collective-permute-start = (bf16[64,1152]{1,0:T(8,128)(2,1)S(1)}, bf16[64,1152]{1,0:T(8,128)(2,1)S(1)}, u32[]{:S(2)}, u32[]{:S(2)}) collective-permute-start(bf16[64,1152]{1,0:T(8,128)(2,1)S(1)} %get-tuple-element.33.rows), channel_id=1, source_target_pairs={{0,16},{16,0},{1,17},{17,1},{2,18},{18,2},{3,19},{19,3},{4,20},{20... | collective-permute-start | bytes 442376 | tf_op jit(solution)/shard_map/ppermute | solution.py:601
  7.4 3.8 %all-to-all-start = ((bf16[8,2,2,128,128]{4,3,2,1,0:T(8,128)(2,1)}), bf16[8,2,2,128,128]{4,3,2,1,0:T(8,128)(2,1)S(1)}, u32[]{:S(2)}, u32[]{:S(2)}) async-start(bf16[8,2,2,128,128]{4,3,2,1,0:T(8,128)(2,1)} %get-tuple-element.37), calls=%async_computation | async-start | bytes 2097152 | tf_op jit(solution)/shard_map/all_to_all | solution.py:648
  11.2 3.2 %collective-permute-done.over = bf16[64,1152]{1,0:T(8,128)(2,1)S(1)} collective-permute-done((bf16[64,1152]{1,0:T(8,128)(2,1)S(1)}, bf16[64,1152]{1,0:T(8,128)(2,1)S(1)}, u32[]{:S(2)}, u32[]{:S(2)}) %collective-permute-start) | collective-permute-done | bytes 147488 | tf_op jit(solution)/shard_map/ppermute | solution.py:601
  14.5 1.6 %collective-permute-start.1 = (bf16[2,64,1152]{2,1,0:T(8,128)(2,1)S(1)}, bf16[2,64,1152]{2,1,0:T(8,128)(2,1)S(1)}, u32[]{:S(2)}, u32[]{:S(2)}) collective-permute-start(bf16[2,64,1152]{2,1,0:T(8,128)(2,1)S(1)} %relay.1.refs_0_), channel_id=1, source_target_pairs={{0,4},{4,0},{1,5},{5,1},{2,6},{6,2},{3,7},{7,3},{8,12},{12,8},{9,1... | collective-permute-start | bytes 884744 | tf_op jit(solution)/shard_map/ppermute | solution.py:601
  16.1 0.5 collective-permute-start.2
  16.6 10.2 %collective-permute-done.3.refs_4_ = bf16[64,1152]{1,0:T(8,128)(2,1)S(1)} collective-permute-done((bf16[64,1152]{1,0:T(8,128)(2,1)S(1)}, bf16[64,1152]{1,0:T(8,128)(2,1)S(1)}, u32[]{:S(2)}, u32[]{:S(2)}) %collective-permute-start.3) | collective-permute-done | bytes 147488 | tf_op jit(solution)/shard_map/ppermute | solution.py:601
  26.8 1.5 %collective-permute-start.4 = (bf16[64,1152]{1,0:T(8,128)(2,1)S(1)}, bf16[64,1152]{1,0:T(8,128)(2,1)S(1)}, u32[]{:S(2)}, u32[]{:S(2)}) collective-permute-start(bf16[64,1152]{1,0:T(8,128)(2,1)S(1)} %collective-permute-done.3.refs_4_), channel_id=1, source_target_pairs={{0,4},{4,0},{1,5},{5,1},{2,6},{6,2},{3,7},{7,3},{8,12},{12,8},{9,1... | collective-permute-start | bytes 442376 | tf_op jit(solution)/shard_map/ppermute | solution.py:601
  28.3 0.6 all-to-all-done.refs_2_.refs_6_.recv
  28.9 3.3 %first.1 = (bf16[2,2,512,128]{3,2,1,0:T(8,128)(2,1)S(1)}, bf16[2,2,512,128]{3,2,1,0:T(8,128)(2,1)S(1)}, f32[128,1152]{1,0:T(8,128)S(1)}, bf16[128,1152]{1,0:T(8,128)(2,1)S(1)}) custom-call(bf16[2,64,1152]{2,1,0:T(8,128)(2,1)S(1)} %relay.1.refs_0_, bf16[2,64,1152]{2,1,0:T(8,128)(2,1)S(1)} %collective-permute-done.1.refs_1_, ...), custom_call_target="tpu_custom_call" | custom-call | flops 3000000000 | bytes 1 | tf_op jit(solution)/shard_map/first/pallas_call | solution.py:401
  32.2 2.9 %collective-permute-start.6 = (bf16[128,1152]{1,0:T(8,128)(2,1)S(1)}, bf16[128,1152]{1,0:T(8,128)(2,1)S(1)}, u32[]{:S(2)}, u32[]{:S(2)}) collective-permute-start(bf16[128,1152]{1,0:T(8,128)(2,1)S(1)} %get-tuple-element.52), channel_id=1, source_target_pairs={{0,16},{16,0},{1,17},{17,1},{2,18},{18,2},{3,19},{19,3},{4,20},{20... | collective-permute-start | bytes 884744 | tf_op jit(solution)/shard_map/ppermute | solution.py:601
  35.1 4.0 %second.1 = (bf16[2,2,512,128]{3,2,1,0:T(8,128)(2,1)}, bf16[8,2,2,128,128]{4,3,2,1,0:T(8,128)(2,1)}) custom-call(bf16[2,64,1152]{2,1,0:T(8,128)(2,1)S(1)} %relay.1.refs_0_, bf16[2,64,1152]{2,1,0:T(8,128)(2,1)S(1)} %collective-permute-done.1.refs_1_, bf16[64,1152]{1,0:T(8,128)(2,1)S(1)} %get-tuple-element.36.refs_2_, ...), custom_call_target="tpu_custom_call" | custom-call | flops 20000000000 | bytes 1 | tf_op jit(solution)/shard_map/second/pallas_call | solution.py:495
  39.1 3.6 %all-to-all-start.1 = ((bf16[8,2,2,128,128]{4,3,2,1,0:T(8,128)(2,1)}), bf16[8,2,2,128,128]{4,3,2,1,0:T(8,128)(2,1)S(1)}, u32[]{:S(2)}, u32[]{:S(2)}) async-start(bf16[8,2,2,128,128]{4,3,2,1,0:T(8,128)(2,1)} %get-tuple-element.40), calls=%async_computation.1 | async-start | bytes 2097152 | tf_op jit(solution)/shard_map/all_to_all | solution.py:648
  42.7 2.8 %lower.1 = (f32[64,1152]{1,0:T(8,128)S(1)}, f32[64,1152]{1,0:T(8,128)S(1)}, bf16[64,1152]{1,0:T(8,128)(2,1)S(1)}, bf16[64,1152]{1,0:T(8,128)(2,1)S(1)}, f32[64,1...) custom-call(bf16[8,2,2,128,128]{4,3,2,1,0:T(8,128)(2,1)S(1)} %all-to-all-done.refs_2_.refs_6, ...), custom_call_target="tpu_custom_call" | custom-call | flops 20000000000 | bytes 1 | tf_op jit(solution)/shard_map/lower/pallas_call | solution.py:539
  45.4 1.4 %collective-permute-start.5 = (bf16[64,1152]{1,0:T(8,128)(2,1)S(1)}, bf16[64,1152]{1,0:T(8,128)(2,1)S(1)}, u32[]{:S(2)}, u32[]{:S(2)}) collective-permute-start(bf16[64,1152]{1,0:T(8,128)(2,1)S(1)} %get-tuple-element.50), channel_id=1, source_target_pairs={{0,4},{4,0},{1,5},{5,1},{2,6},{6,2},{3,7},{7,3},{8,12},{12,8},{9,1... | collective-permute-start | bytes 442376 | tf_op jit(solution)/shard_map/ppermute | solution.py:601
  46.8 1.5 %collective-permute-done.6.recv = bf16[128,1152]{1,0:T(8,128)(2,1)S(1)} collective-permute-done((bf16[128,1152]{1,0:T(8,128)(2,1)S(1)}, bf16[128,1152]{1,0:T(8,128)(2,1)S(1)}, u32[]{:S(2)}, u32[]{:S(2)}) %collective-permute-start.6) | collective-permute-done | bytes 294944 | tf_op jit(solution)/shard_map/ppermute | solution.py:601
  48.3 0.1 halve.1
  48.4 3.3 %collective-permute-done.5.recv = bf16[64,1152]{1,0:T(8,128)(2,1)S(1)} collective-permute-done((bf16[64,1152]{1,0:T(8,128)(2,1)S(1)}, bf16[64,1152]{1,0:T(8,128)(2,1)S(1)}, u32[]{:S(2)}, u32[]{:S(2)}) %collective-permute-start.5) | collective-permute-done | bytes 147488 | tf_op jit(solution)/shard_map/ppermute | solution.py:601
  51.7 0.8 %collective-permute-start.7 = (bf16[64,1152]{1,0:T(8,128)(2,1)S(1)}, bf16[64,1152]{1,0:T(8,128)(2,1)S(1)}, u32[]{:S(2)}, u32[]{:S(2)}) collective-permute-start(bf16[64,1152]{1,0:T(8,128)(2,1)S(1)} %fold.1), channel_id=1, source_target_pairs={{0,16},{16,0},{1,17},{17,1},{2,18},{18,2},{3,19},{19,3},{4,20},{20... | collective-permute-start | bytes 442376 | tf_op jit(solution)/shard_map/ppermute | solution.py:601
  52.5 1.5 %collective-permute-start.8 = (bf16[64,1152]{1,0:T(8,128)(2,1)S(1)}, bf16[64,1152]{1,0:T(8,128)(2,1)S(1)}, u32[]{:S(2)}, u32[]{:S(2)}) collective-permute-start(bf16[64,1152]{1,0:T(8,128)(2,1)S(1)} %get-tuple-element.57), channel_id=1, source_target_pairs={{0,4},{4,0},{1,5},{5,1},{2,6},{6,2},{3,7},{7,3},{8,12},{12,8},{9,1... | collective-permute-start | bytes 442376 | tf_op jit(solution)/shard_map/ppermute | solution.py:601
  54.0 0.5 collective-permute-start.9
  54.6 6.8 %collective-permute-done.7.recv = bf16[64,1152]{1,0:T(8,128)(2,1)S(1)} collective-permute-done((bf16[64,1152]{1,0:T(8,128)(2,1)S(1)}, bf16[64,1152]{1,0:T(8,128)(2,1)S(1)}, u32[]{:S(2)}, u32[]{:S(2)}) %collective-permute-start.7) | collective-permute-done | bytes 147488 | tf_op jit(solution)/shard_map/ppermute | solution.py:601
  61.5 1.2 %pull_rows.1 = (f32[64,1152]{1,0:T(8,128)}, f32[64,1152]{1,0:T(8,128)}) custom-call(f32[64,1152]{1,0:T(8,128)S(1)} %get-tuple-element.44.k1, f32[64,1152]{1,0:T(8,128)S(1)} %get-tuple-element.45.k2, f32[1,64]{1,0:T(1,128)S(1)} %get-tuple-element.46.g1, f32[1,64]{1,0:T(1,128)S(1)} %get-tuple-element.47.g2, f32[64,1152]{1,0:T(8,128)S(1)} %add.1.refs_0_, ...), custom_call_target="tpu_custom_call" | custom-call | flops 1 | bytes 1 | tf_op jit(solution)/shard_map/pull_rows/pallas_call | solution.py:98
  62.7 1.6 %merge.1 = (bf16[128,2048]{1,0:T(8,128)(2,1)}, bf16[128,2048]{1,0:T(8,128)(2,1)}) custom-call(bf16[128,2048]{1,0:T(8,128)(2,1)S(1)} %bitcast.9, bf16[128,2048]{1,0:T(8,128)(2,1)S(1)} %bitcast.11, bf16[8,2,2,128,128]{4,3,2,1,0:T(8,128)(2,1)S(1)} %all-to-all-done.1.recv), custom_call_target="tpu_custom_call" | custom-call | flops 1 | bytes 1 | tf_op jit(solution)/shard_map/merge/pallas_call | solution.py:192
  (14 shorter events, 0.1 us)
Async XLA Ops:
  3.3 11.1 %collective-permute-start = (bf16[64,1152]{1,0:T(8,128)(2,1)S(1)}, bf16[64,1152]{1,0:T(8,128)(2,1)S(1)}, u32[]{:S(2)}, u32[]{:S(2)}) collective-permute-start(bf16[64,1152]{1,0:T(8,128)(2,1)S(1)} %get-tuple-element.33.rows), channel_id=1, source_target_pairs={{0,16},{16,0},{1,17},{17,1},{2,18},{18,2},{3,19},{19,3},{4,20},{20... | collective-permute-start | bytes 442376 | tf_op jit(solution)/shard_map/ppermute | solution.py:601
  7.4 21.4 %all-to-all-start = ((bf16[8,2,2,128,128]{4,3,2,1,0:T(8,128)(2,1)}), bf16[8,2,2,128,128]{4,3,2,1,0:T(8,128)(2,1)S(1)}, u32[]{:S(2)}, u32[]{:S(2)}) async-start(bf16[8,2,2,128,128]{4,3,2,1,0:T(8,128)(2,1)} %get-tuple-element.37), calls=%async_computation | async-start | bytes 2097152 | tf_op jit(solution)/shard_map/all_to_all | solution.py:648
  14.5 13.8 %collective-permute-start.1 = (bf16[2,64,1152]{2,1,0:T(8,128)(2,1)S(1)}, bf16[2,64,1152]{2,1,0:T(8,128)(2,1)S(1)}, u32[]{:S(2)}, u32[]{:S(2)}) collective-permute-start(bf16[2,64,1152]{2,1,0:T(8,128)(2,1)S(1)} %relay.1.refs_0_), channel_id=1, source_target_pairs={{0,4},{4,0},{1,5},{5,1},{2,6},{6,2},{3,7},{7,3},{8,12},{12,8},{9,1... | collective-permute-start | bytes 884744 | tf_op jit(solution)/shard_map/ppermute | solution.py:601
  16.1 10.7 %collective-permute-start.3 = (bf16[64,1152]{1,0:T(8,128)(2,1)S(1)}, bf16[64,1152]{1,0:T(8,128)(2,1)S(1)}, u32[]{:S(2)}, u32[]{:S(2)}) collective-permute-start(bf16[64,1152]{1,0:T(8,128)(2,1)S(1)} %get-tuple-element.36.refs_2_), channel_id=1, source_target_pairs={{0,16},{16,0},{1,17},{17,1},{2,18},{18,2},{3,19},{19,3},{4,20},{20... | collective-permute-start | bytes 442376 | tf_op jit(solution)/shard_map/ppermute | solution.py:601
  16.1 19.0 %collective-permute-start.2 = (bf16[64,1152]{1,0:T(8,128)(2,1)S(1)}, bf16[64,1152]{1,0:T(8,128)(2,1)S(1)}, u32[]{:S(2)}, u32[]{:S(2)}) collective-permute-start(bf16[64,1152]{1,0:T(8,128)(2,1)S(1)} %get-tuple-element.36.refs_2_), channel_id=1, source_target_pairs={{0,4},{4,0},{1,5},{5,1},{2,6},{6,2},{3,7},{7,3},{8,12},{12,8},{9,1... | collective-permute-start | bytes 442376 | tf_op jit(solution)/shard_map/ppermute | solution.py:601
  26.8 8.3 %collective-permute-start.4 = (bf16[64,1152]{1,0:T(8,128)(2,1)S(1)}, bf16[64,1152]{1,0:T(8,128)(2,1)S(1)}, u32[]{:S(2)}, u32[]{:S(2)}) collective-permute-start(bf16[64,1152]{1,0:T(8,128)(2,1)S(1)} %collective-permute-done.3.refs_4_), channel_id=1, source_target_pairs={{0,4},{4,0},{1,5},{5,1},{2,6},{6,2},{3,7},{7,3},{8,12},{12,8},{9,1... | collective-permute-start | bytes 442376 | tf_op jit(solution)/shard_map/ppermute | solution.py:601
  32.2 16.1 %collective-permute-start.6 = (bf16[128,1152]{1,0:T(8,128)(2,1)S(1)}, bf16[128,1152]{1,0:T(8,128)(2,1)S(1)}, u32[]{:S(2)}, u32[]{:S(2)}) collective-permute-start(bf16[128,1152]{1,0:T(8,128)(2,1)S(1)} %get-tuple-element.52), channel_id=1, source_target_pairs={{0,16},{16,0},{1,17},{17,1},{2,18},{18,2},{3,19},{19,3},{4,20},{20... | collective-permute-start | bytes 884744 | tf_op jit(solution)/shard_map/ppermute | solution.py:601
  39.1 23.6 %all-to-all-start.1 = ((bf16[8,2,2,128,128]{4,3,2,1,0:T(8,128)(2,1)}), bf16[8,2,2,128,128]{4,3,2,1,0:T(8,128)(2,1)S(1)}, u32[]{:S(2)}, u32[]{:S(2)}) async-start(bf16[8,2,2,128,128]{4,3,2,1,0:T(8,128)(2,1)} %get-tuple-element.40), calls=%async_computation.1 | async-start | bytes 2097152 | tf_op jit(solution)/shard_map/all_to_all | solution.py:648
  45.4 6.2 %collective-permute-start.5 = (bf16[64,1152]{1,0:T(8,128)(2,1)S(1)}, bf16[64,1152]{1,0:T(8,128)(2,1)S(1)}, u32[]{:S(2)}, u32[]{:S(2)}) collective-permute-start(bf16[64,1152]{1,0:T(8,128)(2,1)S(1)} %get-tuple-element.50), channel_id=1, source_target_pairs={{0,4},{4,0},{1,5},{5,1},{2,6},{6,2},{3,7},{7,3},{8,12},{12,8},{9,1... | collective-permute-start | bytes 442376 | tf_op jit(solution)/shard_map/ppermute | solution.py:601
  51.7 9.7 %collective-permute-start.7 = (bf16[64,1152]{1,0:T(8,128)(2,1)S(1)}, bf16[64,1152]{1,0:T(8,128)(2,1)S(1)}, u32[]{:S(2)}, u32[]{:S(2)}) collective-permute-start(bf16[64,1152]{1,0:T(8,128)(2,1)S(1)} %fold.1), channel_id=1, source_target_pairs={{0,16},{16,0},{1,17},{17,1},{2,18},{18,2},{3,19},{19,3},{4,20},{20... | collective-permute-start | bytes 442376 | tf_op jit(solution)/shard_map/ppermute | solution.py:601
  52.5 8.9 %collective-permute-start.8 = (bf16[64,1152]{1,0:T(8,128)(2,1)S(1)}, bf16[64,1152]{1,0:T(8,128)(2,1)S(1)}, u32[]{:S(2)}, u32[]{:S(2)}) collective-permute-start(bf16[64,1152]{1,0:T(8,128)(2,1)S(1)} %get-tuple-element.57), channel_id=1, source_target_pairs={{0,4},{4,0},{1,5},{5,1},{2,6},{6,2},{3,7},{7,3},{8,12},{12,8},{9,1... | collective-permute-start | bytes 442376 | tf_op jit(solution)/shard_map/ppermute | solution.py:601
  54.0 7.4 %collective-permute-start.9 = (bf16[64,1152]{1,0:T(8,128)(2,1)S(1)}, bf16[64,1152]{1,0:T(8,128)(2,1)S(1)}, u32[]{:S(2)}, u32[]{:S(2)}) collective-permute-start(bf16[64,1152]{1,0:T(8,128)(2,1)S(1)} %get-tuple-element.59), channel_id=1, source_target_pairs={{0,4},{4,0},{1,5},{5,1},{2,6},{6,2},{3,7},{7,3},{8,12},{12,8},{9,1... | collective-permute-start | bytes 442376 | tf_op jit(solution)/shard_map/ppermute | solution.py:601
  61.5 1.2 %copy-start = (bf16[1,4,32,2048]{3,2,1,0:T(8,128)(2,1)S(1)}, bf16[1,4,32,2048]{3,2,1,0:T(8,128)(2,1)}, u32[]{:S(2)}) copy-start(bf16[1,4,32,2048]{3,2,1,0:T(8,128)(2,1)} %param.6) | copy-start | bytes 1572868
  61.5 1.2 %copy-start.1 = (bf16[1,4,32,2048]{3,2,1,0:T(8,128)(2,1)S(1)}, bf16[1,4,32,2048]{3,2,1,0:T(8,128)(2,1)}, u32[]{:S(2)}) copy-start(bf16[1,4,32,2048]{3,2,1,0:T(8,128)(2,1)} %param.7) | copy-start | bytes 1572868

commit v5 on v4

--- a/solution.py
+++ b/solution.py
@@ -421,7 +421,6 @@
         for n in range(geo["maps"]):
             for at, size in strips(geo):
                 fill_strip(geo, x2, n, at, read_strip(geo, recv, 0, slot, n, at, size))
-                fill_strip(geo, g2, n, at, read_strip(geo, recv, 1, slot, n, at, size))
         for n in range(geo["maps"]):
             for at, size in strips(geo):
                 z = conv(geo, x2, n, at, size, fw, False).astype(BF16).astype(F32)
@@ -430,6 +429,7 @@
                 h_out[slot, n, at : at + size, :] = h
                 s_out[slot, n, at : at + size, :] = slope.astype(BF16)
                 fill_strip(geo, y2, n, at, h)
+                fill_strip(geo, g2, n, at, read_strip(geo, recv, 1, slot, n, at, size))
         terms(geo, g2, y2, total)
         split_slots(geo, slot, total, t_out)
 
@@ -464,11 +464,11 @@
         for n in range(geo["maps"]):
             for at, size in strips(geo):
                 fill_strip(geo, x2, n, at, h_in[slot, n, at : at + size, :])
-                fill_strip(geo, y2, n, at, read_strip(geo, recv, 1, slot, n, at, size))
         for n in range(geo["maps"]):
             for at, size in strips(geo):
                 value = ALPHA * conv(geo, x2, n, at, size, fw2, False)
                 write_strip(geo, stage.at[0, slot], n, at, value.astype(BF16))
+                fill_strip(geo, y2, n, at, read_strip(geo, recv, 1, slot, n, at, size))
         leave(0, slot)
         for n in range(geo["maps"]):
             for at, size in strips(geo):
@@ -514,7 +514,7 @@
                for n, (src, dst) in enumerate(zip((k1, k2, g1, g2), held))]
     slots = range(geo["slots"])
     moves = [pltpu.make_async_copy(low.at[slot], l_in.at[slot], sems.at[slot]) for slot in slots]
-    for move in moves + brought:
+    for move in moves:
         move.start()
     for slot in slots:
         x2 = buffers[0].at[slot]
@@ -525,6 +525,9 @@
     for slot in slots:
         x2, g2, total = [ref.at[slot] for ref in buffers]
         moves[slot].wait()
+        if slot == 0:
+            for move in brought:
+                move.start()
         for n in range(geo["maps"]):
             for at, size in strips(geo):
                 fill_strip(geo, g2, n, at, l_in[slot, n, at : at + size, :])

time: 64.5 us -> 64.5 us (level)
  transfers between devices with their start and end apart: 12 -> 12, of which waited for: 6 -> 7; matrix products, arithmetic and copies ran while one was open for 0% -> 0% of each run, Pallas kernels for 18% -> 18%
where the time goes in v5:
time: 64.5 us; the launch traced here: 64.2 us
  waiting for transfers between devices  25.9 us (40%)
  starting transfers between devices  22.1 us (34%)
  Pallas kernels  15.5 us (24%)
  between operations  0.73 us (1%)
    ppermute x10, waiting for transfers between devices, swap(): return lax.ppermute(value, axis, [(0, 1), (1, 0)])  25.1 us
    ppermute x10, starting transfers between devices, swap(): return lax.ppermute(value, axis, [(0, 1), (1, 0)])  14.7 us
    all_to_all x2, starting transfers between devices, exchange(): return lax.all_to_all(x, ('db', 'row', 'col'), 0, 0, tiled=True)  7.38 us
    pallas_call x1, Pallas kernels, second(): pl.pallas_call(functools.partial(second_kernel, geo, nw), out_shape=[pltp...  3.98 us
    pallas_call x1, Pallas kernels, call(): pl.pallas_call(functools.partial(body, geo), out_shape=out_shape, scratch...  3.35 us
    pallas_call x1, Pallas kernels, prep(): pl.pallas_call(functools.partial(prep_kernel, geo), in_specs=[hbm] * 6, o...  2.7 us
    pallas_call x1, Pallas kernels, lower(): pl.pallas_call(functools.partial(lower_kernel, geo), in_specs=[vmem] + [h...  2.6 us
    pallas_call x1, Pallas kernels, merge(): pl.pallas_call(functools.partial(merge_kernel, geo), out_specs=[pl.BlockS...  1.55 us
  transfers between devices with their start and end apart: 12, of which 7 were waited for; matrix products, arithmetic and copies ran while one was open for 0% of the time, Pallas kernels for 18%

profile of v5, /device:TPU:0, one launch (start us, length us, event | category | flops | bytes accessed | tf_op | source)
XLA Modules:
  0.0 64.2 jit_solution(7609958155785423733)
XLA Ops:
  0.6 2.7 %prep.1 = (bf16[64,1152]{1,0:T(8,128)(2,1)S(1)}, bf16[64,1152]{1,0:T(8,128)(2,1)S(1)}, bf16[8,2,2,128,128]{4,3,2,1,0:T(8,128)(2,1)}) custom-call(f32[64,1152]{1,0:T(8,128)} %bitcast.12, f32[64,1152]{1,0:T(8,128)} %bitcast.14, f32[1,64]{1,0:T(1,128)} %g1.3, f32[1,64]{1,0:T(1,128)} %g2.3, bf16[128,2048]{1,0:T(8,128)(2,1)} %bitcast.8, bf16[128,2048]{1,0:T(8,128)(2,1)} %bitcast.10), custom_call_target="tpu_custom_call" | custom-call | flops 1 | bytes 1 | tf_op jit(solution)/shard_map/prep/pallas_call | solution.py:151
  3.3 4.1 %collective-permute-start = (bf16[64,1152]{1,0:T(8,128)(2,1)S(1)}, bf16[64,1152]{1,0:T(8,128)(2,1)S(1)}, u32[]{:S(2)}, u32[]{:S(2)}) collective-permute-start(bf16[64,1152]{1,0:T(8,128)(2,1)S(1)} %get-tuple-element.33.rows), channel_id=1, source_target_pairs={{0,16},{16,0},{1,17},{17,1},{2,18},{18,2},{3,19},{19,3},{4,20},{20... | collective-permute-start | bytes 442376 | tf_op jit(solution)/shard_map/ppermute | solution.py:604
  7.4 3.8 %all-to-all-start = ((bf16[8,2,2,128,128]{4,3,2,1,0:T(8,128)(2,1)}), bf16[8,2,2,128,128]{4,3,2,1,0:T(8,128)(2,1)S(1)}, u32[]{:S(2)}, u32[]{:S(2)}) async-start(bf16[8,2,2,128,128]{4,3,2,1,0:T(8,128)(2,1)} %get-tuple-element.37), calls=%async_computation | async-start | bytes 2097152 | tf_op jit(solution)/shard_map/all_to_all | solution.py:651
  11.2 3.2 %collective-permute-done.over = bf16[64,1152]{1,0:T(8,128)(2,1)S(1)} collective-permute-done((bf16[64,1152]{1,0:T(8,128)(2,1)S(1)}, bf16[64,1152]{1,0:T(8,128)(2,1)S(1)}, u32[]{:S(2)}, u32[]{:S(2)}) %collective-permute-start) | collective-permute-done | bytes 147488 | tf_op jit(solution)/shard_map/ppermute | solution.py:604
  14.5 1.6 %collective-permute-start.1 = (bf16[2,64,1152]{2,1,0:T(8,128)(2,1)S(1)}, bf16[2,64,1152]{2,1,0:T(8,128)(2,1)S(1)}, u32[]{:S(2)}, u32[]{:S(2)}) collective-permute-start(bf16[2,64,1152]{2,1,0:T(8,128)(2,1)S(1)} %relay.1.refs_0_), channel_id=1, source_target_pairs={{0,4},{4,0},{1,5},{5,1},{2,6},{6,2},{3,7},{7,3},{8,12},{12,8},{9,1... | collective-permute-start | bytes 884744 | tf_op jit(solution)/shard_map/ppermute | solution.py:604
  16.1 0.5 collective-permute-start.2
  16.6 10.2 %collective-permute-done.3.refs_4_ = bf16[64,1152]{1,0:T(8,128)(2,1)S(1)} collective-permute-done((bf16[64,1152]{1,0:T(8,128)(2,1)S(1)}, bf16[64,1152]{1,0:T(8,128)(2,1)S(1)}, u32[]{:S(2)}, u32[]{:S(2)}) %collective-permute-start.3) | collective-permute-done | bytes 147488 | tf_op jit(solution)/shard_map/ppermute | solution.py:604
  26.8 1.5 %collective-permute-start.4 = (bf16[64,1152]{1,0:T(8,128)(2,1)S(1)}, bf16[64,1152]{1,0:T(8,128)(2,1)S(1)}, u32[]{:S(2)}, u32[]{:S(2)}) collective-permute-start(bf16[64,1152]{1,0:T(8,128)(2,1)S(1)} %collective-permute-done.3.refs_4_), channel_id=1, source_target_pairs={{0,4},{4,0},{1,5},{5,1},{2,6},{6,2},{3,7},{7,3},{8,12},{12,8},{9,1... | collective-permute-start | bytes 442376 | tf_op jit(solution)/shard_map/ppermute | solution.py:604
  28.3 0.6 all-to-all-done.refs_2_.refs_6_.recv
  28.9 3.3 %first.1 = (bf16[2,2,512,128]{3,2,1,0:T(8,128)(2,1)S(1)}, bf16[2,2,512,128]{3,2,1,0:T(8,128)(2,1)S(1)}, f32[128,1152]{1,0:T(8,128)S(1)}, bf16[128,1152]{1,0:T(8,128)(2,1)S(1)}) custom-call(bf16[2,64,1152]{2,1,0:T(8,128)(2,1)S(1)} %relay.1.refs_0_, bf16[2,64,1152]{2,1,0:T(8,128)(2,1)S(1)} %collective-permute-done.1.refs_1_, ...), custom_call_target="tpu_custom_call" | custom-call | flops 3000000000 | bytes 1 | tf_op jit(solution)/shard_map/first/pallas_call | solution.py:401
  32.2 2.9 %collective-permute-start.6 = (bf16[128,1152]{1,0:T(8,128)(2,1)S(1)}, bf16[128,1152]{1,0:T(8,128)(2,1)S(1)}, u32[]{:S(2)}, u32[]{:S(2)}) collective-permute-start(bf16[128,1152]{1,0:T(8,128)(2,1)S(1)} %get-tuple-element.52), channel_id=1, source_target_pairs={{0,16},{16,0},{1,17},{17,1},{2,18},{18,2},{3,19},{19,3},{4,20},{20... | collective-permute-start | bytes 884744 | tf_op jit(solution)/shard_map/ppermute | solution.py:604
  35.1 4.0 %second.1 = (bf16[2,2,512,128]{3,2,1,0:T(8,128)(2,1)}, bf16[8,2,2,128,128]{4,3,2,1,0:T(8,128)(2,1)}) custom-call(bf16[2,64,1152]{2,1,0:T(8,128)(2,1)S(1)} %relay.1.refs_0_, bf16[2,64,1152]{2,1,0:T(8,128)(2,1)S(1)} %collective-permute-done.1.refs_1_, bf16[64,1152]{1,0:T(8,128)(2,1)S(1)} %get-tuple-element.36.refs_2_, ...), custom_call_target="tpu_custom_call" | custom-call | flops 20000000000 | bytes 1 | tf_op jit(solution)/shard_map/second/pallas_call | solution.py:495
  39.1 3.6 %all-to-all-start.1 = ((bf16[8,2,2,128,128]{4,3,2,1,0:T(8,128)(2,1)}), bf16[8,2,2,128,128]{4,3,2,1,0:T(8,128)(2,1)S(1)}, u32[]{:S(2)}, u32[]{:S(2)}) async-start(bf16[8,2,2,128,128]{4,3,2,1,0:T(8,128)(2,1)} %get-tuple-element.40), calls=%async_computation.1 | async-start | bytes 2097152 | tf_op jit(solution)/shard_map/all_to_all | solution.py:651
  42.7 2.6 %lower.1 = (f32[64,1152]{1,0:T(8,128)S(1)}, f32[64,1152]{1,0:T(8,128)S(1)}, bf16[64,1152]{1,0:T(8,128)(2,1)S(1)}, bf16[64,1152]{1,0:T(8,128)(2,1)S(1)}, f32[64,1...) custom-call(bf16[8,2,2,128,128]{4,3,2,1,0:T(8,128)(2,1)S(1)} %all-to-all-done.refs_2_.refs_6, ...), custom_call_target="tpu_custom_call" | custom-call | flops 20000000000 | bytes 1 | tf_op jit(solution)/shard_map/lower/pallas_call | solution.py:542
  45.3 1.4 %collective-permute-start.5 = (bf16[64,1152]{1,0:T(8,128)(2,1)S(1)}, bf16[64,1152]{1,0:T(8,128)(2,1)S(1)}, u32[]{:S(2)}, u32[]{:S(2)}) collective-permute-start(bf16[64,1152]{1,0:T(8,128)(2,1)S(1)} %get-tuple-element.50), channel_id=1, source_target_pairs={{0,4},{4,0},{1,5},{5,1},{2,6},{6,2},{3,7},{7,3},{8,12},{12,8},{9,1... | collective-permute-start | bytes 442376 | tf_op jit(solution)/shard_map/ppermute | solution.py:604
  46.6 1.7 %collective-permute-done.6.recv = bf16[128,1152]{1,0:T(8,128)(2,1)S(1)} collective-permute-done((bf16[128,1152]{1,0:T(8,128)(2,1)S(1)}, bf16[128,1152]{1,0:T(8,128)(2,1)S(1)}, u32[]{:S(2)}, u32[]{:S(2)}) %collective-permute-start.6) | collective-permute-done | bytes 294944 | tf_op jit(solution)/shard_map/ppermute | solution.py:604
  48.4 3.1 %collective-permute-done.5.recv = bf16[64,1152]{1,0:T(8,128)(2,1)S(1)} collective-permute-done((bf16[64,1152]{1,0:T(8,128)(2,1)S(1)}, bf16[64,1152]{1,0:T(8,128)(2,1)S(1)}, u32[]{:S(2)}, u32[]{:S(2)}) %collective-permute-start.5) | collective-permute-done | bytes 147488 | tf_op jit(solution)/shard_map/ppermute | solution.py:604
  51.6 0.8 %collective-permute-start.7 = (bf16[64,1152]{1,0:T(8,128)(2,1)S(1)}, bf16[64,1152]{1,0:T(8,128)(2,1)S(1)}, u32[]{:S(2)}, u32[]{:S(2)}) collective-permute-start(bf16[64,1152]{1,0:T(8,128)(2,1)S(1)} %fold.1), channel_id=1, source_target_pairs={{0,16},{16,0},{1,17},{17,1},{2,18},{18,2},{3,19},{19,3},{4,20},{20... | collective-permute-start | bytes 442376 | tf_op jit(solution)/shard_map/ppermute | solution.py:604
  52.4 1.5 %collective-permute-start.8 = (bf16[64,1152]{1,0:T(8,128)(2,1)S(1)}, bf16[64,1152]{1,0:T(8,128)(2,1)S(1)}, u32[]{:S(2)}, u32[]{:S(2)}) collective-permute-start(bf16[64,1152]{1,0:T(8,128)(2,1)S(1)} %get-tuple-element.57), channel_id=1, source_target_pairs={{0,4},{4,0},{1,5},{5,1},{2,6},{6,2},{3,7},{7,3},{8,12},{12,8},{9,1... | collective-permute-start | bytes 442376 | tf_op jit(solution)/shard_map/ppermute | solution.py:604
  53.9 0.5 collective-permute-start.9
  54.4 6.8 %collective-permute-done.7.recv = bf16[64,1152]{1,0:T(8,128)(2,1)S(1)} collective-permute-done((bf16[64,1152]{1,0:T(8,128)(2,1)S(1)}, bf16[64,1152]{1,0:T(8,128)(2,1)S(1)}, u32[]{:S(2)}, u32[]{:S(2)}) %collective-permute-start.7) | collective-permute-done | bytes 147488 | tf_op jit(solution)/shard_map/ppermute | solution.py:604
  61.3 1.2 %pull_rows.1 = (f32[64,1152]{1,0:T(8,128)}, f32[64,1152]{1,0:T(8,128)}) custom-call(f32[64,1152]{1,0:T(8,128)S(1)} %get-tuple-element.44.k1, f32[64,1152]{1,0:T(8,128)S(1)} %get-tuple-element.45.k2, f32[1,64]{1,0:T(1,128)S(1)} %get-tuple-element.46.g1, f32[1,64]{1,0:T(1,128)S(1)} %get-tuple-element.47.g2, f32[64,1152]{1,0:T(8,128)S(1)} %add.1.refs_0_, ...), custom_call_target="tpu_custom_call" | custom-call | flops 1 | bytes 1 | tf_op jit(solution)/shard_map/pull_rows/pallas_call | solution.py:98
  62.5 0.2 all-to-all-done.1.recv
  62.7 1.6 %merge.1 = (bf16[128,2048]{1,0:T(8,128)(2,1)}, bf16[128,2048]{1,0:T(8,128)(2,1)}) custom-call(bf16[128,2048]{1,0:T(8,128)(2,1)S(1)} %bitcast.9, bf16[128,2048]{1,0:T(8,128)(2,1)S(1)} %bitcast.11, bf16[8,2,2,128,128]{4,3,2,1,0:T(8,128)(2,1)S(1)} %all-to-all-done.1.recv), custom_call_target="tpu_custom_call" | custom-call | flops 1 | bytes 1 | tf_op jit(solution)/shard_map/merge/pallas_call | solution.py:192
  (14 shorter events, 0.2 us)
Async XLA Ops:
  3.3 11.1 %collective-permute-start = (bf16[64,1152]{1,0:T(8,128)(2,1)S(1)}, bf16[64,1152]{1,0:T(8,128)(2,1)S(1)}, u32[]{:S(2)}, u32[]{:S(2)}) collective-permute-start(bf16[64,1152]{1,0:T(8,128)(2,1)S(1)} %get-tuple-element.33.rows), channel_id=1, source_target_pairs={{0,16},{16,0},{1,17},{17,1},{2,18},{18,2},{3,19},{19,3},{4,20},{20... | collective-permute-start | bytes 442376 | tf_op jit(solution)/shard_map/ppermute | solution.py:604
  7.4 21.4 %all-to-all-start = ((bf16[8,2,2,128,128]{4,3,2,1,0:T(8,128)(2,1)}), bf16[8,2,2,128,128]{4,3,2,1,0:T(8,128)(2,1)S(1)}, u32[]{:S(2)}, u32[]{:S(2)}) async-start(bf16[8,2,2,128,128]{4,3,2,1,0:T(8,128)(2,1)} %get-tuple-element.37), calls=%async_computation | async-start | bytes 2097152 | tf_op jit(solution)/shard_map/all_to_all | solution.py:651
  14.5 13.8 %collective-permute-start.1 = (bf16[2,64,1152]{2,1,0:T(8,128)(2,1)S(1)}, bf16[2,64,1152]{2,1,0:T(8,128)(2,1)S(1)}, u32[]{:S(2)}, u32[]{:S(2)}) collective-permute-start(bf16[2,64,1152]{2,1,0:T(8,128)(2,1)S(1)} %relay.1.refs_0_), channel_id=1, source_target_pairs={{0,4},{4,0},{1,5},{5,1},{2,6},{6,2},{3,7},{7,3},{8,12},{12,8},{9,1... | collective-permute-start | bytes 884744 | tf_op jit(solution)/shard_map/ppermute | solution.py:604
  16.1 10.7 %collective-permute-start.3 = (bf16[64,1152]{1,0:T(8,128)(2,1)S(1)}, bf16[64,1152]{1,0:T(8,128)(2,1)S(1)}, u32[]{:S(2)}, u32[]{:S(2)}) collective-permute-start(bf16[64,1152]{1,0:T(8,128)(2,1)S(1)} %get-tuple-element.36.refs_2_), channel_id=1, source_target_pairs={{0,16},{16,0},{1,17},{17,1},{2,18},{18,2},{3,19},{19,3},{4,20},{20... | collective-permute-start | bytes 442376 | tf_op jit(solution)/shard_map/ppermute | solution.py:604
  16.1 19.0 %collective-permute-start.2 = (bf16[64,1152]{1,0:T(8,128)(2,1)S(1)}, bf16[64,1152]{1,0:T(8,128)(2,1)S(1)}, u32[]{:S(2)}, u32[]{:S(2)}) collective-permute-start(bf16[64,1152]{1,0:T(8,128)(2,1)S(1)} %get-tuple-element.36.refs_2_), channel_id=1, source_target_pairs={{0,4},{4,0},{1,5},{5,1},{2,6},{6,2},{3,7},{7,3},{8,12},{12,8},{9,1... | collective-permute-start | bytes 442376 | tf_op jit(solution)/shard_map/ppermute | solution.py:604
  26.8 8.3 %collective-permute-start.4 = (bf16[64,1152]{1,0:T(8,128)(2,1)S(1)}, bf16[64,1152]{1,0:T(8,128)(2,1)S(1)}, u32[]{:S(2)}, u32[]{:S(2)}) collective-permute-start(bf16[64,1152]{1,0:T(8,128)(2,1)S(1)} %collective-permute-done.3.refs_4_), channel_id=1, source_target_pairs={{0,4},{4,0},{1,5},{5,1},{2,6},{6,2},{3,7},{7,3},{8,12},{12,8},{9,1... | collective-permute-start | bytes 442376 | tf_op jit(solution)/shard_map/ppermute | solution.py:604
  32.2 16.1 %collective-permute-start.6 = (bf16[128,1152]{1,0:T(8,128)(2,1)S(1)}, bf16[128,1152]{1,0:T(8,128)(2,1)S(1)}, u32[]{:S(2)}, u32[]{:S(2)}) collective-permute-start(bf16[128,1152]{1,0:T(8,128)(2,1)S(1)} %get-tuple-element.52), channel_id=1, source_target_pairs={{0,16},{16,0},{1,17},{17,1},{2,18},{18,2},{3,19},{19,3},{4,20},{20... | collective-permute-start | bytes 884744 | tf_op jit(solution)/shard_map/ppermute | solution.py:604
  39.1 23.6 %all-to-all-start.1 = ((bf16[8,2,2,128,128]{4,3,2,1,0:T(8,128)(2,1)}), bf16[8,2,2,128,128]{4,3,2,1,0:T(8,128)(2,1)S(1)}, u32[]{:S(2)}, u32[]{:S(2)}) async-start(bf16[8,2,2,128,128]{4,3,2,1,0:T(8,128)(2,1)} %get-tuple-element.40), calls=%async_computation.1 | async-start | bytes 2097152 | tf_op jit(solution)/shard_map/all_to_all | solution.py:651
  45.3 6.2 %collective-permute-start.5 = (bf16[64,1152]{1,0:T(8,128)(2,1)S(1)}, bf16[64,1152]{1,0:T(8,128)(2,1)S(1)}, u32[]{:S(2)}, u32[]{:S(2)}) collective-permute-start(bf16[64,1152]{1,0:T(8,128)(2,1)S(1)} %get-tuple-element.50), channel_id=1, source_target_pairs={{0,4},{4,0},{1,5},{5,1},{2,6},{6,2},{3,7},{7,3},{8,12},{12,8},{9,1... | collective-permute-start | bytes 442376 | tf_op jit(solution)/shard_map/ppermute | solution.py:604
  51.6 9.7 %collective-permute-start.7 = (bf16[64,1152]{1,0:T(8,128)(2,1)S(1)}, bf16[64,1152]{1,0:T(8,128)(2,1)S(1)}, u32[]{:S(2)}, u32[]{:S(2)}) collective-permute-start(bf16[64,1152]{1,0:T(8,128)(2,1)S(1)} %fold.1), channel_id=1, source_target_pairs={{0,16},{16,0},{1,17},{17,1},{2,18},{18,2},{3,19},{19,3},{4,20},{20... | collective-permute-start | bytes 442376 | tf_op jit(solution)/shard_map/ppermute | solution.py:604
  52.4 8.9 %collective-permute-start.8 = (bf16[64,1152]{1,0:T(8,128)(2,1)S(1)}, bf16[64,1152]{1,0:T(8,128)(2,1)S(1)}, u32[]{:S(2)}, u32[]{:S(2)}) collective-permute-start(bf16[64,1152]{1,0:T(8,128)(2,1)S(1)} %get-tuple-element.57), channel_id=1, source_target_pairs={{0,4},{4,0},{1,5},{5,1},{2,6},{6,2},{3,7},{7,3},{8,12},{12,8},{9,1... | collective-permute-start | bytes 442376 | tf_op jit(solution)/shard_map/ppermute | solution.py:604
  53.9 7.4 %collective-permute-start.9 = (bf16[64,1152]{1,0:T(8,128)(2,1)S(1)}, bf16[64,1152]{1,0:T(8,128)(2,1)S(1)}, u32[]{:S(2)}, u32[]{:S(2)}) collective-permute-start(bf16[64,1152]{1,0:T(8,128)(2,1)S(1)} %get-tuple-element.59), channel_id=1, source_target_pairs={{0,4},{4,0},{1,5},{5,1},{2,6},{6,2},{3,7},{7,3},{8,12},{12,8},{9,1... | collective-permute-start | bytes 442376 | tf_op jit(solution)/shard_map/ppermute | solution.py:604
  61.3 1.4 %copy-start = (bf16[1,4,32,2048]{3,2,1,0:T(8,128)(2,1)S(1)}, bf16[1,4,32,2048]{3,2,1,0:T(8,128)(2,1)}, u32[]{:S(2)}) copy-start(bf16[1,4,32,2048]{3,2,1,0:T(8,128)(2,1)} %param.6) | copy-start | bytes 1572868
  61.3 1.4 %copy-start.1 = (bf16[1,4,32,2048]{3,2,1,0:T(8,128)(2,1)S(1)}, bf16[1,4,32,2048]{3,2,1,0:T(8,128)(2,1)}, u32[]{:S(2)}) copy-start(bf16[1,4,32,2048]{3,2,1,0:T(8,128)(2,1)} %param.7) | copy-start | bytes 1572868
